TPU v7x, 32 devices: a whole 2x2x4 slice. The times are simulated.
32 devices in a mesh: gx: 4 (over y, x), pa: 8 (over z, core).
Axes of the slice: x: 2, y: 2, z: 4, core: 2. Of those that a mesh axis runs over, the one named last changes fastest.
Arguments:
- plastic: float32 [6, 128, 128, 128], P(None, 'gx', 'pa'), may hold values from -6 to 6
- offsets: float32 [3, 8, 16, 128], P(None, 'pa', 'gx'), may hold values from 0 to 1
- lines: float32 [3, 8, 16, 128], P(None, 'pa', 'gx'), may hold values from -3 to 3
- burgers: float32 [3, 8, 16, 128], P(None, 'pa', 'gx'), may hold values from -3.6 to 3.6
- counts: int32 [8, 16], P('pa', 'gx'), may hold values from 1 to 128, as said below
- voxels: int32 [8, 16, 128], P('pa', 'gx'), may hold values from 0 to 65535, as said below
Outputs:
- stress: float32 [6, 128, 128, 128], P(None, 'gx', 'pa')
- moved: float32 [3, 8, 16, 128], P(None, 'pa', 'gx')
Inputs may be any that keep to these rules, and one draw needn't show every extreme that they name: `counts`: each count is at least 1 and some cell holds 128 live segments. `voxels`: A segment of cell c lies in its device's block of 32 x 16 x 128 grid points: v = (x * 16 + y) * 128 + z with local plane x among the 8 planes of cell c % 4.
All inputs are finite; a program needn't handle non-finite values.
Results may differ from a plain program's by a relative error of at most 0.0003.
Values sent between devices are 32-bit elements; how exact they have to be, the bound alone decides.
No kernel may reach another device: no remote copies, remote signals or barrier semaphores. Data moves between devices by JAX's collectives and lax.ppermute only.
A program may use at most 128 MiB of HBM per device.

v0:
```python
import math

import jax
import jax.numpy as jnp
from jax import lax
from jax.sharding import PartitionSpec as P

SUB = 3


lame_lambda = 1.5
shear_modulus = 1.0
green_coef = 2.5 / 3.5
core_square = 0.09
pair_factor = 1.0 / (4.0 * math.pi)
step_size = 0.05
full_index = ((0, 5, 4), (5, 1, 3), (4, 3, 2))


def with_halo(block, sides, width):
    for axis, dim in sides:
        count = lax.axis_size(axis)
        forward = [(i, i + 1) for i in range(count - 1)]
        forward.append((count - 1, 0))
        backward = [(target, source) for source, target in forward]
        low = lax.ppermute(
            lax.slice_in_dim(block, block.shape[dim] - width, None, axis=dim), axis, forward
        )
        high = lax.ppermute(lax.slice_in_dim(block, 0, width, axis=dim), axis, backward)
        block = jnp.concatenate([low, block, high], axis=dim)
    return block


def stress_of(strain, freq_x, freq_y, freq_z):
    strain_xx, strain_yy, strain_zz = (strain[0], strain[1], strain[2])
    strain_yz, strain_xz, strain_xy = (strain[3], strain[4], strain[5])
    trace = strain_xx + strain_yy + strain_zz
    tau_xx = lame_lambda * trace + 2.0 * shear_modulus * strain_xx
    tau_yy = lame_lambda * trace + 2.0 * shear_modulus * strain_yy
    tau_zz = lame_lambda * trace + 2.0 * shear_modulus * strain_zz
    tau_yz = 2.0 * shear_modulus * strain_yz
    tau_xz = 2.0 * shear_modulus * strain_xz
    tau_xy = 2.0 * shear_modulus * strain_xy
    norm_x = tau_xx * freq_x + tau_xy * freq_y + tau_xz * freq_z
    norm_y = tau_xy * freq_x + tau_yy * freq_y + tau_yz * freq_z
    norm_z = tau_xz * freq_x + tau_yz * freq_y + tau_zz * freq_z
    square = freq_x * freq_x + freq_y * freq_y + freq_z * freq_z
    inverse = 1.0 / jnp.maximum(square, 1.0)
    along_k = (freq_x * norm_x + freq_y * norm_y + freq_z * norm_z) * inverse * inverse * green_coef

    def strain_term(first_q, second_q, first_n, second_n, plastic_part):
        total = (first_q * second_n + second_q * first_n) * inverse / (
            2.0 * shear_modulus
        ) - first_q * second_q * along_k
        return total - plastic_part

    el_xx = strain_term(freq_x, freq_x, norm_x, norm_x, strain_xx)
    el_yy = strain_term(freq_y, freq_y, norm_y, norm_y, strain_yy)
    el_zz = strain_term(freq_z, freq_z, norm_z, norm_z, strain_zz)
    el_yz = strain_term(freq_y, freq_z, norm_y, norm_z, strain_yz)
    el_xz = strain_term(freq_x, freq_z, norm_x, norm_z, strain_xz)
    el_xy = strain_term(freq_x, freq_y, norm_x, norm_y, strain_xy)
    el_trace = el_xx + el_yy + el_zz
    return jnp.stack(
        [
            lame_lambda * el_trace + 2.0 * shear_modulus * el_xx,
            lame_lambda * el_trace + 2.0 * shear_modulus * el_yy,
            lame_lambda * el_trace + 2.0 * shear_modulus * el_zz,
            2.0 * shear_modulus * el_yz,
            2.0 * shear_modulus * el_xz,
            2.0 * shear_modulus * el_xy,
        ]
    )


def advance(position, lines, burgers, sampled):
    cell_count = sampled.shape[1]
    unit_x = jnp.array([1.0, 0.0, 0.0], jnp.float32)[:, None, None]
    source = jnp.concatenate(
        [
            position[:, shifted : shifted + cell_count] + (shifted - 1.0) * unit_x
            for shifted in range(3)
        ],
        axis=2,
    )
    source_line = jnp.concatenate(
        [lines[:, shifted : shifted + cell_count] for shifted in range(3)], axis=2
    )
    source_burgers = jnp.concatenate(
        [burgers[:, shifted : shifted + cell_count] for shifted in range(3)], axis=2
    )
    target = position[:, 1 : cell_count + 1]
    own_line = lines[:, 1 : cell_count + 1]
    own_burgers = burgers[:, 1 : cell_count + 1]
    offset_vec = target[:, :, :, None] - source[:, :, None, :]
    radius = offset_vec[0] ** 2 + offset_vec[1] ** 2 + offset_vec[2] ** 2 + core_square
    weight = lax.rsqrt(radius) / radius
    line_b = source_line[:, :, None, :]
    cross = (
        jnp.stack(
            [
                offset_vec[1] * line_b[2] - offset_vec[2] * line_b[1],
                offset_vec[2] * line_b[0] - offset_vec[0] * line_b[2],
                offset_vec[0] * line_b[1] - offset_vec[1] * line_b[0],
            ]
        )
        * weight[None]
    )
    moment = jnp.einsum("acij,bcj->abci", cross, source_burgers, precision=lax.Precision.HIGHEST)
    pair_field = pair_factor * (moment + jnp.swapaxes(moment, 0, 1))
    traction = []
    for first in range(3):
        acc_row = jnp.zeros_like(target[0])
        for second in range(3):
            acc_row = (
                acc_row
                + (sampled[full_index[first][second]] + pair_field[first, second])
                * own_burgers[second]
            )
        traction.append(acc_row)
    force_x = traction[1] * own_line[2] - traction[2] * own_line[1]
    force_y = traction[2] * own_line[0] - traction[0] * own_line[2]
    force_z = traction[0] * own_line[1] - traction[1] * own_line[0]
    return target + step_size * jnp.stack([force_x, force_y, force_z])


def phases(row_index, col_index, grid_len):
    product = row_index[:, None] * col_index[None, :] % grid_len
    angle = product.astype(jnp.float32) * (2.0 * math.pi / grid_len)
    return (jnp.cos(angle), jnp.sin(angle))


def transform_last(field, matrix):
    shape = field.shape
    flat = field.reshape(-1, shape[-2] * shape[-1])
    result = jnp.dot(flat, matrix, precision=lax.Precision.HIGHEST)
    return result.reshape(shape[:-2] + (2, matrix.shape[1] // 2))


def body(plastic, offsets, lines, burgers, counts, voxels):
    grid_len = plastic.shape[3]
    pa_count = lax.axis_size("pa")
    grid_index = jnp.arange(grid_len, dtype=jnp.int32)
    bin_count = grid_len // 2 + pa_count
    bin_index = jnp.arange(bin_count, dtype=jnp.int32)
    kept_bins = (bin_index <= grid_len // 2).astype(jnp.float32)
    weights = jnp.where((bin_index == 0) | (bin_index == grid_len // 2), 1.0, 2.0) * kept_bins
    front_cos, front_sin = phases(grid_index, bin_index, grid_len)
    front_table = jnp.concatenate(
        [front_cos * kept_bins[None, :], -front_sin * kept_bins[None, :]], axis=1
    )
    final_cos, final_sin = phases(bin_index, grid_index, grid_len)
    final_table = (
        jnp.concatenate([final_cos * weights[:, None], -final_sin * weights[:, None]], axis=0)
        / grid_len
    )
    turn_cos, turn_sin = phases(grid_index, grid_index, grid_len)
    ahead_table = jnp.block([[turn_cos, -turn_sin], [turn_sin, turn_cos]])
    return_table = jnp.block([[turn_cos, turn_sin], [-turn_sin, turn_cos]]) / grid_len
    comp_count, x_local, y_local = (plastic.shape[0], plastic.shape[1], plastic.shape[2])
    field = jnp.dot(plastic.reshape(-1, grid_len), front_table, precision=lax.Precision.HIGHEST)
    field = field.reshape(comp_count, x_local, y_local, 2, bin_count)
    field = lax.all_to_all(field, "pa", split_axis=4, concat_axis=2, tiled=True)
    field = jnp.transpose(field, (0, 1, 4, 3, 2))
    field = transform_last(field, ahead_table)
    field = lax.all_to_all(field, "gx", split_axis=4, concat_axis=1, tiled=True)
    field = jnp.transpose(field, (0, 4, 2, 3, 1))
    field = transform_last(field, ahead_table)
    y_count = field.shape[1]
    z_count = field.shape[2]
    signed = jnp.where(
        grid_index < grid_len // 2,
        grid_index,
        jnp.where(grid_index == grid_len // 2, 0, grid_index - grid_len),
    ).astype(jnp.float32)
    freq_x = signed[None, None, :]
    freq_y = lax.dynamic_slice_in_dim(signed, lax.axis_index("gx") * y_count, y_count)[
        :, None, None
    ]
    freq_z = lax.dynamic_slice_in_dim(signed, lax.axis_index("pa") * z_count, z_count)[
        None, :, None
    ]
    real_part = stress_of(field[:, :, :, 0], freq_x, freq_y, freq_z)
    imag_part = stress_of(field[:, :, :, 1], freq_x, freq_y, freq_z)
    field = jnp.stack([real_part, imag_part], axis=3)
    field = transform_last(field, return_table)
    field = lax.all_to_all(field, "gx", split_axis=4, concat_axis=1, tiled=True)
    field = jnp.transpose(field, (0, 4, 2, 3, 1))
    field = transform_last(field, return_table)
    field = lax.all_to_all(field, "pa", split_axis=4, concat_axis=2, tiled=True)
    field = jnp.transpose(field, (0, 1, 4, 3, 2))
    flat = field.reshape(-1, 2 * bin_count)
    stress = jnp.dot(flat, final_table, precision=lax.Precision.HIGHEST).reshape(
        comp_count, x_local, y_local, grid_len
    )
    cell_count = offsets.shape[2]
    width_cap = offsets.shape[3]
    flat_stress = stress.reshape(6, -1)
    sampled = jnp.take(flat_stress, voxels.reshape(-1), axis=1).reshape(6, cell_count, width_cap)
    live_mask = (jnp.arange(width_cap, dtype=jnp.int32)[None, :] < counts[0][:, None]).astype(
        jnp.float32
    )
    initial = offsets[:, 0]
    line_dirs = lines[:, 0]
    masked = burgers[:, 0] * live_mask[None]
    fixed_rim = with_halo(jnp.concatenate([line_dirs, masked], axis=0), (("gx", 1),), 1)
    position = initial
    for repeat in range(SUB):
        widened = with_halo(position, (("gx", 1),), 1)
        position = advance(widened, fixed_rim[0:3], fixed_rim[3:6], sampled)
    moved = position - initial
    return (stress, moved[:, None])


def solution(mesh):
    placed = (
        P(None, "gx", "pa", None),
        P(None, "pa", "gx", None),
        P(None, "pa", "gx", None),
        P(None, "pa", "gx", None),
        P("pa", "gx"),
        P("pa", "gx", None),
    )
    return jax.shard_map(
        body,
        mesh=mesh,
        in_specs=placed,
        out_specs=(P(None, "gx", "pa", None), P(None, "pa", "gx", None)),
        check_vma=False,
    )
```

profile of v0, /device:TPU:0, one launch (start us, length us, event | category | flops | bytes accessed | tf_op | source)
XLA Modules:
  0.0 452.5 jit_solution(4670893569905264718)
XLA Ops:
  2.0 2.7 convolution_bitcast_fusion
  7.0 5.2 %reshape.2200 = f32[6,32,16,2,72]{4,3,2,1,0:T(2,128)} reshape(f32[3072,144]{1,0:T(8,128)} %copy.272) | data formatting | bytes 3538944 | tf_op jit(solution)/shard_map/reshape | solution.py:162
  12.2 10.1 %copy.273 = f32[6,32,16,2,72]{1,2,3,0,4:T(8,128)} copy(f32[6,32,16,2,72]{4,3,2,1,0:T(2,128)} %reshape.2200) | data formatting | bytes 3538944 | tf_op jit(solution)/shard_map/reshape | solution.py:162
  22.3 8.0 %reshape.2232 = f32[8,1,55296]{2,1,0:T(1,128)} reshape(f32[72,6,2,16,32]{4,3,2,1,0:T(8,128)} %bitcast.671) | data formatting | bytes 3538944
  30.3 6.6 %all-to-all-start = ((f32[8,1,55296]{2,1,0:T(1,128)}), f32[8,1,55296]{2,1,0:T(1,128)S(1)}, u32[]{:S(2)}, u32[]{:S(2)}) async-start(f32[8,1,55296]{2,1,0:T(1,128)} %reshape.2232), calls=%async_computation | async-start | bytes 3538944 | tf_op jit(solution)/shard_map/all_to_all | solution.py:163
  37.6 41.3 %all-to-all-done = f32[8,1,55296]{2,1,0:T(1,128)S(1)} async-done(((f32[8,1,55296]{2,1,0:T(1,128)}), f32[8,1,55296]{2,1,0:T(1,128)S(1)}, u32[]{:S(2)}, u32[]{:S(2)}) %all-to-all-start) | async-done | bytes 1769504 | tf_op jit(solution)/shard_map/all_to_all | solution.py:163
  79.4 6.7 %reduce.12 = f32[8,55296]{1,0:T(8,128)} reduce(f32[8,1,55296]{2,1,0:T(1,128)S(1)} %all-to-all-done, f32[]{:T(128)} %broadcast.2087), dimensions={1}, to_apply=%all_to_all.52.reduce_sub_computation | reduce | bytes 3538948 | tf_op jit(solution)/shard_map/all_to_all | solution.py:163
  86.1 6.7 %reshape.2233 = f32[72,6,2,16,32]{4,3,2,1,0:T(8,128)} reshape(f32[8,55296]{1,0:T(8,128)} %reduce.12) | data formatting | bytes 3538944
  92.7 7.0 %copy.275 = f32[6,32,8,16,2,9]{1,3,2,5,4,0:T(8,128)} copy(f32[6,32,8,16,2,9]{1,3,4,0,5,2:T(8,128)} %bitcast.672) | data formatting | bytes 3538944 | tf_op jit(solution)/shard_map/all_to_all | solution.py:163
  99.8 6.5 %copy.276 = f32[6,32,9,2,128]{4,3,1,2,0:T(2,128)} copy(f32[6,32,9,2,128]{1,4,2,3,0:T(8,128)} %bitcast.673) | data formatting | bytes 3538944 | tf_op jit(solution)/shard_map/transpose | solution.py:164
  106.2 2.7 reshape.2213
  108.9 2.9 fusion.21
  111.8 10.0 %copy.277 = f32[6,32,9,2,128]{1,3,2,0,4:T(2,128)} copy(f32[6,32,9,2,128]{4,1,3,2,0:T(8,128)} %fusion.21) | data formatting | bytes 3538944 | tf_op jit(solution)/shard_map/dot_general | solution.py:136
  121.8 9.3 %reshape.2234 = f32[4,1,110592]{2,1,0:T(1,128)} reshape(f32[128,6,9,2,32]{4,3,2,1,0:T(2,128)} %bitcast.679) | data formatting | bytes 3538944
  131.1 3.7 all-to-all-start.1
  135.1 21.0 %all-to-all-done.1 = f32[4,1,110592]{2,1,0:T(1,128)S(1)} async-done(((f32[4,1,110592]{2,1,0:T(1,128)}), f32[4,1,110592]{2,1,0:T(1,128)S(1)}, u32[]{:S(2)}, u32[]{:S(2)}) %all-to-all-start.1) | async-done | bytes 1769504 | tf_op jit(solution)/shard_map/all_to_all | solution.py:166
  156.1 7.1 %reduce.13 = f32[4,110592]{1,0:T(4,128)} reduce(f32[4,1,110592]{2,1,0:T(1,128)S(1)} %all-to-all-done.1, f32[]{:T(128)} %broadcast.2087), dimensions={1}, to_apply=%all_to_all.56.reduce_sub_computation | reduce | bytes 3538948 | tf_op jit(solution)/shard_map/all_to_all | solution.py:166
  163.2 10.5 %reshape.2235 = f32[128,6,9,2,32]{4,3,2,1,0:T(2,128)} reshape(f32[4,110592]{1,0:T(4,128)} %reduce.13) | data formatting | bytes 3538944
  173.6 10.7 %copy.357 = f32[6,32,9,2,4,32]{1,4,5,3,2,0:T(4,128)} copy(f32[6,32,9,2,4,32]{1,3,2,0,5,4:T(2,128)} %bitcast.674) | data formatting | bytes 3538944 | tf_op jit(solution)/shard_map/all_to_all | solution.py:166
  184.3 6.5 %all_to_all.59 = f32[6,128,9,2,32]{1,4,3,2,0:T(8,128)} reshape(f32[6,4,32,9,2,32]{2,1,5,4,3,0:T(4,128)} %bitcast.675) | data formatting | bytes 3538944 | tf_op jit(solution)/shard_map/all_to_all | solution.py:166
  190.8 3.1 copy.279
  193.8 2.6 reshape.2215
  196.5 3.1 fusion.19
  203.0 2.6 reshape.2216
  205.6 3.1 fusion.17
  208.7 7.9 %copy.292 = f32[6,32,9,2,128]{1,3,2,0,4:T(2,128)} copy(f32[6,32,9,2,128]{4,1,3,2,0:T(8,128)S(1)} %fusion.17) | data formatting | bytes 3538944 | tf_op jit(solution)/shard_map/dot_general | solution.py:136
  216.6 9.3 %reshape.2236 = f32[4,1,110592]{2,1,0:T(1,128)} reshape(f32[128,6,9,2,32]{4,3,2,1,0:T(2,128)} %bitcast.680) | data formatting | bytes 3538944
  225.9 4.1 all-to-all-start.2
  230.1 20.3 %all-to-all-done.2 = f32[4,1,110592]{2,1,0:T(1,128)S(1)} async-done(((f32[4,1,110592]{2,1,0:T(1,128)}), f32[4,1,110592]{2,1,0:T(1,128)S(1)}, u32[]{:S(2)}, u32[]{:S(2)}) %all-to-all-start.2) | async-done | bytes 1769504 | tf_op jit(solution)/shard_map/all_to_all | solution.py:187
  250.4 7.1 %reduce.14 = f32[4,110592]{1,0:T(4,128)} reduce(f32[4,1,110592]{2,1,0:T(1,128)S(1)} %all-to-all-done.2, f32[]{:T(128)} %broadcast.2087), dimensions={1}, to_apply=%all_to_all.60.reduce_sub_computation | reduce | bytes 3538948 | tf_op jit(solution)/shard_map/all_to_all | solution.py:187
  257.4 10.5 %reshape.2237 = f32[128,6,9,2,32]{4,3,2,1,0:T(2,128)} reshape(f32[4,110592]{1,0:T(4,128)} %reduce.14) | data formatting | bytes 3538944
  267.9 10.7 %copy.356 = f32[6,32,9,2,4,32]{1,4,5,3,2,0:T(4,128)} copy(f32[6,32,9,2,4,32]{1,3,2,0,5,4:T(2,128)} %bitcast.676) | data formatting | bytes 3538944 | tf_op jit(solution)/shard_map/all_to_all | solution.py:187
  278.6 6.5 %all_to_all.63 = f32[6,128,9,2,32]{1,4,3,2,0:T(8,128)} reshape(f32[6,4,32,9,2,32]{2,1,5,4,3,0:T(4,128)} %bitcast.677) | data formatting | bytes 3538944 | tf_op jit(solution)/shard_map/all_to_all | solution.py:187
  285.1 3.1 copy.294
  290.8 3.1 fusion.15
  293.8 7.9 %copy.295 = f32[6,32,9,2,128]{1,3,2,0,4:T(2,128)} copy(f32[6,32,9,2,128]{4,1,3,2,0:T(8,128)S(1)} %fusion.15) | data formatting | bytes 3538944 | tf_op jit(solution)/shard_map/dot_general | solution.py:136
  301.7 10.3 %reshape.2238 = f32[8,1,55296]{2,1,0:T(1,128)} reshape(f32[128,6,9,2,32]{4,3,2,1,0:T(2,128)} %bitcast.681) | data formatting | bytes 3538944
  312.1 3.7 all-to-all-start.3
  326.8 31.0 %all-to-all-done.3 = f32[8,1,55296]{2,1,0:T(1,128)S(1)} async-done(((f32[8,1,55296]{2,1,0:T(1,128)}), f32[8,1,55296]{2,1,0:T(1,128)S(1)}, u32[]{:S(2)}, u32[]{:S(2)}) %all-to-all-start.3) | async-done | bytes 1769504 | tf_op jit(solution)/shard_map/all_to_all | solution.py:190
  357.8 6.7 %reduce.15 = f32[8,55296]{1,0:T(8,128)} reduce(f32[8,1,55296]{2,1,0:T(1,128)S(1)} %all-to-all-done.3, f32[]{:T(128)} %broadcast.2087), dimensions={1}, to_apply=%all_to_all.64.reduce_sub_computation | reduce | bytes 3538948 | tf_op jit(solution)/shard_map/all_to_all | solution.py:190
  364.5 10.5 %reshape.2239 = f32[128,6,9,2,32]{4,3,2,1,0:T(2,128)} reshape(f32[8,55296]{1,0:T(8,128)} %reduce.15) | data formatting | bytes 3538944
  375.0 4.0 copy.296
  379.0 3.8 copy.297
  382.8 10.3 %copy.298 = f32[6,32,16,2,72]{4,3,2,1,0:T(2,128)} copy(f32[6,32,16,2,72]{1,2,3,4,0:T(8,128)} %bitcast.670) | data formatting | bytes 3538944 | tf_op jit(solution)/shard_map/transpose | solution.py:191
  393.0 5.2 %reshape.2201 = f32[3072,144]{1,0:T(8,128)} reshape(f32[6,32,16,2,72]{4,3,2,1,0:T(2,128)} %copy.298) | data formatting | bytes 3538944 | tf_op jit(solution)/shard_map/reshape | solution.py:192
  398.2 4.5 fusion.35
  404.5 16.4 %copy.299 = f32[6,65536]{0,1:T(8,128)} copy(f32[6,65536]{1,0:T(8,128)} %reshape_reshape.3) | data formatting | bytes 3145728 | tf_op jit(solution)/shard_map/reshape;reshape | solution.py:198
  420.9 11.6 %gather_fusion = f32[512,6]{1,0:T(8,128)S(1)} fusion(f32[6,65536]{0,1:T(8,128)} %copy.299, s32[1024]{0:T(1024)S(1)} %pad_clamp_fusion), kind=kCustom, calls=%fused_computation | custom fusion | bytes 26624 | tf_op jit(solution)/shard_map/jit(_take)/gather | solution.py:199
  (118 shorter events, 43.1 us)
Async XLA Ops:
  0.6 1.4 copy-start
  30.3 48.6 %all-to-all-start = ((f32[8,1,55296]{2,1,0:T(1,128)}), f32[8,1,55296]{2,1,0:T(1,128)S(1)}, u32[]{:S(2)}, u32[]{:S(2)}) async-start(f32[8,1,55296]{2,1,0:T(1,128)} %reshape.2232), calls=%async_computation | async-start | bytes 3538944 | tf_op jit(solution)/shard_map/all_to_all | solution.py:163
  131.1 25.0 %all-to-all-start.1 = ((f32[4,1,110592]{2,1,0:T(1,128)}), f32[4,1,110592]{2,1,0:T(1,128)S(1)}, u32[]{:S(2)}, u32[]{:S(2)}) async-start(f32[4,1,110592]{2,1,0:T(1,128)} %reshape.2234), calls=%async_computation.1 | async-start | bytes 3538944 | tf_op jit(solution)/shard_map/all_to_all | solution.py:166
  225.9 4.1 copy-start.9
  225.9 24.5 %all-to-all-start.2 = ((f32[4,1,110592]{2,1,0:T(1,128)}), f32[4,1,110592]{2,1,0:T(1,128)S(1)}, u32[]{:S(2)}, u32[]{:S(2)}) async-start(f32[4,1,110592]{2,1,0:T(1,128)} %reshape.2236), calls=%async_computation.2 | async-start | bytes 3538944 | tf_op jit(solution)/shard_map/all_to_all | solution.py:187
  312.1 3.8 copy-start.6
  312.1 3.8 copy-start.3
  312.1 6.8 %copy-start.4 = (f32[3,1,4,128]{3,2,1,0:T(4,128)S(1)}, f32[3,1,4,128]{3,2,1,0:T(4,128)}, u32[]{:S(2)}) copy-start(f32[3,1,4,128]{3,2,1,0:T(4,128)} %param.10) | copy-start | bytes 18436
  312.1 10.0 %copy-start.5 = (s32[1,4,128]{2,1,0:T(4,128)S(1)}, s32[1,4,128]{2,1,0:T(4,128)}, u32[]{:S(2)}) copy-start(s32[1,4,128]{2,1,0:T(4,128)} %param.14) | copy-start | bytes 6148
  312.1 11.5 %copy-start.7 = (f32[3]{0:T(128)S(1)}, f32[3]{0:T(128)}, u32[]{:S(2)}) copy-start(f32[3]{0:T(128)} %constant.111.clone) | copy-start | bytes 40
  312.1 11.5 %copy-start.8 = (f32[3]{0:T(128)S(1)}, f32[3]{0:T(128)}, u32[]{:S(2)}) copy-start(f32[3]{0:T(128)} %constant.117) | copy-start | bytes 40
  312.1 45.7 %all-to-all-start.3 = ((f32[8,1,55296]{2,1,0:T(1,128)}), f32[8,1,55296]{2,1,0:T(1,128)S(1)}, u32[]{:S(2)}, u32[]{:S(2)}) async-start(f32[8,1,55296]{2,1,0:T(1,128)} %reshape.2238), calls=%async_computation.3 | async-start | bytes 3538944 | tf_op jit(solution)/shard_map/all_to_all | solution.py:190
  315.9 8.1 %collective-permute-start = (f32[6,1,128]{2,1,0:T(1,128)S(1)}, f32[6,1,128]{2,1,0:T(1,128)S(1)}, u32[]{:S(2)}, u32[]{:S(2)}) collective-permute-start(f32[6,1,128]{2,1,0:T(1,128)S(1)} %get-tuple-element.68), channel_id=1, source_target_pairs={{0,8},{8,16},{16,24},{24,0},{1,9},{9,17},{17,25},{25,1},{2,10},{10... | collective-permute-start | bytes 9224 | tf_op jit(solution)/shard_map/ppermute | solution.py:26
  317.4 6.6 %collective-permute-start.1 = (f32[6,1,128]{2,1,0:T(1,128)S(1)}, f32[6,1,128]{2,1,0:T(1,128)S(1)}, u32[]{:S(2)}, u32[]{:S(2)}) collective-permute-start(f32[6,1,128]{2,1,0:T(1,128)S(1)} %get-tuple-element.69), channel_id=1, source_target_pairs={{8,0},{16,8},{24,16},{0,24},{9,1},{17,9},{25,17},{1,25},{10,2},{18... | collective-permute-start | bytes 9224 | tf_op jit(solution)/shard_map/ppermute | solution.py:29
  318.9 4.5 collective-permute-start.2
  319.4 4.2 collective-permute-start.3
  402.7 18.2 %copy-start.2 = (f32[3072,128]{1,0:T(8,128)}, f32[3072,128]{1,0:T(8,128)S(1)}, u32[]{:S(2)}) copy-start(f32[3072,128]{1,0:T(8,128)S(1)} %fusion.35) | copy-start | bytes 4718596
  433.6 4.5 %collective-permute-start.4 = (f32[3,1,128]{2,1,0:T(1,128)S(1)}, f32[3,1,128]{2,1,0:T(1,128)S(1)}, u32[]{:S(2)}, u32[]{:S(2)}) collective-permute-start(f32[3,1,128]{2,1,0:T(1,128)S(1)} %get-tuple-element.76), channel_id=1, source_target_pairs={{0,8},{8,16},{16,24},{24,0},{1,9},{9,17},{17,25},{25,1},{2,10},{10... | collective-permute-start | bytes 4616 | tf_op jit(solution)/shard_map/ppermute | solution.py:26
  435.1 3.6 collective-permute-start.5
  441.9 4.5 %collective-permute-start.6 = (f32[3,1,128]{2,1,0:T(1,128)S(1)}, f32[3,1,128]{2,1,0:T(1,128)S(1)}, u32[]{:S(2)}, u32[]{:S(2)}) collective-permute-start(f32[3,1,128]{2,1,0:T(1,128)S(1)} %get-tuple-element.72), channel_id=1, source_target_pairs={{0,8},{8,16},{16,24},{24,0},{1,9},{9,17},{17,25},{25,1},{2,10},{10... | collective-permute-start | bytes 4616 | tf_op jit(solution)/shard_map/ppermute | solution.py:26
  444.3 3.8 collective-permute-start.7
  448.5 3.4 copy-start.1
where the time goes:
time: 459 us; the launch traced here: 452 us
  local copies, waits for them, and re-layouts  240 us (52%)
  waiting for transfers between devices  120 us (26%)
  other arithmetic  34.2 us (7%)
  starting transfers between devices  30.5 us (7%)
  matrix products  25.9 us (6%)
    unnamed x28, local copies, waits for them, and re-layouts  76.1 us
    all_to_all x2, waiting for transfers between devices, body(): field = lax.all_to_all(field, 'pa', split_axis=4, concat_axis=2, tiled=True)  72.3 us
    all_to_all x2, waiting for transfers between devices, body(): field = lax.all_to_all(field, 'gx', split_axis=4, concat_axis=1, tiled=True)  41.3 us
    dot_general x7, local copies, waits for them, and re-layouts, transform_last(): result = jnp.dot(flat, matrix, precision=lax.Precision.HIGHEST)  36.5 us
    all_to_all x4, local copies, waits for them, and re-layouts, body(): field = lax.all_to_all(field, 'gx', split_axis=4, concat_axis=1, tiled=True)  34.3 us
    another operation x2, local copies, waits for them, and re-layouts, body(): flat_stress = stress.reshape(6, -1)  18.2 us
    transpose x2, local copies, waits for them, and re-layouts, body(): field = jnp.transpose(field, (0, 1, 4, 3, 2))  16.7 us
    all_to_all x4, local copies, waits for them, and re-layouts, body(): field = lax.all_to_all(field, 'pa', split_axis=4, concat_axis=2, tiled=True)  15.4 us
  transfers between devices with their start and end apart: 12, of which 10 were waited for; matrix products, arithmetic and copies ran while one was open for 1% of the time, Pallas kernels for 0%

commit v1 on v0

--- a/solution.py
+++ b/solution.py
@@ -1,8 +1,13 @@
+import functools
 import math
 
 import jax
 import jax.numpy as jnp
+import ml_dtypes
+import numpy as np
 from jax import lax
+from jax.experimental import pallas as pl
+from jax.experimental.pallas import tpu as pltpu
 from jax.sharding import PartitionSpec as P
 
 SUB = 3
@@ -212,6 +217,498 @@
     return (stress, moved[:, None])
 
 
+LANES = 128
+COMPS = 6
+FEATURES = 24
+SLOTS = 16
+VMEM_LIMIT = 48 * 1024 * 1024
+
+
+def split(value):
+    high = value.astype(jnp.bfloat16)
+    low = (value - high.astype(jnp.float32)).astype(jnp.bfloat16)
+    return high, low
+
+
+def split_table(table):
+    table = np.asarray(table, np.float32)
+    high = table.astype(ml_dtypes.bfloat16)
+    low = (table - high.astype(np.float32)).astype(ml_dtypes.bfloat16)
+    return high, low
+
+
+def product(left, right, dims=((1,), (0,))):
+    def one(first, second):
+        return lax.dot_general(
+            first, second, (dims, ((), ())), preferred_element_type=jnp.float32
+        )
+
+    left_high, left_low = left
+    right_high, right_low = right
+    return one(left_high, right_high) + (one(left_high, right_low) + one(left_low, right_high))
+
+
+def tables(grid_len, pa_count, y_local):
+    index = np.arange(grid_len)
+    bins = np.arange(grid_len // 2)
+    angle = 2.0 * np.pi * (np.outer(bins, index) % grid_len) / grid_len
+    nyquist = 1.0 - 2.0 * (index % 2)
+    forward_z = np.stack([np.cos(angle), -np.sin(angle)], axis=1)
+    forward_z[0, 1] = nyquist
+    inverse_z = 2.0 * forward_z / grid_len
+    inverse_z[0] = forward_z[0] / grid_len
+    forward_z = forward_z.reshape(grid_len, grid_len)
+    inverse_z = inverse_z.reshape(grid_len, grid_len)
+    turn = 2.0 * np.pi * (np.outer(index, index) % grid_len) / grid_len
+    cos, sin = np.cos(turn), np.sin(turn)
+    ahead = np.array([[cos, sin], [-sin, cos]]).transpose(0, 2, 1, 3)
+    back = np.array([[cos, -sin], [sin, cos]]).transpose(0, 2, 1, 3) / grid_len
+    size = 2 * grid_len
+    forward_y = ahead.reshape(2, grid_len, 2, pa_count, y_local).transpose(0, 1, 3, 2, 4)
+    forward_y = forward_y.reshape(size, size)
+    forward_x = ahead.reshape(size, size).T
+    inverse_x = back.reshape(size, size).T
+    inverse_y = back.reshape(2, pa_count, y_local, 2, grid_len).transpose(1, 0, 2, 3, 4)
+    inverse_y = inverse_y.reshape(size, size)
+    return [split_table(t) for t in (forward_z, forward_y, forward_x, inverse_x, inverse_y, inverse_z)]
+
+
+def lane_iota(rows):
+    return lax.broadcasted_iota(jnp.int32, (rows, LANES), 1)
+
+
+def forward_z_kernel(x_local, y_local, plane_ref, high_ref, low_ref, out_ref):
+    table = (high_ref[...], low_ref[...])
+    half = LANES // 2
+    per_comp = x_local * y_local
+    stride = (COMPS // 2) * y_local
+    first_half = lane_iota(half) < half
+    for pair in range(y_local // 2):
+        for tile in range(COMPS // 2):
+            rows = [
+                plane_ref[pl.ds((2 * tile + c) * per_comp + 2 * pair + y, x_local, stride=y_local), :]
+                for y in range(2)
+                for c in range(2)
+            ]
+            lines = split(jnp.concatenate(rows, axis=0))
+            waves = product(table, lines, ((1,), (1,)))
+            low_bins, high_bins = waves[:half], waves[half:]
+            even = jnp.where(first_half, low_bins, pltpu.roll(high_bins, half, 1))
+            odd = jnp.where(first_half, pltpu.roll(low_bins, half, 1), high_bins)
+            base = tile * y_local + 2 * pair
+            out_ref[pl.ds(base, half, stride=stride), :] = even
+            out_ref[pl.ds(base + 1, half, stride=stride), :] = odd
+
+
+def swap_blocks(tiles):
+    lane = lane_iota(tiles[0].shape[0])
+    lower = lane < LANES // 2
+    even = (lane // (LANES // 4)) % 2 == 0
+    tiles = list(tiles)
+    for a, b in ((0, 2), (1, 3)):
+        first, second = tiles[a], tiles[b]
+        tiles[a] = jnp.where(lower, first, pltpu.roll(second, LANES // 2, 1))
+        tiles[b] = jnp.where(lower, pltpu.roll(first, LANES // 2, 1), second)
+    for a, b in ((0, 1), (2, 3)):
+        first, second = tiles[a], tiles[b]
+        tiles[a] = jnp.where(even, first, pltpu.roll(second, LANES // 4, 1))
+        tiles[b] = jnp.where(even, pltpu.roll(first, 3 * LANES // 4, 1), second)
+    return tiles
+
+
+def spectral_kernel(
+    gx_count,
+    pa_count,
+    y_local,
+    freq_ref,
+    data_ref,
+    fyh_ref,
+    fyl_ref,
+    fxh_ref,
+    fxl_ref,
+    ixh_ref,
+    ixl_ref,
+    iyh_ref,
+    iyl_ref,
+    out_ref,
+    waves,
+):
+    grid_len = LANES
+    size = 2 * grid_len
+    tile_count = COMPS // 2
+    forward_y = (fyh_ref[...], fyl_ref[...])
+    forward_x = (fxh_ref[...], fxl_ref[...])
+    inverse_x = (ixh_ref[...], ixl_ref[...])
+    inverse_y = (iyh_ref[...], iyl_ref[...])
+    for tile in range(tile_count):
+        blocks = []
+        for g in range(gx_count):
+            field = data_ref[pl.ds(g * pa_count, pa_count), :, tile, :, :].reshape(size, LANES)
+            blocks.append(product(forward_y, split(field)))
+        for slot, block in enumerate(swap_blocks(blocks)):
+            rows = jnp.concatenate([block[:grid_len], block[grid_len:]], axis=1)
+            waves[tile, slot] = product(split(rows), forward_x)
+
+    def signed(index):
+        plain = jnp.where(index < grid_len // 2, index, index - grid_len)
+        return jnp.where(index == grid_len // 2, 0, plain).astype(jnp.float32)
+
+    step = 16
+    freq_x = signed(lax.broadcasted_iota(jnp.int32, (step, LANES), 1))
+    row_index = lax.broadcasted_iota(jnp.int32, (step, LANES), 0)
+
+    def operate(chunk, carry):
+        start = pl.multiple_of(chunk * step, step)
+        freq_y = signed(row_index + start)
+        for j in range(2):
+            freq_z = freq_ref[j]
+            square = freq_x * freq_x + freq_y * freq_y + freq_z * freq_z
+            inverse = 1.0 / jnp.maximum(square, 1.0)
+            scaled = inverse * inverse * green_coef
+            for part in range(2):
+                lanes = pl.ds(part * LANES, LANES)
+
+                def at(comp):
+                    return (comp // 2, 2 * j + comp % 2, pl.ds(start, step), lanes)
+
+                e_xx, e_yy, e_zz, e_yz, e_xz, e_xy = [waves[at(c)] for c in range(COMPS)]
+                trace = (0.5 * lame_lambda) * (e_xx + e_yy + e_zz)
+                n_x = (trace + e_xx) * freq_x + e_xy * freq_y + e_xz * freq_z
+                n_y = e_xy * freq_x + (trace + e_yy) * freq_y + e_yz * freq_z
+                n_z = e_xz * freq_x + e_yz * freq_y + (trace + e_zz) * freq_z
+                along = (freq_x * n_x + freq_y * n_y + freq_z * n_z) * scaled
+                u_x = n_x * inverse - freq_x * along
+                u_y = n_y * inverse - freq_y * along
+                u_z = n_z * inverse - freq_z * along
+                waves[at(0)] = 2.0 * (freq_x * u_x)
+                waves[at(1)] = 2.0 * (freq_y * u_y)
+                waves[at(2)] = 2.0 * (freq_z * u_z)
+                waves[at(3)] = freq_y * u_z + freq_z * u_y
+                waves[at(4)] = freq_x * u_z + freq_z * u_x
+                waves[at(5)] = freq_x * u_y + freq_y * u_x
+        return carry
+
+    lax.fori_loop(0, grid_len // step, operate, 0)
+
+    for tile in range(tile_count):
+        blocks = []
+        for slot in range(4):
+            rows = product(split(waves[tile, slot]), inverse_x)
+            blocks.append(jnp.concatenate([rows[:, :LANES], rows[:, LANES:]], axis=0))
+        for g, block in enumerate(swap_blocks(blocks)):
+            field = product(inverse_y, split(block))
+            out_ref[pl.ds(g * pa_count, pa_count), :, tile, :, :] = field.reshape(
+                pa_count, 2, y_local, LANES
+            )
+
+
+def inverse_z_kernel(
+    x_local,
+    y_local,
+    cell_count,
+    voxel_ref,
+    waves_ref,
+    plastic_ref,
+    high_ref,
+    low_ref,
+    stress_ref,
+    own_ref,
+    low_cells_ref,
+    high_cells_ref,
+):
+    table = (high_ref[...], low_ref[...])
+    half = LANES // 2
+    per_comp = x_local * y_local
+    stride = (COMPS // 2) * y_local
+    first_half = lane_iota(half) < half
+    for pair in range(y_local // 2):
+        elastic = [[None] * COMPS for _ in range(2)]
+        for tile in range(COMPS // 2):
+            base = tile * y_local + 2 * pair
+            even = waves_ref[pl.ds(base, half, stride=stride), :]
+            odd = waves_ref[pl.ds(base + 1, half, stride=stride), :]
+            low_bins = jnp.where(first_half, even, pltpu.roll(odd, half, 1))
+            high_bins = jnp.where(first_half, pltpu.roll(even, half, 1), odd)
+            turned = jnp.concatenate([low_bins, high_bins], axis=0).T
+            lines = product(split(turned), table)
+            for y in range(2):
+                for c in range(2):
+                    begin = (2 * y + c) * x_local
+                    comp = 2 * tile + c
+                    own = plastic_ref[
+                        pl.ds(comp * per_comp + 2 * pair + y, x_local, stride=y_local), :
+                    ]
+                    elastic[y][comp] = lines[begin : begin + x_local] - own
+        for y in range(2):
+            trace = lame_lambda * (elastic[y][0] + elastic[y][1] + elastic[y][2])
+            for comp in range(COMPS):
+                value = 2.0 * shear_modulus * elastic[y][comp]
+                if comp < 3:
+                    value = value + trace
+                stress_ref[
+                    pl.ds(comp * per_comp + 2 * pair + y, x_local, stride=y_local), :
+                ] = value
+
+    cell_rows = per_comp // cell_count
+    lane = lane_iota(LANES)
+    row_lane = lax.broadcasted_iota(jnp.int32, (LANES, cell_rows), 1)
+    for cell in range(cell_count):
+        places = jnp.broadcast_to(voxel_ref[pl.ds(cell, 1), :], (LANES, LANES)).astype(jnp.float32)
+        places = places.T.astype(jnp.int32)
+        picked_row = lax.div(places, LANES)
+        picked_lane = places - picked_row * LANES
+        picked_row = picked_row[:, :1] - cell * cell_rows
+        choose = (row_lane == picked_row).astype(jnp.bfloat16)
+        keep = lane == picked_lane
+        found = jnp.zeros((LANES, LANES), jnp.float32)
+        for comp in range(COMPS):
+            block = stress_ref[pl.ds(comp * per_comp + cell * cell_rows, cell_rows), :]
+            high, low = split(block)
+            rows = jnp.dot(choose, high, preferred_element_type=jnp.float32) + jnp.dot(
+                choose, low, preferred_element_type=jnp.float32
+            )
+            value = jnp.sum(jnp.where(keep, rows, 0.0), axis=1, keepdims=True)
+            found = jnp.where(lane == comp, value, found)
+        found = found.T[:8]
+        own_ref[cell] = found
+        if cell < 2:
+            low_cells_ref[cell] = found
+        if cell >= cell_count - 2:
+            high_cells_ref[cell - cell_count + 2] = found
+
+
+def pair_moments(state, fixed, scratch, first, last):
+    position = state
+    columns, features, moments = scratch
+    slots = position[0].shape[0]
+    lines, burgers = fixed
+    moved = [
+        position[1] * lines[2] - position[2] * lines[1],
+        position[2] * lines[0] - position[0] * lines[2],
+        position[0] * lines[1] - position[1] * lines[0],
+    ]
+    for shift in range(3):
+        offset = shift - 1.0
+        shifted = [moved[0], moved[1] - offset * lines[2], moved[2] + offset * lines[1]]
+        for b in range(3):
+            for a in range(3):
+                features[shift, pl.ds((3 * a + b) * slots, slots), :] = lines[a] * burgers[b]
+                features[shift, pl.ds((9 + 3 * a + b) * slots, slots), :] = shifted[a] * burgers[b]
+    for source in range(first - 1, last + 1):
+        for a in range(3):
+            row = position[a][source : source + 1]
+            columns[source, a] = jnp.broadcast_to(row, (LANES, LANES)).T
+    for target in range(first, last):
+        weights = []
+        sources = []
+        own = [position[a][target : target + 1] for a in range(3)]
+        for shift in range(3):
+            source = target + shift - 1
+            d_x = (own[0] - (shift - 1.0)) - columns[source, 0]
+            d_y = own[1] - columns[source, 1]
+            d_z = own[2] - columns[source, 2]
+            inverse = lax.rsqrt(d_x * d_x + d_y * d_y + d_z * d_z + core_square)
+            weights.append(inverse * inverse * inverse)
+            sources.append(features[shift, pl.ds(source, FEATURES, stride=slots), :])
+        total = product(
+            split(jnp.concatenate(sources, axis=1)), split(jnp.concatenate(weights, axis=0))
+        )
+        moments[pl.ds(target * FEATURES, FEATURES), :] = total
+
+
+def pair_field(position, moments):
+    slots = position[0].shape[0]
+
+    def feature(index):
+        return moments[pl.ds(index, slots, stride=FEATURES), :]
+
+    moment = [[None] * 3 for _ in range(3)]
+    for b in range(3):
+        g = [feature(3 * a + b) for a in range(3)]
+        moment[0][b] = position[1] * g[2] - position[2] * g[1] - feature(9 + b)
+        moment[1][b] = position[2] * g[0] - position[0] * g[2] - feature(12 + b)
+        moment[2][b] = position[0] * g[1] - position[1] * g[0] - feature(15 + b)
+    pairs = ((0, 0), (1, 1), (2, 2), (1, 2), (0, 2), (0, 1))
+    return [pair_factor * (moment[a][b] + moment[b][a]) for a, b in pairs]
+
+
+def load_fixed(start_ref):
+    values = [start_ref[a] for a in range(9)]
+    return values[0:3], values[3:6], values[6:9]
+
+
+def clear(features, moments):
+    features[...] = jnp.zeros_like(features)
+    moments[...] = jnp.zeros_like(moments)
+
+
+def first_field_kernel(last, start_ref, out_ref, columns, features, moments):
+    clear(features, moments)
+    position, lines, burgers = load_fixed(start_ref)
+    pair_moments(position, (lines, burgers), (columns, features, moments), 1, last)
+    for comp, value in enumerate(pair_field(position, moments)):
+        out_ref[comp] = value
+
+
+def moves_kernel(
+    cell_count,
+    start_ref,
+    first_ref,
+    left_ref,
+    own_ref,
+    right_ref,
+    out_ref,
+    columns,
+    features,
+    moments,
+    sampled_ref,
+):
+    clear(features, moments)
+    position, lines, burgers = load_fixed(start_ref)
+    initial = position
+    sampled_ref[...] = jnp.zeros_like(sampled_ref)
+    sampled_ref[pl.ds(8, 16), :] = left_ref[...].reshape(16, LANES)
+    sampled_ref[pl.ds(24, 8 * cell_count), :] = own_ref[...].reshape(8 * cell_count, LANES)
+    sampled_ref[pl.ds(24 + 8 * cell_count, 16), :] = right_ref[...].reshape(16, LANES)
+    slots = position[0].shape[0]
+    sampled = [sampled_ref[pl.ds(comp, slots, stride=8), :] for comp in range(COMPS)]
+    for repeat in range(SUB):
+        if repeat == 0:
+            field = [first_ref[comp] for comp in range(COMPS)]
+        else:
+            pair_moments(
+                position,
+                (lines, burgers),
+                (columns, features, moments),
+                1 + repeat,
+                cell_count + 5 - repeat,
+            )
+            field = pair_field(position, moments)
+        sigma = [sampled[comp] + field[comp] for comp in range(COMPS)]
+        traction = [
+            sigma[full_index[a][0]] * burgers[0]
+            + sigma[full_index[a][1]] * burgers[1]
+            + sigma[full_index[a][2]] * burgers[2]
+            for a in range(3)
+        ]
+        position = [
+            position[0] + step_size * (traction[1] * lines[2] - traction[2] * lines[1]),
+            position[1] + step_size * (traction[2] * lines[0] - traction[0] * lines[2]),
+            position[2] + step_size * (traction[0] * lines[1] - traction[1] * lines[0]),
+        ]
+    for a in range(3):
+        out_ref[a] = (position[a] - initial[a])[3 : 3 + cell_count]
+
+
+def kernel_call(kernel, outs, scratch=(), flops=0, scalars=0, count=0):
+    specs = [pl.BlockSpec(memory_space=pltpu.SMEM)] * scalars
+    specs += [pl.BlockSpec(memory_space=pltpu.VMEM)] * (count - scalars)
+    return pl.pallas_call(
+        kernel,
+        out_shape=outs,
+        in_specs=specs,
+        out_specs=jax.tree.map(lambda _: pl.BlockSpec(memory_space=pltpu.VMEM), outs),
+        scratch_shapes=list(scratch),
+        compiler_params=pltpu.CompilerParams(vmem_limit_bytes=VMEM_LIMIT),
+        cost_estimate=pl.CostEstimate(flops=flops, bytes_accessed=1 << 20, transcendentals=0),
+    )
+
+
+def neighbours(low, high):
+    count = lax.axis_size("gx")
+    forward = [(i, (i + 1) % count) for i in range(count)]
+    backward = [(target, source) for source, target in forward]
+    return lax.ppermute(high, "gx", forward), lax.ppermute(low, "gx", backward)
+
+
+def slab_body(plastic, offsets, lines, burgers, counts, voxels):
+    f32 = jnp.float32
+    comp_count, x_local, y_local, grid_len = plastic.shape
+    gx_count = lax.axis_size("gx")
+    pa_count = lax.axis_size("pa")
+    devices = gx_count * pa_count
+    cell_count, cap = voxels.shape[1:]
+    rows = devices * 2 * (comp_count // 2) * y_local
+    blocks = (devices, rows // devices, LANES)
+    parts = (devices, 2, comp_count // 2, y_local, LANES)
+    forward_z, forward_y, forward_x, inverse_x, inverse_y, inverse_z = [
+        [jnp.asarray(t) for t in pair] for pair in tables(grid_len, pa_count, y_local)
+    ]
+    axes = ("gx", "pa")
+    own = lax.axis_index(axes)
+    bins = (own + devices * jnp.arange(2, dtype=jnp.int32)).astype(f32)
+    flat_plastic = plastic.reshape(-1, grid_len)
+
+    waves = kernel_call(
+        functools.partial(forward_z_kernel, x_local, y_local),
+        jax.ShapeDtypeStruct((rows, LANES), f32),
+        count=3,
+    )(flat_plastic, *forward_z)
+    waves = lax.all_to_all(waves.reshape(blocks), axes, 0, 0, tiled=True)
+    waves = kernel_call(
+        functools.partial(spectral_kernel, gx_count, pa_count, y_local),
+        jax.ShapeDtypeStruct(parts, f32),
+        [pltpu.VMEM((comp_count // 2, 4, grid_len, 2 * grid_len), f32)],
+        count=10,
+        scalars=1,
+    )(bins, waves.reshape(parts), *forward_y, *forward_x, *inverse_x, *inverse_y)
+    waves = lax.all_to_all(waves.reshape(blocks), axes, 0, 0, tiled=True)
+
+    live = (jnp.arange(cap, dtype=jnp.int32)[None, :] < counts[0][:, None]).astype(f32)
+    start = jnp.concatenate([offsets[:, 0], lines[:, 0], burgers[:, 0] * live[None]], axis=0)
+    below, above = neighbours(start[:, :3], start[:, cell_count - 3 :])
+    padding = jnp.zeros((9, SLOTS - cell_count - 6, cap), f32)
+    start = jnp.concatenate([below, start, above, padding], axis=1)
+    pair_scratch = [
+        pltpu.VMEM((SLOTS, 3, LANES, LANES), f32),
+        pltpu.VMEM((3, FEATURES * SLOTS, LANES), f32),
+        pltpu.VMEM((SLOTS * FEATURES, LANES), f32),
+    ]
+    first = kernel_call(
+        functools.partial(first_field_kernel, cell_count + 5),
+        jax.ShapeDtypeStruct((comp_count, SLOTS, cap), f32),
+        pair_scratch,
+        count=1,
+        flops=1 << 28,
+    )(start)
+
+    end = jax.ShapeDtypeStruct((2, 8, cap), f32)
+    stress, own_cells, low_cells, high_cells = kernel_call(
+        functools.partial(inverse_z_kernel, x_local, y_local, cell_count),
+        [
+            jax.ShapeDtypeStruct(flat_plastic.shape, f32),
+            jax.ShapeDtypeStruct((cell_count, 8, cap), f32),
+            end,
+            end,
+        ],
+        count=5,
+    )(voxels[0], waves.reshape(rows, LANES), flat_plastic, *inverse_z)
+    left, right = neighbours(low_cells, high_cells)
+    moved = kernel_call(
+        functools.partial(moves_kernel, cell_count),
+        jax.ShapeDtypeStruct((3, cell_count, cap), f32),
+        pair_scratch + [pltpu.VMEM((8 * SLOTS, LANES), f32)],
+        count=5,
+    )(start, first, left, own_cells, right)
+    return (stress.reshape(plastic.shape), moved[:, None])
+
+
+def fits(mesh, plastic, voxels):
+    gx_count, pa_count = mesh.shape["gx"], mesh.shape["pa"]
+    grid_len = plastic.shape[3]
+    x_local, y_local = plastic.shape[1] // gx_count, plastic.shape[2] // pa_count
+    cell_count = voxels.shape[1] // gx_count
+    return (
+        plastic.shape == (COMPS, LANES, LANES, LANES)
+        and 4 * gx_count * pa_count == grid_len
+        and 4 * x_local == LANES
+        and y_local % 8 == 0
+        and voxels.shape[2] == LANES
+        and 3 <= cell_count <= SLOTS - 6
+        and x_local % cell_count == 0
+    )
+
+
 def solution(mesh):
     placed = (
         P(None, "gx", "pa", None),
@@ -221,10 +718,15 @@
         P("pa", "gx"),
         P("pa", "gx", None),
     )
-    return jax.shard_map(
-        body,
-        mesh=mesh,
-        in_specs=placed,
-        out_specs=(P(None, "gx", "pa", None), P(None, "pa", "gx", None)),
-        check_vma=False,
-    )
+
+    def step(plastic, offsets, lines, burgers, counts, voxels):
+        chosen = slab_body if fits(mesh, plastic, voxels) else body
+        return jax.shard_map(
+            chosen,
+            mesh=mesh,
+            in_specs=placed,
+            out_specs=(P(None, "gx", "pa", None), P(None, "pa", "gx", None)),
+            check_vma=False,
+        )(plastic, offsets, lines, burgers, counts, voxels)
+
+    return step

time: 459 us -> 114 us (0.25); the launches traced: 452 us -> 113 us
  local copies, waits for them, and re-layouts: 240 us -> 3.09 us
  waiting for transfers between devices: 120 us -> 75.2 us
  other arithmetic: 34.2 us -> 0.16 us
  matrix products: 25.9 us -> 0 us
  Pallas kernels: 0 us -> 18.2 us
  starting transfers between devices: 30.5 us -> 15.7 us
    unnamed x28 -> x38, local copies, waits for them, and re-layouts: 76.1 us -> 3 us
    all_to_all x8 -> x0, local copies, waits for them, and re-layouts: 49.7 us -> none  [the longest x4 34.3 us: body(): field = lax.all_to_all(field, 'gx', split_axis=4, concat_axis=1, tiled=True)]
    all_to_all x4 -> x2, waiting for transfers between devices: 114 us -> 65.4 us  [slab_body(): waves = lax.all_to_all(waves.reshape(blocks), axes, 0, 0, tiled=True)]
    dot_general x8 -> x0, local copies, waits for them, and re-layouts: 38.7 us -> none  [the longest x7 36.5 us: transform_last(): result = jnp.dot(flat, matrix, precision=lax.Precision.HIGHEST)]
    all_to_all x4 -> x0, other arithmetic: 27.5 us -> none  [the longest x2 14.1 us: body(): field = lax.all_to_all(field, 'gx', split_axis=4, concat_axis=1, tiled=True)]
    dot_general x9 -> x0, matrix products: 25.9 us -> none  [the longest x4 12 us: transform_last(): result = jnp.dot(flat, matrix, precision=lax.Precision.HIGHEST)]
    transpose x4 -> x0, local copies, waits for them, and re-layouts: 22.8 us -> none  [the longest x2 16.7 us: body(): field = jnp.transpose(field, (0, 1, 4, 3, 2))]
    reshape x3 -> x0, local copies, waits for them, and re-layouts: 20.5 us -> none  [the longest x2 15.3 us: body(): field = field.reshape(comp_count, x_local, y_local, 2, bin_count)]
  transfers between devices with their start and end apart: 12 -> 6, of which waited for: 10 -> 5; matrix products, arithmetic and copies ran while one was open for 1% -> 0% of each run, Pallas kernels for 0% -> 1%
where the time goes in v1:
time: 114 us; the launch traced here: 113 us
  waiting for transfers between devices  75.2 us (66%)
  Pallas kernels  18.2 us (16%)
  starting transfers between devices  15.7 us (14%)
  local copies, waits for them, and re-layouts  3.09 us (3%)
    all_to_all x2, waiting for transfers between devices, slab_body(): waves = lax.all_to_all(waves.reshape(blocks), axes, 0, 0, tiled=True)  65.4 us
    all_to_all x2, starting transfers between devices, slab_body(): waves = lax.all_to_all(waves.reshape(blocks), axes, 0, 0, tiled=True)  10.1 us
    ppermute x2, waiting for transfers between devices, neighbours(): lax.ppermute(low, 'gx', backward)  8.26 us
    pallas_call x1, Pallas kernels, slab_body(): kernel_call(functools.partial(spectral_kernel, gx_count, pa_count, y_loca...  7.91 us
    ppermute x2, starting transfers between devices, neighbours(): lax.ppermute(low, 'gx', backward)  5.53 us
    pallas_call x1, Pallas kernels, slab_body(): kernel_call(functools.partial(inverse_z_kernel, x_local, y_local, cell_co...  3.37 us
    pallas_call x1, Pallas kernels, slab_body(): kernel_call(functools.partial(forward_z_kernel, x_local, y_local), jax.Sh...  3.35 us
    unnamed x38, local copies, waits for them, and re-layouts  3 us
  transfers between devices with their start and end apart: 6, of which 5 were waited for; matrix products, arithmetic and copies ran while one was open for 0% of the time, Pallas kernels for 1%

profile of v1, /device:TPU:0, one launch (start us, length us, event | category | flops | bytes accessed | tf_op | source)
XLA Modules:
  0.0 113.2 jit_solution(2572694421560193122)
XLA Ops:
  0.6 0.0 copy-start
  0.6 1.4 %copy-done = f32[6,32,16,128]{3,2,1,0:T(8,128)S(1)} copy-done((f32[6,32,16,128]{3,2,1,0:T(8,128)S(1)}, f32[6,32,16,128]{3,2,1,0:T(8,128)}, u32[]{:S(2)}) %copy-start) | copy-done | bytes 1572888
  2.0 0.8 copy-done.12
  2.8 0.8 copy-done.13
  3.6 3.3 %shard_map.185 = f32[3072,128]{1,0:T(8,128)} custom-call(f32[3072,128]{1,0:T(8,128)S(1)} %bitcast.16, bf16[128,128]{1,0:T(8,128)(2,1)S(1)} %copy-done.12, bf16[128,128]{1,0:T(8,128)(2,1)S(1)} %copy-done.13), custom_call_target="tpu_custom_call" | custom-call | bytes 1048576 | tf_op jit(solution)/shard_map/pallas_call | solution.py:642
  6.9 0.0 copy-start.6
  6.9 0.0 copy-start.7
  6.9 0.0 copy-start.8
  7.0 0.0 copy-start.9
  7.0 7.3 %all-to-all-start = ((f32[32,96,128]{2,1,0:T(8,128)}), f32[32,96,128]{2,1,0:T(8,128)S(1)}, u32[]{:S(2)}, u32[]{:S(2)}) async-start(f32[32,96,128]{2,1,0:T(8,128)} %bitcast.2), calls=%async_computation | async-start | bytes 3145728 | tf_op jit(solution)/shard_map/all_to_all | solution.py:647
  14.3 38.9 %all-to-all-done = f32[32,96,128]{2,1,0:T(8,128)S(1)} async-done(((f32[32,96,128]{2,1,0:T(8,128)}), f32[32,96,128]{2,1,0:T(8,128)S(1)}, u32[]{:S(2)}, u32[]{:S(2)}) %all-to-all-start) | async-done | bytes 1572896 | tf_op jit(solution)/shard_map/all_to_all | solution.py:647
  53.1 0.0 copy-done.2
  53.1 0.0 copy-done.3
  53.1 0.0 copy-done.4
  53.1 0.0 copy-done.5
  53.2 0.0 copy-done.6
  53.2 0.0 copy-done.7
  53.2 0.0 copy-done.8
  53.2 0.0 copy-done.9
  53.2 7.9 %shard_map.186 = f32[32,2,3,16,128]{4,3,2,1,0:T(8,128)} custom-call(f32[2]{0:T(128)S(1)} %add_convert_fusion.freq_ref, f32[32,2,3,16,128]{4,3,2,1,0:T(8,128)S(1)} %bitcast.15, bf16[256,256]{1,0:T(8,128)(2,1)S(1)} %copy-done.2, bf16[256,256]{1,0:T(8,128)(2,1)S(1)} %copy-done.3, bf16[256,256]{1,0:T(8,128)(2,1)S(1)} %copy-done.4, ...), custom_call_target="tpu_custom_call" | custom-call | bytes 1048576 | tf_op jit(solution)/shard_map/pallas_call | solution.py:648
  61.1 0.0 copy-start.1
  61.1 0.0 copy-start.10
  61.1 0.0 copy-start.11
  61.2 0.0 copy-start.14
  61.2 2.8 %all-to-all-start.1 = ((f32[32,96,128]{2,1,0:T(8,128)}), f32[32,96,128]{2,1,0:T(8,128)S(1)}, u32[]{:S(2)}, u32[]{:S(2)}) async-start(f32[32,96,128]{2,1,0:T(8,128)} %bitcast.4), calls=%async_computation.1 | async-start | bytes 3145728 | tf_op jit(solution)/shard_map/all_to_all | solution.py:655
  64.0 0.0 copy-done.18
  64.0 0.1 fusion
  64.1 0.0 copy-done.17
  64.1 0.0 copy-done.15
  64.1 0.0 copy-done.16
  64.1 2.6 %collective-permute-start.1 = (f32[9,3,128]{2,1,0:T(4,128)S(1)}, f32[9,3,128]{2,1,0:T(4,128)S(1)}, u32[]{:S(2)}, u32[]{:S(2)}) collective-permute-start(f32[9,3,128]{2,1,0:T(4,128)S(1)} %get-tuple-element.13), channel_id=1, source_target_pairs={{8,0},{16,8},{24,16},{0,24},{9,1},{17,9},{25,17},{1,25},{10,2},{18... | collective-permute-start | bytes 41480 | tf_op jit(solution)/shard_map/ppermute | solution.py:621
  66.8 0.0 collective-permute-start
  66.8 0.1 pad.5.clone
  66.9 8.3 %collective-permute-done.1 = f32[9,3,128]{2,1,0:T(4,128)S(1)} collective-permute-done((f32[9,3,128]{2,1,0:T(4,128)S(1)}, f32[9,3,128]{2,1,0:T(4,128)S(1)}, u32[]{:S(2)}, u32[]{:S(2)}) %collective-permute-start.1) | collective-permute-done | bytes 13856 | tf_op jit(solution)/shard_map/ppermute | solution.py:621
  75.1 1.2 %collective-permute-done = f32[9,3,128]{2,1,0:T(4,128)S(1)} collective-permute-done((f32[9,3,128]{2,1,0:T(4,128)S(1)}, f32[9,3,128]{2,1,0:T(4,128)S(1)}, u32[]{:S(2)}, u32[]{:S(2)}) %collective-permute-start) | collective-permute-done | bytes 13856 | tf_op jit(solution)/shard_map/ppermute | solution.py:621
  76.3 0.1 maximum_maximum_fusion.start_ref
  76.3 26.5 %all-to-all-done.1 = f32[32,96,128]{2,1,0:T(8,128)S(1)} async-done(((f32[32,96,128]{2,1,0:T(8,128)}), f32[32,96,128]{2,1,0:T(8,128)S(1)}, u32[]{:S(2)}, u32[]{:S(2)}) %all-to-all-start.1) | async-done | bytes 1572896 | tf_op jit(solution)/shard_map/all_to_all | solution.py:655
  102.9 0.0 copy-done.1
  102.9 0.0 copy-done.10
  102.9 0.0 copy-done.11
  102.9 0.0 copy-done.14
  102.9 3.4 %shard_map.187 = (f32[3072,128]{1,0:T(8,128)}, f32[4,8,128]{2,1,0:T(8,128)S(1)}, f32[2,8,128]{2,1,0:T(8,128)S(1)}, f32[2,8,128]{2,1,0:T(8,128)S(1)}) custom-call(s32[4,128]{1,0:T(4,128)S(1)} %bitcast.19, f32[3072,128]{1,0:T(8,128)S(1)} %bitcast.18, f32[3072,128]{1,0:T(8,128)S(1)} %bitcast.17, bf16[128,128]{1,0:T(8,128)(2,1)S(1)} %copy-done.10, ...), custom_call_target="tpu_custom_call" | custom-call | bytes 1048576 | tf_op jit(solution)/shard_map/pallas_call | solution.py:676
  106.3 0.0 collective-permute-start.2
  106.3 2.9 %collective-permute-start.3 = (f32[2,8,128]{2,1,0:T(8,128)S(1)}, f32[2,8,128]{2,1,0:T(8,128)S(1)}, u32[]{:S(2)}, u32[]{:S(2)}) collective-permute-start(f32[2,8,128]{2,1,0:T(8,128)S(1)} %get-tuple-element.9), channel_id=1, source_target_pairs={{8,0},{16,8},{24,16},{0,24},{9,1},{17,9},{25,17},{1,25},{10,2},{18... | collective-permute-start | bytes 24584 | tf_op jit(solution)/shard_map/ppermute | solution.py:621
  109.2 1.3 %shard_map.188.first_ref = f32[6,16,128]{2,1,0:T(8,128)S(1)} custom-call(f32[9,16,128]{2,1,0:T(8,128)S(1)} %maximum_maximum_fusion.start_ref), custom_call_target="tpu_custom_call" | custom-call | flops 268435456 | bytes 1048576 | tf_op jit(solution)/shard_map/pallas_call | solution.py:667
  110.5 0.4 collective-permute-done.2.left_ref
  110.8 0.0 collective-permute-done.3.right_ref
  110.8 2.4 %shard_map.189 = f32[3,4,128]{2,1,0:T(4,128)} custom-call(f32[9,16,128]{2,1,0:T(8,128)S(1)} %maximum_maximum_fusion.start_ref, f32[6,16,128]{2,1,0:T(8,128)S(1)} %shard_map.188.first_ref, f32[2,8,128]{2,1,0:T(8,128)S(1)} %collective-permute-done.2.left_ref, f32[4,8,128]{2,1,0:T(8,128)S(1)} %get-tuple-element.8.own_ref, ...), custom_call_target="tpu_custom_call" | custom-call | bytes 1048576 | tf_op jit(solution)/shard_map/pallas_call | solution.py:687
  (15 shorter events, 0.0 us)
Async XLA Ops:
  0.6 1.4 %copy-start = (f32[6,32,16,128]{3,2,1,0:T(8,128)S(1)}, f32[6,32,16,128]{3,2,1,0:T(8,128)}, u32[]{:S(2)}) copy-start(f32[6,32,16,128]{3,2,1,0:T(8,128)} %param.18) | copy-start | bytes 4718596
  2.0 0.8 copy-start.12
  2.8 0.8 copy-start.13
  6.9 46.2 %copy-start.2 = (bf16[256,256]{1,0:T(8,128)(2,1)S(1)}, bf16[256,256]{1,0:T(8,128)(2,1)}, u32[]{:S(2)}) copy-start(bf16[256,256]{1,0:T(8,128)(2,1)} %constant.40.clone.fyh_ref) | copy-start | bytes 393220
  6.9 46.2 %copy-start.3 = (bf16[256,256]{1,0:T(8,128)(2,1)S(1)}, bf16[256,256]{1,0:T(8,128)(2,1)}, u32[]{:S(2)}) copy-start(bf16[256,256]{1,0:T(8,128)(2,1)} %constant.41.clone.fyl_ref) | copy-start | bytes 393220
  6.9 46.2 %copy-start.4 = (bf16[256,256]{1,0:T(8,128)(2,1)S(1)}, bf16[256,256]{1,0:T(8,128)(2,1)}, u32[]{:S(2)}) copy-start(bf16[256,256]{1,0:T(8,128)(2,1)} %constant.42.clone.fxh_ref) | copy-start | bytes 393220
  6.9 46.2 %copy-start.5 = (bf16[256,256]{1,0:T(8,128)(2,1)S(1)}, bf16[256,256]{1,0:T(8,128)(2,1)}, u32[]{:S(2)}) copy-start(bf16[256,256]{1,0:T(8,128)(2,1)} %constant.43.clone.fxl_ref) | copy-start | bytes 393220
  6.9 46.2 %copy-start.6 = (bf16[256,256]{1,0:T(8,128)(2,1)S(1)}, bf16[256,256]{1,0:T(8,128)(2,1)}, u32[]{:S(2)}) copy-start(bf16[256,256]{1,0:T(8,128)(2,1)} %constant.44.clone.ixh_ref) | copy-start | bytes 393220
  6.9 46.2 %copy-start.7 = (bf16[256,256]{1,0:T(8,128)(2,1)S(1)}, bf16[256,256]{1,0:T(8,128)(2,1)}, u32[]{:S(2)}) copy-start(bf16[256,256]{1,0:T(8,128)(2,1)} %constant.45.clone.ixl_ref) | copy-start | bytes 393220
  6.9 46.2 %copy-start.8 = (bf16[256,256]{1,0:T(8,128)(2,1)S(1)}, bf16[256,256]{1,0:T(8,128)(2,1)}, u32[]{:S(2)}) copy-start(bf16[256,256]{1,0:T(8,128)(2,1)} %constant.46.clone.iyh_ref) | copy-start | bytes 393220
  7.0 46.2 %copy-start.9 = (bf16[256,256]{1,0:T(8,128)(2,1)S(1)}, bf16[256,256]{1,0:T(8,128)(2,1)}, u32[]{:S(2)}) copy-start(bf16[256,256]{1,0:T(8,128)(2,1)} %constant.47.clone.iyl_ref) | copy-start | bytes 393220
  7.0 46.2 %all-to-all-start = ((f32[32,96,128]{2,1,0:T(8,128)}), f32[32,96,128]{2,1,0:T(8,128)S(1)}, u32[]{:S(2)}, u32[]{:S(2)}) async-start(f32[32,96,128]{2,1,0:T(8,128)} %bitcast.2), calls=%async_computation | async-start | bytes 3145728 | tf_op jit(solution)/shard_map/all_to_all | solution.py:647
  61.1 2.9 %copy-start.18 = (s32[1,4]{1,0:T(1,128)S(1)}, s32[1,4]{1,0:T(1,128)}, u32[]{:S(2)}) copy-start(s32[1,4]{1,0:T(1,128)} %param.22) | copy-start | bytes 52
  61.1 3.0 %copy-start.17 = (f32[3,1,4,128]{3,2,1,0:T(4,128)S(1)}, f32[3,1,4,128]{3,2,1,0:T(4,128)}, u32[]{:S(2)}) copy-start(f32[3,1,4,128]{3,2,1,0:T(4,128)} %param.21) | copy-start | bytes 18436
  61.1 3.0 %copy-start.15 = (f32[3,1,4,128]{3,2,1,0:T(4,128)S(1)}, f32[3,1,4,128]{3,2,1,0:T(4,128)}, u32[]{:S(2)}) copy-start(f32[3,1,4,128]{3,2,1,0:T(4,128)} %param.20) | copy-start | bytes 18436
  61.1 3.0 %copy-start.16 = (f32[3,1,4,128]{3,2,1,0:T(4,128)S(1)}, f32[3,1,4,128]{3,2,1,0:T(4,128)}, u32[]{:S(2)}) copy-start(f32[3,1,4,128]{3,2,1,0:T(4,128)} %param.19) | copy-start | bytes 18436
  61.1 41.8 %copy-start.1 = (f32[6,32,16,128]{3,2,1,0:T(8,128)S(1)}, f32[6,32,16,128]{3,2,1,0:T(8,128)}, u32[]{:S(2)}) copy-start(f32[6,32,16,128]{3,2,1,0:T(8,128)} %param.18) | copy-start | bytes 4718596
  61.1 41.8 %copy-start.10 = (bf16[128,128]{1,0:T(8,128)(2,1)S(1)}, bf16[128,128]{1,0:T(8,128)(2,1)}, u32[]{:S(2)}) copy-start(bf16[128,128]{1,0:T(8,128)(2,1)} %constant.48.clone.high_ref) | copy-start | bytes 98308
  61.1 41.7 %copy-start.11 = (bf16[128,128]{1,0:T(8,128)(2,1)S(1)}, bf16[128,128]{1,0:T(8,128)(2,1)}, u32[]{:S(2)}) copy-start(bf16[128,128]{1,0:T(8,128)(2,1)} %constant.49.clone.low_ref) | copy-start | bytes 98308
  61.2 41.7 %copy-start.14 = (s32[1,4,128]{2,1,0:T(4,128)S(1)}, s32[1,4,128]{2,1,0:T(4,128)}, u32[]{:S(2)}) copy-start(s32[1,4,128]{2,1,0:T(4,128)} %param.23) | copy-start | bytes 6148
  61.2 41.7 %all-to-all-start.1 = ((f32[32,96,128]{2,1,0:T(8,128)}), f32[32,96,128]{2,1,0:T(8,128)S(1)}, u32[]{:S(2)}, u32[]{:S(2)}) async-start(f32[32,96,128]{2,1,0:T(8,128)} %bitcast.4), calls=%async_computation.1 | async-start | bytes 3145728 | tf_op jit(solution)/shard_map/all_to_all | solution.py:655
  64.1 11.0 %collective-permute-start.1 = (f32[9,3,128]{2,1,0:T(4,128)S(1)}, f32[9,3,128]{2,1,0:T(4,128)S(1)}, u32[]{:S(2)}, u32[]{:S(2)}) collective-permute-start(f32[9,3,128]{2,1,0:T(4,128)S(1)} %get-tuple-element.13), channel_id=1, source_target_pairs={{8,0},{16,8},{24,16},{0,24},{9,1},{17,9},{25,17},{1,25},{10,2},{18... | collective-permute-start | bytes 41480 | tf_op jit(solution)/shard_map/ppermute | solution.py:621
  66.8 9.5 %collective-permute-start = (f32[9,3,128]{2,1,0:T(4,128)S(1)}, f32[9,3,128]{2,1,0:T(4,128)S(1)}, u32[]{:S(2)}, u32[]{:S(2)}) collective-permute-start(f32[9,3,128]{2,1,0:T(4,128)S(1)} %get-tuple-element.12), channel_id=1, source_target_pairs={{0,8},{8,16},{16,24},{24,0},{1,9},{9,17},{17,25},{25,1},{2,10},{10... | collective-permute-start | bytes 41480 | tf_op jit(solution)/shard_map/ppermute | solution.py:621
  106.3 4.6 %collective-permute-start.2 = (f32[2,8,128]{2,1,0:T(8,128)S(1)}, f32[2,8,128]{2,1,0:T(8,128)S(1)}, u32[]{:S(2)}, u32[]{:S(2)}) collective-permute-start(f32[2,8,128]{2,1,0:T(8,128)S(1)} %get-tuple-element.7), channel_id=1, source_target_pairs={{0,8},{8,16},{16,24},{24,0},{1,9},{9,17},{17,25},{25,1},{2,10},{10... | collective-permute-start | bytes 24584 | tf_op jit(solution)/shard_map/ppermute | solution.py:621
  106.3 4.5 %collective-permute-start.3 = (f32[2,8,128]{2,1,0:T(8,128)S(1)}, f32[2,8,128]{2,1,0:T(8,128)S(1)}, u32[]{:S(2)}, u32[]{:S(2)}) collective-permute-start(f32[2,8,128]{2,1,0:T(8,128)S(1)} %get-tuple-element.9), channel_id=1, source_target_pairs={{8,0},{16,8},{24,16},{0,24},{9,1},{17,9},{25,17},{1,25},{10,2},{18... | collective-permute-start | bytes 24584 | tf_op jit(solution)/shard_map/ppermute | solution.py:621

commit v2 on v1

--- a/solution.py
+++ b/solution.py
@@ -222,6 +222,7 @@
 FEATURES = 24
 SLOTS = 16
 VMEM_LIMIT = 48 * 1024 * 1024
+VMEM_WHOLE = 63 * 1024 * 1024
 
 
 def split(value):
@@ -234,18 +235,17 @@
     table = np.asarray(table, np.float32)
     high = table.astype(ml_dtypes.bfloat16)
     low = (table - high.astype(np.float32)).astype(ml_dtypes.bfloat16)
-    return high, low
+    return np.stack([high, low])
 
 
 def product(left, right, dims=((1,), (0,))):
-    def one(first, second):
-        return lax.dot_general(
-            first, second, (dims, ((), ())), preferred_element_type=jnp.float32
-        )
-
     left_high, left_low = left
     right_high, right_low = right
-    return one(left_high, right_high) + (one(left_high, right_low) + one(left_low, right_high))
+    left_all = jnp.concatenate([left_high, left_high, left_low], axis=dims[0][0])
+    right_all = jnp.concatenate([right_high, right_low, right_high], axis=dims[1][0])
+    return lax.dot_general(
+        left_all, right_all, (dims, ((), ())), preferred_element_type=jnp.float32
+    )
 
 
 def tables(grid_len, pa_count, y_local):
@@ -277,27 +277,51 @@
     return lax.broadcasted_iota(jnp.int32, (rows, LANES), 1)
 
 
-def forward_z_kernel(x_local, y_local, plane_ref, high_ref, low_ref, out_ref):
-    table = (high_ref[...], low_ref[...])
+def forward_z_kernel(
+    x_local,
+    y_local,
+    plane_ref,
+    table_ref,
+    out_ref,
+    planes,
+    table,
+    table_sem,
+    in_sems,
+):
     half = LANES // 2
+    tiles = COMPS // 2
     per_comp = x_local * y_local
-    stride = (COMPS // 2) * y_local
     first_half = lane_iota(half) < half
-    for pair in range(y_local // 2):
-        for tile in range(COMPS // 2):
+    fetch_table = pltpu.make_async_copy(table_ref, table, table_sem)
+    fetch_table.start()
+    fetches = []
+    for tile in range(tiles):
+        span = pl.ds(2 * tile * per_comp, 2 * per_comp)
+        fetches.append(
+            pltpu.make_async_copy(plane_ref.at[span], planes.at[span], in_sems.at[tile])
+        )
+        fetches[-1].start()
+    fetch_table.wait()
+    stride = tiles * y_local
+    for tile in range(tiles):
+        fetches[tile].wait()
+        for base in range(0, y_local, 4):
             rows = [
-                plane_ref[pl.ds((2 * tile + c) * per_comp + 2 * pair + y, x_local, stride=y_local), :]
-                for y in range(2)
+                planes[pl.ds((2 * tile + c) * per_comp + base + y, x_local, stride=y_local), :]
+                for y in range(4)
                 for c in range(2)
             ]
             lines = split(jnp.concatenate(rows, axis=0))
-            waves = product(table, lines, ((1,), (1,)))
-            low_bins, high_bins = waves[:half], waves[half:]
-            even = jnp.where(first_half, low_bins, pltpu.roll(high_bins, half, 1))
-            odd = jnp.where(first_half, pltpu.roll(low_bins, half, 1), high_bins)
-            base = tile * y_local + 2 * pair
-            out_ref[pl.ds(base, half, stride=stride), :] = even
-            out_ref[pl.ds(base + 1, half, stride=stride), :] = odd
+            waves = product((table[0], table[1]), lines, ((1,), (1,)))
+            for y in range(0, 4, 2):
+                begin = y * LANES // 2
+                low_bins = waves[:half, begin : begin + LANES]
+                high_bins = waves[half:, begin : begin + LANES]
+                even = jnp.where(first_half, low_bins, pltpu.roll(high_bins, half, 1))
+                odd = jnp.where(first_half, pltpu.roll(low_bins, half, 1), high_bins)
+                begin = tile * y_local + base + y
+                out_ref[pl.ds(begin, half, stride=stride), :] = even
+                out_ref[pl.ds(begin + 1, half, stride=stride), :] = odd
 
 
 def swap_blocks(tiles):
@@ -322,29 +346,29 @@
     y_local,
     freq_ref,
     data_ref,
-    fyh_ref,
-    fyl_ref,
-    fxh_ref,
-    fxl_ref,
-    ixh_ref,
-    ixl_ref,
-    iyh_ref,
-    iyl_ref,
+    forward_y_ref,
+    forward_x_ref,
+    inverse_x_ref,
+    inverse_y_ref,
     out_ref,
     waves,
+    blocks_ref,
+    sems,
 ):
     grid_len = LANES
     size = 2 * grid_len
     tile_count = COMPS // 2
-    forward_y = (fyh_ref[...], fyl_ref[...])
-    forward_x = (fxh_ref[...], fxl_ref[...])
-    inverse_x = (ixh_ref[...], ixl_ref[...])
-    inverse_y = (iyh_ref[...], iyl_ref[...])
+    forward_y = (forward_y_ref[0], forward_y_ref[1])
+    forward_x = (forward_x_ref[0], forward_x_ref[1])
+    inverse_x = (inverse_x_ref[0], inverse_x_ref[1])
+    inverse_y = (inverse_y_ref[0], inverse_y_ref[1])
     for tile in range(tile_count):
-        blocks = []
-        for g in range(gx_count):
-            field = data_ref[pl.ds(g * pa_count, pa_count), :, tile, :, :].reshape(size, LANES)
-            blocks.append(product(forward_y, split(field)))
+        fields = [
+            data_ref[pl.ds(g * pa_count, pa_count), :, tile, :, :].reshape(size, LANES)
+            for g in range(gx_count)
+        ]
+        wide = product(forward_y, split(jnp.concatenate(fields, axis=1)))
+        blocks = [wide[:, g * LANES : (g + 1) * LANES] for g in range(gx_count)]
         for slot, block in enumerate(swap_blocks(blocks)):
             rows = jnp.concatenate([block[:grid_len], block[grid_len:]], axis=1)
             waves[tile, slot] = product(split(rows), forward_x)
@@ -390,16 +414,21 @@
 
     lax.fori_loop(0, grid_len // step, operate, 0)
 
+    stores = []
     for tile in range(tile_count):
         blocks = []
         for slot in range(4):
             rows = product(split(waves[tile, slot]), inverse_x)
             blocks.append(jnp.concatenate([rows[:, :LANES], rows[:, LANES:]], axis=0))
-        for g, block in enumerate(swap_blocks(blocks)):
-            field = product(inverse_y, split(block))
-            out_ref[pl.ds(g * pa_count, pa_count), :, tile, :, :] = field.reshape(
-                pa_count, 2, y_local, LANES
-            )
+        wide = jnp.concatenate(swap_blocks(blocks), axis=1)
+        wide = product(inverse_y, split(wide))
+        for g in range(gx_count):
+            blocks_ref[tile, pl.ds(g * size, size), :] = wide[:, g * LANES : (g + 1) * LANES]
+        done = blocks_ref.at[tile].reshape(gx_count * pa_count, 2, y_local, LANES)
+        stores.append(pltpu.make_async_copy(done, out_ref.at[:, :, tile], sems.at[tile]))
+        stores[-1].start()
+    for store in stores:
+        store.wait()
 
 
 def inverse_z_kernel(
@@ -409,14 +438,13 @@
     voxel_ref,
     waves_ref,
     plastic_ref,
-    high_ref,
-    low_ref,
+    table_ref,
     stress_ref,
     own_ref,
     low_cells_ref,
     high_cells_ref,
 ):
-    table = (high_ref[...], low_ref[...])
+    table = (table_ref[0], table_ref[1])
     half = LANES // 2
     per_comp = x_local * y_local
     stride = (COMPS // 2) * y_local
@@ -600,18 +628,21 @@
         out_ref[a] = (position[a] - initial[a])[3 : 3 + cell_count]
 
 
-def kernel_call(kernel, outs, scratch=(), flops=0, scalars=0, count=0):
-    specs = [pl.BlockSpec(memory_space=pltpu.SMEM)] * scalars
-    specs += [pl.BlockSpec(memory_space=pltpu.VMEM)] * (count - scalars)
+def kernel_call(kernel, outs, scratch=(), flops=0, places="", out_places="", limit=VMEM_LIMIT):
+    spaces = {"s": pltpu.SMEM, "v": pltpu.VMEM, "h": pltpu.HBM}
     return pl.pallas_call(
         kernel,
         out_shape=outs,
-        in_specs=specs,
-        out_specs=jax.tree.map(lambda _: pl.BlockSpec(memory_space=pltpu.VMEM), outs),
+        in_specs=[pl.BlockSpec(memory_space=spaces[p]) for p in places],
+        out_specs=[pl.BlockSpec(memory_space=spaces[p]) for p in out_places],
         scratch_shapes=list(scratch),
-        compiler_params=pltpu.CompilerParams(vmem_limit_bytes=VMEM_LIMIT),
+        compiler_params=pltpu.CompilerParams(vmem_limit_bytes=limit),
         cost_estimate=pl.CostEstimate(flops=flops, bytes_accessed=1 << 20, transcendentals=0),
     )
+
+
+def in_hbm(array):
+    return pltpu.with_memory_space_constraint(array, pltpu.HBM)
 
 
 def neighbours(low, high):
@@ -628,30 +659,48 @@
     pa_count = lax.axis_size("pa")
     devices = gx_count * pa_count
     cell_count, cap = voxels.shape[1:]
-    rows = devices * 2 * (comp_count // 2) * y_local
+    tiles = comp_count // 2
+    rows = devices * 2 * tiles * y_local
     blocks = (devices, rows // devices, LANES)
-    parts = (devices, 2, comp_count // 2, y_local, LANES)
+    parts = (devices, 2, tiles, y_local, LANES)
     forward_z, forward_y, forward_x, inverse_x, inverse_y, inverse_z = [
-        [jnp.asarray(t) for t in pair] for pair in tables(grid_len, pa_count, y_local)
+        jnp.asarray(t) for t in tables(grid_len, pa_count, y_local)
     ]
     axes = ("gx", "pa")
     own = lax.axis_index(axes)
     bins = (own + devices * jnp.arange(2, dtype=jnp.int32)).astype(f32)
     flat_plastic = plastic.reshape(-1, grid_len)
-
-    waves = kernel_call(
+    tile_sems = pltpu.SemaphoreType.DMA((tiles,))
+
+    bins, flat_plastic = lax.optimization_barrier((bins, flat_plastic))
+
+    (waves,) = kernel_call(
         functools.partial(forward_z_kernel, x_local, y_local),
-        jax.ShapeDtypeStruct((rows, LANES), f32),
-        count=3,
-    )(flat_plastic, *forward_z)
+        [pltpu.VMEM((rows, LANES), f32)],
+        [
+            pltpu.VMEM(flat_plastic.shape, f32),
+            pltpu.VMEM(forward_z.shape, jnp.bfloat16),
+            pltpu.SemaphoreType.DMA,
+            tile_sems,
+        ],
+        places="hh",
+        out_places="v",
+    )(in_hbm(flat_plastic), in_hbm(forward_z))
     waves = lax.all_to_all(waves.reshape(blocks), axes, 0, 0, tiled=True)
-    waves = kernel_call(
+    (waves,) = kernel_call(
         functools.partial(spectral_kernel, gx_count, pa_count, y_local),
-        jax.ShapeDtypeStruct(parts, f32),
-        [pltpu.VMEM((comp_count // 2, 4, grid_len, 2 * grid_len), f32)],
-        count=10,
-        scalars=1,
-    )(bins, waves.reshape(parts), *forward_y, *forward_x, *inverse_x, *inverse_y)
+        [jax.ShapeDtypeStruct(parts, f32)],
+        [
+            pltpu.VMEM((tiles, 4, grid_len, 2 * grid_len), f32),
+            pltpu.VMEM((tiles, rows // tiles, LANES), f32),
+            tile_sems,
+        ],
+        places="svvvvv",
+        out_places="h",
+    )(bins, waves.reshape(parts), forward_y, forward_x, inverse_x, inverse_y)
+    waves, offsets, lines, burgers, counts = lax.optimization_barrier(
+        (waves, offsets, lines, burgers, counts)
+    )
     waves = lax.all_to_all(waves.reshape(blocks), axes, 0, 0, tiled=True)
 
     live = (jnp.arange(cap, dtype=jnp.int32)[None, :] < counts[0][:, None]).astype(f32)
@@ -664,12 +713,12 @@
         pltpu.VMEM((3, FEATURES * SLOTS, LANES), f32),
         pltpu.VMEM((SLOTS * FEATURES, LANES), f32),
     ]
-    first = kernel_call(
+    (first,) = kernel_call(
         functools.partial(first_field_kernel, cell_count + 5),
-        jax.ShapeDtypeStruct((comp_count, SLOTS, cap), f32),
+        [jax.ShapeDtypeStruct((comp_count, SLOTS, cap), f32)],
         pair_scratch,
-        count=1,
-        flops=1 << 28,
+        places="v",
+        out_places="v",
     )(start)
 
     end = jax.ShapeDtypeStruct((2, 8, cap), f32)
@@ -681,14 +730,16 @@
             end,
             end,
         ],
-        count=5,
-    )(voxels[0], waves.reshape(rows, LANES), flat_plastic, *inverse_z)
+        places="vvvv",
+        out_places="vvvv",
+    )(voxels[0], waves.reshape(rows, LANES), flat_plastic, inverse_z)
     left, right = neighbours(low_cells, high_cells)
-    moved = kernel_call(
+    (moved,) = kernel_call(
         functools.partial(moves_kernel, cell_count),
-        jax.ShapeDtypeStruct((3, cell_count, cap), f32),
+        [jax.ShapeDtypeStruct((3, cell_count, cap), f32)],
         pair_scratch + [pltpu.VMEM((8 * SLOTS, LANES), f32)],
-        count=5,
+        places="vvvvv",
+        out_places="v",
     )(start, first, left, own_cells, right)
     return (stress.reshape(plastic.shape), moved[:, None])
 

time: 114 us -> 108 us (0.947)
  blocking collectives: 0 us -> 45.9 us
  waiting for transfers between devices: 75.2 us -> 36.4 us
  starting transfers between devices: 15.7 us -> 8.4 us
  local copies, waits for them, and re-layouts: 3.09 us -> 0.16 us
  Pallas kernels: 18.2 us -> 16.4 us
    all_to_all x0 -> x1, blocking collectives: none -> 45.9 us  [slab_body(): waves = lax.all_to_all(waves.reshape(blocks), axes, 0, 0, tiled=True)]
    all_to_all x2 -> x1, waiting for transfers between devices: 65.4 us -> 36 us  [slab_body(): waves = lax.all_to_all(waves.reshape(blocks), axes, 0, 0, tiled=True)]
    ppermute x2, waiting for transfers between devices: 8.26 us -> 0.01 us  [neighbours(): lax.ppermute(low, 'gx', backward)]
    all_to_all x2 -> x1, starting transfers between devices: 10.1 us -> 2.84 us  [slab_body(): waves = lax.all_to_all(waves.reshape(blocks), axes, 0, 0, tiled=True)]
    unnamed x38 -> x22, local copies, waits for them, and re-layouts: 3 us -> 0.07 us
    ppermute x2, waiting for transfers between devices: 1.53 us -> 0.33 us  [neighbours(): lax.ppermute(high, 'gx', forward)]
  transfers between devices with their start and end apart: 6 -> 5, of which waited for: 5 -> 2; matrix products, arithmetic and copies ran while one was open for 0% -> 0% of each run, Pallas kernels for 1% -> 4%
where the time goes in v2:
time: 108 us
  blocking collectives  45.9 us (42%)
  waiting for transfers between devices  36.4 us (34%)
  Pallas kernels  16.4 us (15%)
  starting transfers between devices  8.4 us (8%)
    all_to_all x1, blocking collectives, slab_body(): waves = lax.all_to_all(waves.reshape(blocks), axes, 0, 0, tiled=True)  45.9 us
    all_to_all x1, waiting for transfers between devices, slab_body(): waves = lax.all_to_all(waves.reshape(blocks), axes, 0, 0, tiled=True)  36 us
    pallas_call x1, Pallas kernels, slab_body(): kernel_call(functools.partial(spectral_kernel, gx_count, pa_count, y_loca...  6.89 us
    ppermute x2, starting transfers between devices, neighbours(): lax.ppermute(low, 'gx', backward)  5.53 us
    pallas_call x1, Pallas kernels, slab_body(): kernel_call(functools.partial(inverse_z_kernel, x_local, y_local, cell_co...  3.25 us
    all_to_all x1, starting transfers between devices, slab_body(): waves = lax.all_to_all(waves.reshape(blocks), axes, 0, 0, tiled=True)  2.84 us
    pallas_call x1, Pallas kernels, slab_body(): kernel_call(functools.partial(forward_z_kernel, x_local, y_local), [pltpu...  2.74 us
    pallas_call x1, Pallas kernels, slab_body(): kernel_call(functools.partial(moves_kernel, cell_count), [jax.ShapeDtypeS...  2.34 us
  transfers between devices with their start and end apart: 5, of which 2 were waited for; matrix products, arithmetic and copies ran while one was open for 0% of the time, Pallas kernels for 4%

profile of v2, /device:TPU:0, one launch (start us, length us, event | category | flops | bytes accessed | tf_op | source)
XLA Modules:
  0.0 108.3 jit_solution(8944893458000275109)
XLA Ops:
  0.6 2.7 %shard_map.131 = f32[3072,128]{1,0:T(8,128)S(1)} custom-call(f32[3072,128]{1,0:T(8,128)} %bitcast.17, bf16[2,128,128]{2,1,0:T(8,128)(2,1)} %constant.26.clone.table_ref), custom_call_target="tpu_custom_call" | custom-call | bytes 1048576 | tf_op jit(solution)/shard_map/pallas_call | solution.py:677
  3.4 0.0 copy-start.1
  3.4 0.0 copy-start.2
  3.4 0.0 copy-start.3
  3.4 0.0 copy-start.4
  3.4 45.9 %all_to_all.10 = f32[32,96,128]{2,1,0:T(8,128)S(1)} all-to-all(f32[32,96,128]{2,1,0:T(8,128)S(1)} %bitcast.16), channel_id=1, replica_groups=mesh['gx'=4,'pa'=8] {'gx','pa'}, dimensions={0} | all-to-all | bytes 3145728 | tf_op jit(solution)/shard_map/all_to_all | solution.py:689
  49.4 0.0 copy-done.1
  49.4 0.0 copy-done.2
  49.4 0.0 copy-done.3
  49.4 0.0 copy-done.4
  49.4 6.9 %shard_map.132 = f32[32,2,3,16,128]{4,3,2,1,0:T(8,128)} custom-call(f32[2]{0:T(128)S(1)} %add_convert_fusion.freq_ref, f32[32,2,3,16,128]{4,3,2,1,0:T(8,128)S(1)} %bitcast.15, bf16[2,256,256]{2,1,0:T(8,128)(2,1)S(1)} %copy-done.1, bf16[2,256,256]{2,1,0:T(8,128)(2,1)S(1)} %copy-done.2, bf16[2,256,256]{2,1,0:T(8,128)(2,1)S(1)} %copy-done.3, ...), custom_call_target="tpu_custom_call" | custom-call | bytes 1048576 | tf_op jit(solution)/shard_map/pallas_call | solution.py:690
  56.3 0.0 copy-start.10
  56.3 0.0 copy-start.9
  56.3 0.0 copy-start.7
  56.3 0.0 copy-start.8
  56.3 0.0 copy-start
  56.4 0.0 copy-start.5
  56.4 0.0 copy-start.6
  56.4 2.8 %all-to-all-start.1 = ((f32[32,96,128]{2,1,0:T(8,128)}), f32[32,96,128]{2,1,0:T(8,128)S(1)}, u32[]{:S(2)}, u32[]{:S(2)}) async-start(f32[32,96,128]{2,1,0:T(8,128)} %bitcast.4), calls=%async_computation.1 | async-start | bytes 3145728 | tf_op jit(solution)/shard_map/all_to_all | solution.py:704
  59.2 0.0 copy-done.10
  59.2 0.1 fusion
  59.3 0.0 copy-done.9
  59.3 0.0 copy-done.7
  59.3 0.0 copy-done.8
  59.4 2.6 %collective-permute-start.1 = (f32[9,3,128]{2,1,0:T(4,128)S(1)}, f32[9,3,128]{2,1,0:T(4,128)S(1)}, u32[]{:S(2)}, u32[]{:S(2)}) collective-permute-start(f32[9,3,128]{2,1,0:T(4,128)S(1)} %get-tuple-element.27), channel_id=1, source_target_pairs={{8,0},{16,8},{24,16},{0,24},{9,1},{17,9},{25,17},{1,25},{10,2},{18... | collective-permute-start | bytes 41480 | tf_op jit(solution)/shard_map/ppermute | solution.py:652
  62.0 0.0 collective-permute-start
  62.0 0.1 pad.5.clone
  62.1 36.0 %all-to-all-done.1 = f32[32,96,128]{2,1,0:T(8,128)S(1)} async-done(((f32[32,96,128]{2,1,0:T(8,128)}), f32[32,96,128]{2,1,0:T(8,128)S(1)}, u32[]{:S(2)}, u32[]{:S(2)}) %all-to-all-start.1) | async-done | bytes 1572896 | tf_op jit(solution)/shard_map/all_to_all | solution.py:704
  98.1 0.0 copy-done
  98.1 0.0 copy-done.5
  98.1 0.0 copy-done.6
  98.1 3.2 %shard_map.133 = (f32[3072,128]{1,0:T(8,128)}, f32[4,8,128]{2,1,0:T(8,128)S(1)}, f32[2,8,128]{2,1,0:T(8,128)S(1)}, f32[2,8,128]{2,1,0:T(8,128)S(1)}) custom-call(s32[4,128]{1,0:T(4,128)S(1)} %bitcast.20, f32[3072,128]{1,0:T(8,128)S(1)} %bitcast.19, f32[3072,128]{1,0:T(8,128)S(1)} %bitcast.18, bf16[2,128,128]{2,1,0:T(8,128)(2,1)S(1)} %copy-done.5), custom_call_target="tpu_custom_call" | custom-call | bytes 1048576 | tf_op jit(solution)/shard_map/pallas_call | solution.py:725
  101.3 0.0 collective-permute-start.2
  101.4 2.9 %collective-permute-start.3 = (f32[2,8,128]{2,1,0:T(8,128)S(1)}, f32[2,8,128]{2,1,0:T(8,128)S(1)}, u32[]{:S(2)}, u32[]{:S(2)}) collective-permute-start(f32[2,8,128]{2,1,0:T(8,128)S(1)} %get-tuple-element.23), channel_id=1, source_target_pairs={{8,0},{16,8},{24,16},{0,24},{9,1},{17,9},{25,17},{1,25},{10,2},{18... | collective-permute-start | bytes 24584 | tf_op jit(solution)/shard_map/ppermute | solution.py:652
  104.3 0.0 collective-permute-done.1
  104.3 0.0 collective-permute-done
  104.3 0.1 maximum_maximum_fusion.start_ref
  104.4 1.2 %shard_map.134.first_ref = f32[6,16,128]{2,1,0:T(8,128)S(1)} custom-call(f32[9,16,128]{2,1,0:T(8,128)S(1)} %maximum_maximum_fusion.start_ref), custom_call_target="tpu_custom_call" | custom-call | bytes 1048576 | tf_op jit(solution)/shard_map/pallas_call | solution.py:716
  105.6 0.3 collective-permute-done.2.left_ref
  105.9 0.0 collective-permute-done.3.right_ref
  105.9 2.3 %shard_map.135 = f32[3,4,128]{2,1,0:T(4,128)} custom-call(f32[9,16,128]{2,1,0:T(8,128)S(1)} %maximum_maximum_fusion.start_ref, f32[6,16,128]{2,1,0:T(8,128)S(1)} %shard_map.134.first_ref, f32[2,8,128]{2,1,0:T(8,128)S(1)} %collective-permute-done.2.left_ref, f32[4,8,128]{2,1,0:T(8,128)S(1)} %get-tuple-element.22.own_ref, ...), custom_call_target="tpu_custom_call" | custom-call | bytes 1048576 | tf_op jit(solution)/shard_map/pallas_call | solution.py:737
  (5 shorter events, 0.0 us)
Async XLA Ops:
  3.4 46.0 %copy-start.1 = (bf16[2,256,256]{2,1,0:T(8,128)(2,1)S(1)}, bf16[2,256,256]{2,1,0:T(8,128)(2,1)}, u32[]{:S(2)}) copy-start(bf16[2,256,256]{2,1,0:T(8,128)(2,1)} %constant.27.clone.forward_y_ref) | copy-start | bytes 786436
  3.4 46.0 %copy-start.2 = (bf16[2,256,256]{2,1,0:T(8,128)(2,1)S(1)}, bf16[2,256,256]{2,1,0:T(8,128)(2,1)}, u32[]{:S(2)}) copy-start(bf16[2,256,256]{2,1,0:T(8,128)(2,1)} %constant.28.clone.forward_x_ref) | copy-start | bytes 786436
  3.4 46.0 %copy-start.3 = (bf16[2,256,256]{2,1,0:T(8,128)(2,1)S(1)}, bf16[2,256,256]{2,1,0:T(8,128)(2,1)}, u32[]{:S(2)}) copy-start(bf16[2,256,256]{2,1,0:T(8,128)(2,1)} %constant.29.clone.inverse_x_ref) | copy-start | bytes 786436
  3.4 46.0 %copy-start.4 = (bf16[2,256,256]{2,1,0:T(8,128)(2,1)S(1)}, bf16[2,256,256]{2,1,0:T(8,128)(2,1)}, u32[]{:S(2)}) copy-start(bf16[2,256,256]{2,1,0:T(8,128)(2,1)} %constant.30.clone.inverse_y_ref) | copy-start | bytes 786436
  56.3 2.9 %copy-start.10 = (s32[1,4]{1,0:T(1,128)S(1)}, s32[1,4]{1,0:T(1,128)}, u32[]{:S(2)}) copy-start(s32[1,4]{1,0:T(1,128)} %param.16) | copy-start | bytes 52
  56.3 3.0 %copy-start.9 = (f32[3,1,4,128]{3,2,1,0:T(4,128)S(1)}, f32[3,1,4,128]{3,2,1,0:T(4,128)}, u32[]{:S(2)}) copy-start(f32[3,1,4,128]{3,2,1,0:T(4,128)} %param.15) | copy-start | bytes 18436
  56.3 3.0 %copy-start.7 = (f32[3,1,4,128]{3,2,1,0:T(4,128)S(1)}, f32[3,1,4,128]{3,2,1,0:T(4,128)}, u32[]{:S(2)}) copy-start(f32[3,1,4,128]{3,2,1,0:T(4,128)} %param.14) | copy-start | bytes 18436
  56.3 3.0 %copy-start.8 = (f32[3,1,4,128]{3,2,1,0:T(4,128)S(1)}, f32[3,1,4,128]{3,2,1,0:T(4,128)}, u32[]{:S(2)}) copy-start(f32[3,1,4,128]{3,2,1,0:T(4,128)} %param.13) | copy-start | bytes 18436
  56.3 41.8 %copy-start = (f32[6,32,16,128]{3,2,1,0:T(8,128)S(1)}, f32[6,32,16,128]{3,2,1,0:T(8,128)}, u32[]{:S(2)}) copy-start(f32[6,32,16,128]{3,2,1,0:T(8,128)} %param.12) | copy-start | bytes 4718596
  56.4 41.7 %copy-start.5 = (bf16[2,128,128]{2,1,0:T(8,128)(2,1)S(1)}, bf16[2,128,128]{2,1,0:T(8,128)(2,1)}, u32[]{:S(2)}) copy-start(bf16[2,128,128]{2,1,0:T(8,128)(2,1)} %constant.31.clone.table_ref) | copy-start | bytes 196612
  56.4 41.7 %copy-start.6 = (s32[1,4,128]{2,1,0:T(4,128)S(1)}, s32[1,4,128]{2,1,0:T(4,128)}, u32[]{:S(2)}) copy-start(s32[1,4,128]{2,1,0:T(4,128)} %param.17) | copy-start | bytes 6148
  56.4 41.7 %all-to-all-start.1 = ((f32[32,96,128]{2,1,0:T(8,128)}), f32[32,96,128]{2,1,0:T(8,128)S(1)}, u32[]{:S(2)}, u32[]{:S(2)}) async-start(f32[32,96,128]{2,1,0:T(8,128)} %bitcast.4), calls=%async_computation.1 | async-start | bytes 3145728 | tf_op jit(solution)/shard_map/all_to_all | solution.py:704
  59.4 44.9 %collective-permute-start.1 = (f32[9,3,128]{2,1,0:T(4,128)S(1)}, f32[9,3,128]{2,1,0:T(4,128)S(1)}, u32[]{:S(2)}, u32[]{:S(2)}) collective-permute-start(f32[9,3,128]{2,1,0:T(4,128)S(1)} %get-tuple-element.27), channel_id=1, source_target_pairs={{8,0},{16,8},{24,16},{0,24},{9,1},{17,9},{25,17},{1,25},{10,2},{18... | collective-permute-start | bytes 41480 | tf_op jit(solution)/shard_map/ppermute | solution.py:652
  62.0 42.3 %collective-permute-start = (f32[9,3,128]{2,1,0:T(4,128)S(1)}, f32[9,3,128]{2,1,0:T(4,128)S(1)}, u32[]{:S(2)}, u32[]{:S(2)}) collective-permute-start(f32[9,3,128]{2,1,0:T(4,128)S(1)} %get-tuple-element.26), channel_id=1, source_target_pairs={{0,8},{8,16},{16,24},{24,0},{1,9},{9,17},{17,25},{25,1},{2,10},{10... | collective-permute-start | bytes 41480 | tf_op jit(solution)/shard_map/ppermute | solution.py:652
  101.3 4.6 %collective-permute-start.2 = (f32[2,8,128]{2,1,0:T(8,128)S(1)}, f32[2,8,128]{2,1,0:T(8,128)S(1)}, u32[]{:S(2)}, u32[]{:S(2)}) collective-permute-start(f32[2,8,128]{2,1,0:T(8,128)S(1)} %get-tuple-element.21), channel_id=1, source_target_pairs={{0,8},{8,16},{16,24},{24,0},{1,9},{9,17},{17,25},{25,1},{2,10},{10... | collective-permute-start | bytes 24584 | tf_op jit(solution)/shard_map/ppermute | solution.py:652
  101.4 4.5 %collective-permute-start.3 = (f32[2,8,128]{2,1,0:T(8,128)S(1)}, f32[2,8,128]{2,1,0:T(8,128)S(1)}, u32[]{:S(2)}, u32[]{:S(2)}) collective-permute-start(f32[2,8,128]{2,1,0:T(8,128)S(1)} %get-tuple-element.23), channel_id=1, source_target_pairs={{8,0},{16,8},{24,16},{0,24},{9,1},{17,9},{25,17},{1,25},{10,2},{18... | collective-permute-start | bytes 24584 | tf_op jit(solution)/shard_map/ppermute | solution.py:652

commit v3 on v2

--- a/solution.py
+++ b/solution.py
@@ -264,12 +264,12 @@
     ahead = np.array([[cos, sin], [-sin, cos]]).transpose(0, 2, 1, 3)
     back = np.array([[cos, -sin], [sin, cos]]).transpose(0, 2, 1, 3) / grid_len
     size = 2 * grid_len
-    forward_y = ahead.reshape(2, grid_len, 2, pa_count, y_local).transpose(0, 1, 3, 2, 4)
+    forward_y = ahead.reshape(2, grid_len, 2, pa_count, y_local).transpose(3, 2, 4, 0, 1)
     forward_y = forward_y.reshape(size, size)
-    forward_x = ahead.reshape(size, size).T
-    inverse_x = back.reshape(size, size).T
-    inverse_y = back.reshape(2, pa_count, y_local, 2, grid_len).transpose(1, 0, 2, 3, 4)
+    inverse_y = back.reshape(2, pa_count, y_local, 2, grid_len).transpose(3, 4, 1, 0, 2)
     inverse_y = inverse_y.reshape(size, size)
+    forward_x = ahead.reshape(size, size)
+    inverse_x = back.reshape(size, size)
     return [split_table(t) for t in (forward_z, forward_y, forward_x, inverse_x, inverse_y, inverse_z)]
 
 
@@ -324,22 +324,6 @@
                 out_ref[pl.ds(begin + 1, half, stride=stride), :] = odd
 
 
-def swap_blocks(tiles):
-    lane = lane_iota(tiles[0].shape[0])
-    lower = lane < LANES // 2
-    even = (lane // (LANES // 4)) % 2 == 0
-    tiles = list(tiles)
-    for a, b in ((0, 2), (1, 3)):
-        first, second = tiles[a], tiles[b]
-        tiles[a] = jnp.where(lower, first, pltpu.roll(second, LANES // 2, 1))
-        tiles[b] = jnp.where(lower, pltpu.roll(first, LANES // 2, 1), second)
-    for a, b in ((0, 1), (2, 3)):
-        first, second = tiles[a], tiles[b]
-        tiles[a] = jnp.where(even, first, pltpu.roll(second, LANES // 4, 1))
-        tiles[b] = jnp.where(even, pltpu.roll(first, 3 * LANES // 4, 1), second)
-    return tiles
-
-
 def spectral_kernel(
     gx_count,
     pa_count,
@@ -362,38 +346,43 @@
     forward_x = (forward_x_ref[0], forward_x_ref[1])
     inverse_x = (inverse_x_ref[0], inverse_x_ref[1])
     inverse_y = (inverse_y_ref[0], inverse_y_ref[1])
+    x_local = grid_len // gx_count
     for tile in range(tile_count):
         fields = [
-            data_ref[pl.ds(g * pa_count, pa_count), :, tile, :, :].reshape(size, LANES)
+            data_ref[pl.ds(g * pa_count, pa_count), :, tile, :, :].reshape(size, LANES).T
             for g in range(gx_count)
         ]
-        wide = product(forward_y, split(jnp.concatenate(fields, axis=1)))
-        blocks = [wide[:, g * LANES : (g + 1) * LANES] for g in range(gx_count)]
-        for slot, block in enumerate(swap_blocks(blocks)):
-            rows = jnp.concatenate([block[:grid_len], block[grid_len:]], axis=1)
-            waves[tile, slot] = product(split(rows), forward_x)
+        lines = product(split(jnp.concatenate(fields, axis=0)), forward_y)
+        planes = []
+        for slot in range(4):
+            rows = [
+                lines[g * LANES + slot * x_local :][:x_local] for g in range(gx_count)
+            ]
+            plane = jnp.concatenate(rows, axis=0)
+            planes.append(jnp.concatenate([plane[:, :LANES], plane[:, LANES:]], axis=0))
+        waves[tile] = product(forward_x, split(jnp.concatenate(planes, axis=1)))
 
     def signed(index):
         plain = jnp.where(index < grid_len // 2, index, index - grid_len)
         return jnp.where(index == grid_len // 2, 0, plain).astype(jnp.float32)
 
     step = 16
-    freq_x = signed(lax.broadcasted_iota(jnp.int32, (step, LANES), 1))
+    freq_y = signed(lax.broadcasted_iota(jnp.int32, (step, LANES), 1))
     row_index = lax.broadcasted_iota(jnp.int32, (step, LANES), 0)
 
     def operate(chunk, carry):
         start = pl.multiple_of(chunk * step, step)
-        freq_y = signed(row_index + start)
+        freq_x = signed(row_index + start)
         for j in range(2):
             freq_z = freq_ref[j]
             square = freq_x * freq_x + freq_y * freq_y + freq_z * freq_z
             inverse = 1.0 / jnp.maximum(square, 1.0)
             scaled = inverse * inverse * green_coef
             for part in range(2):
-                lanes = pl.ds(part * LANES, LANES)
+                rows = pl.ds(part * grid_len + start, step)
 
                 def at(comp):
-                    return (comp // 2, 2 * j + comp % 2, pl.ds(start, step), lanes)
+                    return (comp // 2, rows, pl.ds((2 * j + comp % 2) * LANES, LANES))
 
                 e_xx, e_yy, e_zz, e_yz, e_xz, e_xy = [waves[at(c)] for c in range(COMPS)]
                 trace = (0.5 * lame_lambda) * (e_xx + e_yy + e_zz)
@@ -416,14 +405,18 @@
 
     stores = []
     for tile in range(tile_count):
-        blocks = []
-        for slot in range(4):
-            rows = product(split(waves[tile, slot]), inverse_x)
-            blocks.append(jnp.concatenate([rows[:, :LANES], rows[:, LANES:]], axis=0))
-        wide = jnp.concatenate(swap_blocks(blocks), axis=1)
-        wide = product(inverse_y, split(wide))
+        planes = product(inverse_x, split(waves[tile]))
+        rows = []
         for g in range(gx_count):
-            blocks_ref[tile, pl.ds(g * size, size), :] = wide[:, g * LANES : (g + 1) * LANES]
+            for slot in range(4):
+                lanes = slice(slot * LANES, (slot + 1) * LANES)
+                parts = [
+                    planes[part * grid_len + g * x_local :][:x_local, lanes] for part in range(2)
+                ]
+                rows.append(jnp.concatenate(parts, axis=1))
+        lines = product(split(jnp.concatenate(rows, axis=0)), inverse_y)
+        for g in range(gx_count):
+            blocks_ref[tile, pl.ds(g * size, size), :] = lines[g * LANES : (g + 1) * LANES].T
         done = blocks_ref.at[tile].reshape(gx_count * pa_count, 2, y_local, LANES)
         stores.append(pltpu.make_async_copy(done, out_ref.at[:, :, tile], sems.at[tile]))
         stores[-1].start()
@@ -478,26 +471,35 @@
                 ] = value
 
     cell_rows = per_comp // cell_count
-    lane = lane_iota(LANES)
-    row_lane = lax.broadcasted_iota(jnp.int32, (LANES, cell_rows), 1)
+    place = lax.broadcasted_iota(jnp.int32, (LANES, LANES), 0)
+    row = lax.broadcasted_iota(jnp.int32, (cell_rows, LANES), 0)
+    unused = jnp.zeros((8 - COMPS, LANES), jnp.float32)
     for cell in range(cell_count):
-        places = jnp.broadcast_to(voxel_ref[pl.ds(cell, 1), :], (LANES, LANES)).astype(jnp.float32)
-        places = places.T.astype(jnp.int32)
-        picked_row = lax.div(places, LANES)
-        picked_lane = places - picked_row * LANES
-        picked_row = picked_row[:, :1] - cell * cell_rows
-        choose = (row_lane == picked_row).astype(jnp.bfloat16)
-        keep = lane == picked_lane
-        found = jnp.zeros((LANES, LANES), jnp.float32)
-        for comp in range(COMPS):
-            block = stress_ref[pl.ds(comp * per_comp + cell * cell_rows, cell_rows), :]
-            high, low = split(block)
-            rows = jnp.dot(choose, high, preferred_element_type=jnp.float32) + jnp.dot(
-                choose, low, preferred_element_type=jnp.float32
+        voxel = voxel_ref[pl.ds(cell, 1), :]
+        picked_row = lax.shift_right_logical(voxel, LANES.bit_length() - 1)
+        picked_place = lax.bitwise_and(voxel, LANES - 1)
+        choose = (place == picked_place).astype(jnp.bfloat16)
+        keep = row == picked_row - cell * cell_rows
+        blocks = [
+            jnp.concatenate(
+                split(stress_ref[pl.ds(comp * per_comp + cell * cell_rows, cell_rows), :]), axis=1
             )
-            value = jnp.sum(jnp.where(keep, rows, 0.0), axis=1, keepdims=True)
-            found = jnp.where(lane == comp, value, found)
-        found = found.T[:8]
+            for comp in range(COMPS)
+        ]
+        picked = jnp.dot(
+            jnp.concatenate(blocks, axis=0),
+            jnp.concatenate([choose, choose], axis=0),
+            preferred_element_type=jnp.float32,
+        )
+        found = [
+            jnp.sum(
+                jnp.where(keep, picked[comp * cell_rows : (comp + 1) * cell_rows], 0.0),
+                axis=0,
+                keepdims=True,
+            )
+            for comp in range(COMPS)
+        ]
+        found = jnp.concatenate(found + [unused], axis=0)
         own_ref[cell] = found
         if cell < 2:
             low_cells_ref[cell] = found
@@ -691,7 +693,7 @@
         functools.partial(spectral_kernel, gx_count, pa_count, y_local),
         [jax.ShapeDtypeStruct(parts, f32)],
         [
-            pltpu.VMEM((tiles, 4, grid_len, 2 * grid_len), f32),
+            pltpu.VMEM((tiles, 2 * grid_len, 4 * LANES), f32),
             pltpu.VMEM((tiles, rows // tiles, LANES), f32),
             tile_sems,
         ],
@@ -721,11 +723,12 @@
         out_places="v",
     )(start)
 
+    waves, first = lax.optimization_barrier((waves, first))
     end = jax.ShapeDtypeStruct((2, 8, cap), f32)
     stress, own_cells, low_cells, high_cells = kernel_call(
         functools.partial(inverse_z_kernel, x_local, y_local, cell_count),
         [
-            jax.ShapeDtypeStruct(flat_plastic.shape, f32),
+            pltpu.VMEM(flat_plastic.shape, f32),
             jax.ShapeDtypeStruct((cell_count, 8, cap), f32),
             end,
             end,

time: 108 us -> 107 us (level)
  Pallas kernels: 16.4 us -> 14.5 us
  waiting for transfers between devices: 36.4 us -> 34.9 us
  local copies, waits for them, and re-layouts: 0.16 us -> 1.3 us
    all_to_all x1, waiting for transfers between devices: 36 us -> 25.3 us  [slab_body(): waves = lax.all_to_all(waves.reshape(blocks), axes, 0, 0, tiled=True)]
    ppermute x2, waiting for transfers between devices: 0.33 us -> 9.51 us  [neighbours(): lax.ppermute(high, 'gx', forward)]
    ppermute x2, starting transfers between devices: 0.03 us -> 1.75 us  [neighbours(): lax.ppermute(high, 'gx', forward)]
    ppermute x2, starting transfers between devices: 5.53 us -> 4.2 us  [neighbours(): lax.ppermute(low, 'gx', backward)]
    pallas_call x1, Pallas kernels: 6.89 us -> 5.62 us  [slab_body(): kernel_call(functools.partial(spectral_kernel, gx_count, pa_count, y_loca...]
    unnamed x22 -> x23, local copies, waits for them, and re-layouts: 0.07 us -> 1.21 us
  transfers between devices with their start and end apart: 5 -> 5, of which waited for: 2 -> 3; matrix products, arithmetic and copies ran while one was open for 0% -> 1% of each run, Pallas kernels for 4% -> 1%
where the time goes in v3:
time: 107 us; the launch traced here: 106 us
  blocking collectives  45.9 us (43%)
  waiting for transfers between devices  34.9 us (33%)
  Pallas kernels  14.5 us (14%)
  starting transfers between devices  8.78 us (8%)
  local copies, waits for them, and re-layouts  1.3 us (1%)
    all_to_all x1, blocking collectives, slab_body(): waves = lax.all_to_all(waves.reshape(blocks), axes, 0, 0, tiled=True)  45.9 us
    all_to_all x1, waiting for transfers between devices, slab_body(): waves = lax.all_to_all(waves.reshape(blocks), axes, 0, 0, tiled=True)  25.3 us
    ppermute x2, waiting for transfers between devices, neighbours(): lax.ppermute(high, 'gx', forward)  9.51 us
    pallas_call x1, Pallas kernels, slab_body(): kernel_call(functools.partial(spectral_kernel, gx_count, pa_count, y_loca...  5.62 us
    ppermute x2, starting transfers between devices, neighbours(): lax.ppermute(low, 'gx', backward)  4.2 us
    all_to_all x1, starting transfers between devices, slab_body(): waves = lax.all_to_all(waves.reshape(blocks), axes, 0, 0, tiled=True)  2.84 us
    pallas_call x1, Pallas kernels, slab_body(): kernel_call(functools.partial(forward_z_kernel, x_local, y_local), [pltpu...  2.74 us
    pallas_call x1, Pallas kernels, slab_body(): kernel_call(functools.partial(inverse_z_kernel, x_local, y_local, cell_co...  2.61 us
  transfers between devices with their start and end apart: 5, of which 3 were waited for; matrix products, arithmetic and copies ran while one was open for 1% of the time, Pallas kernels for 1%

profile of v3, /device:TPU:0, one launch (start us, length us, event | category | flops | bytes accessed | tf_op | source)
XLA Modules:
  0.0 106.4 jit_solution(5667379696102074412)
XLA Ops:
  0.6 2.7 %shard_map.131 = f32[3072,128]{1,0:T(8,128)S(1)} custom-call(f32[3072,128]{1,0:T(8,128)} %bitcast.18, bf16[2,128,128]{2,1,0:T(8,128)(2,1)} %constant.26.clone.table_ref), custom_call_target="tpu_custom_call" | custom-call | bytes 1048576 | tf_op jit(solution)/shard_map/pallas_call | solution.py:679
  3.4 0.0 copy-start.1
  3.4 0.0 copy-start.2
  3.4 0.0 copy-start.3
  3.4 0.0 copy-start.4
  3.4 45.9 %all_to_all.10 = f32[32,96,128]{2,1,0:T(8,128)S(1)} all-to-all(f32[32,96,128]{2,1,0:T(8,128)S(1)} %bitcast.17), channel_id=1, replica_groups=mesh['gx'=4,'pa'=8] {'gx','pa'}, dimensions={0} | all-to-all | bytes 3145728 | tf_op jit(solution)/shard_map/all_to_all | solution.py:691
  49.4 0.0 copy-done.1
  49.4 0.0 copy-done.2
  49.4 0.0 copy-done.3
  49.4 0.0 copy-done.4
  49.4 5.6 %shard_map.132 = f32[32,2,3,16,128]{4,3,2,1,0:T(8,128)} custom-call(f32[2]{0:T(128)S(1)} %add_convert_fusion.freq_ref, f32[32,2,3,16,128]{4,3,2,1,0:T(8,128)S(1)} %bitcast.16, bf16[2,256,256]{2,1,0:T(8,128)(2,1)S(1)} %copy-done.4, bf16[2,256,256]{2,1,0:T(8,128)(2,1)S(1)} %copy-done.3, bf16[2,256,256]{2,1,0:T(8,128)(2,1)S(1)} %copy-done.2, ...), custom_call_target="tpu_custom_call" | custom-call | bytes 1048576 | tf_op jit(solution)/shard_map/pallas_call | solution.py:692
  55.0 0.0 copy-start.10
  55.0 0.0 copy-start.9
  55.0 0.0 copy-start.7
  55.1 0.0 copy-start.8
  55.1 0.0 copy-start
  55.1 0.0 copy-start.5
  55.1 0.0 copy-start.6
  55.1 2.8 %all-to-all-start.1 = ((f32[32,96,128]{2,1,0:T(8,128)}), f32[32,96,128]{2,1,0:T(8,128)S(1)}, u32[]{:S(2)}, u32[]{:S(2)}) async-start(f32[32,96,128]{2,1,0:T(8,128)} %bitcast.4), calls=%async_computation.1 | async-start | bytes 3145728 | tf_op jit(solution)/shard_map/all_to_all | solution.py:706
  58.0 0.0 copy-done.10
  58.0 0.1 fusion
  58.0 0.0 copy-done.9
  58.0 0.0 copy-done.7
  58.0 0.0 copy-done.8
  58.1 1.7 %collective-permute-start = (f32[9,3,128]{2,1,0:T(4,128)S(1)}, f32[9,3,128]{2,1,0:T(4,128)S(1)}, u32[]{:S(2)}, u32[]{:S(2)}) collective-permute-start(f32[9,3,128]{2,1,0:T(4,128)S(1)} %get-tuple-element.30), channel_id=1, source_target_pairs={{0,8},{8,16},{16,24},{24,0},{1,9},{9,17},{17,25},{25,1},{2,10},{10... | collective-permute-start | bytes 41480 | tf_op jit(solution)/shard_map/ppermute | solution.py:654
  59.8 1.3 %collective-permute-start.1 = (f32[9,3,128]{2,1,0:T(4,128)S(1)}, f32[9,3,128]{2,1,0:T(4,128)S(1)}, u32[]{:S(2)}, u32[]{:S(2)}) collective-permute-start(f32[9,3,128]{2,1,0:T(4,128)S(1)} %get-tuple-element.31), channel_id=1, source_target_pairs={{8,0},{16,8},{24,16},{0,24},{9,1},{17,9},{25,17},{1,25},{10,2},{18... | collective-permute-start | bytes 41480 | tf_op jit(solution)/shard_map/ppermute | solution.py:654
  61.1 0.1 pad.5.clone
  61.1 9.0 %collective-permute-done = f32[9,3,128]{2,1,0:T(4,128)S(1)} collective-permute-done((f32[9,3,128]{2,1,0:T(4,128)S(1)}, f32[9,3,128]{2,1,0:T(4,128)S(1)}, u32[]{:S(2)}, u32[]{:S(2)}) %collective-permute-start) | collective-permute-done | bytes 13856 | tf_op jit(solution)/shard_map/ppermute | solution.py:654
  70.2 0.0 collective-permute-done.1
  70.2 0.1 maximum_maximum_fusion.start_ref
  70.3 1.2 %shard_map.133.first_ref = f32[6,16,128]{2,1,0:T(8,128)S(1)} custom-call(f32[9,16,128]{2,1,0:T(8,128)S(1)} %maximum_maximum_fusion.start_ref), custom_call_target="tpu_custom_call" | custom-call | bytes 1048576 | tf_op jit(solution)/shard_map/pallas_call | solution.py:718
  71.5 25.3 %all-to-all-done.1 = f32[32,96,128]{2,1,0:T(8,128)S(1)} async-done(((f32[32,96,128]{2,1,0:T(8,128)}), f32[32,96,128]{2,1,0:T(8,128)S(1)}, u32[]{:S(2)}, u32[]{:S(2)}) %all-to-all-start.1) | async-done | bytes 1572896 | tf_op jit(solution)/shard_map/all_to_all | solution.py:706
  96.8 0.0 copy-done
  96.8 0.0 copy-done.5
  96.8 0.0 copy-done.6
  96.8 2.6 %shard_map.134 = (f32[3072,128]{1,0:T(8,128)S(1)}, f32[4,8,128]{2,1,0:T(8,128)S(1)}, f32[2,8,128]{2,1,0:T(8,128)S(1)}, f32[2,8,128]{2,1,0:T(8,128)S(1)}) custom-call(s32[4,128]{1,0:T(4,128)S(1)} %bitcast.21, f32[3072,128]{1,0:T(8,128)S(1)} %bitcast.20, f32[3072,128]{1,0:T(8,128)S(1)} %bitcast.19, bf16[2,128,128]{2,1,0:T(8,128)(2,1)S(1)} %copy-done.5), custom_call_target="tpu_custom_call" | custom-call | bytes 1048576 | tf_op jit(solution)/shard_map/pallas_call | solution.py:728
  99.4 0.1 collective-permute-start.2
  99.5 2.9 %collective-permute-start.3 = (f32[2,8,128]{2,1,0:T(8,128)S(1)}, f32[2,8,128]{2,1,0:T(8,128)S(1)}, u32[]{:S(2)}, u32[]{:S(2)}) collective-permute-start(f32[2,8,128]{2,1,0:T(8,128)S(1)} %get-tuple-element.27), channel_id=1, source_target_pairs={{8,0},{16,8},{24,16},{0,24},{9,1},{17,9},{25,17},{1,25},{10,2},{18... | collective-permute-start | bytes 24584 | tf_op jit(solution)/shard_map/ppermute | solution.py:654
  102.4 1.1 %copy.15 = f32[6,32,16,128]{3,2,1,0:T(8,128)} copy(f32[6,32,16,128]{3,2,1,0:T(8,128)S(1)} %bitcast.15) | data formatting | bytes 3145728
  103.6 0.5 collective-permute-done.2.left_ref
  104.0 0.0 collective-permute-done.3.right_ref
  104.0 2.3 %shard_map.135 = f32[3,4,128]{2,1,0:T(4,128)} custom-call(f32[9,16,128]{2,1,0:T(8,128)S(1)} %maximum_maximum_fusion.start_ref, f32[6,16,128]{2,1,0:T(8,128)S(1)} %shard_map.133.first_ref, f32[2,8,128]{2,1,0:T(8,128)S(1)} %collective-permute-done.2.left_ref, f32[4,8,128]{2,1,0:T(8,128)S(1)} %get-tuple-element.26.own_ref, ...), custom_call_target="tpu_custom_call" | custom-call | bytes 1048576 | tf_op jit(solution)/shard_map/pallas_call | solution.py:740
  (5 shorter events, 0.0 us)
Async XLA Ops:
  3.4 46.0 %copy-start.1 = (bf16[2,256,256]{2,1,0:T(8,128)(2,1)S(1)}, bf16[2,256,256]{2,1,0:T(8,128)(2,1)}, u32[]{:S(2)}) copy-start(bf16[2,256,256]{2,1,0:T(8,128)(2,1)} %constant.30.clone.inverse_y_ref) | copy-start | bytes 786436
  3.4 46.0 %copy-start.2 = (bf16[2,256,256]{2,1,0:T(8,128)(2,1)S(1)}, bf16[2,256,256]{2,1,0:T(8,128)(2,1)}, u32[]{:S(2)}) copy-start(bf16[2,256,256]{2,1,0:T(8,128)(2,1)} %constant.29.clone.inverse_x_ref) | copy-start | bytes 786436
  3.4 46.0 %copy-start.3 = (bf16[2,256,256]{2,1,0:T(8,128)(2,1)S(1)}, bf16[2,256,256]{2,1,0:T(8,128)(2,1)}, u32[]{:S(2)}) copy-start(bf16[2,256,256]{2,1,0:T(8,128)(2,1)} %constant.28.clone.forward_x_ref) | copy-start | bytes 786436
  3.4 46.0 %copy-start.4 = (bf16[2,256,256]{2,1,0:T(8,128)(2,1)S(1)}, bf16[2,256,256]{2,1,0:T(8,128)(2,1)}, u32[]{:S(2)}) copy-start(bf16[2,256,256]{2,1,0:T(8,128)(2,1)} %constant.27.clone.forward_y_ref) | copy-start | bytes 786436
  55.0 2.9 %copy-start.10 = (s32[1,4]{1,0:T(1,128)S(1)}, s32[1,4]{1,0:T(1,128)}, u32[]{:S(2)}) copy-start(s32[1,4]{1,0:T(1,128)} %param.16) | copy-start | bytes 52
  55.0 3.0 %copy-start.9 = (f32[3,1,4,128]{3,2,1,0:T(4,128)S(1)}, f32[3,1,4,128]{3,2,1,0:T(4,128)}, u32[]{:S(2)}) copy-start(f32[3,1,4,128]{3,2,1,0:T(4,128)} %param.15) | copy-start | bytes 18436
  55.0 3.0 %copy-start.7 = (f32[3,1,4,128]{3,2,1,0:T(4,128)S(1)}, f32[3,1,4,128]{3,2,1,0:T(4,128)}, u32[]{:S(2)}) copy-start(f32[3,1,4,128]{3,2,1,0:T(4,128)} %param.14) | copy-start | bytes 18436
  55.1 3.0 %copy-start.8 = (f32[3,1,4,128]{3,2,1,0:T(4,128)S(1)}, f32[3,1,4,128]{3,2,1,0:T(4,128)}, u32[]{:S(2)}) copy-start(f32[3,1,4,128]{3,2,1,0:T(4,128)} %param.13) | copy-start | bytes 18436
  55.1 41.8 %copy-start = (f32[6,32,16,128]{3,2,1,0:T(8,128)S(1)}, f32[6,32,16,128]{3,2,1,0:T(8,128)}, u32[]{:S(2)}) copy-start(f32[6,32,16,128]{3,2,1,0:T(8,128)} %param.12) | copy-start | bytes 4718596
  55.1 41.7 %copy-start.5 = (bf16[2,128,128]{2,1,0:T(8,128)(2,1)S(1)}, bf16[2,128,128]{2,1,0:T(8,128)(2,1)}, u32[]{:S(2)}) copy-start(bf16[2,128,128]{2,1,0:T(8,128)(2,1)} %constant.31.clone.table_ref) | copy-start | bytes 196612
  55.1 41.7 %copy-start.6 = (s32[1,4,128]{2,1,0:T(4,128)S(1)}, s32[1,4,128]{2,1,0:T(4,128)}, u32[]{:S(2)}) copy-start(s32[1,4,128]{2,1,0:T(4,128)} %param.17) | copy-start | bytes 6148
  55.1 41.7 %all-to-all-start.1 = ((f32[32,96,128]{2,1,0:T(8,128)}), f32[32,96,128]{2,1,0:T(8,128)S(1)}, u32[]{:S(2)}, u32[]{:S(2)}) async-start(f32[32,96,128]{2,1,0:T(8,128)} %bitcast.4), calls=%async_computation.1 | async-start | bytes 3145728 | tf_op jit(solution)/shard_map/all_to_all | solution.py:706
  58.1 12.1 %collective-permute-start = (f32[9,3,128]{2,1,0:T(4,128)S(1)}, f32[9,3,128]{2,1,0:T(4,128)S(1)}, u32[]{:S(2)}, u32[]{:S(2)}) collective-permute-start(f32[9,3,128]{2,1,0:T(4,128)S(1)} %get-tuple-element.30), channel_id=1, source_target_pairs={{0,8},{8,16},{16,24},{24,0},{1,9},{9,17},{17,25},{25,1},{2,10},{10... | collective-permute-start | bytes 41480 | tf_op jit(solution)/shard_map/ppermute | solution.py:654
  59.8 10.4 %collective-permute-start.1 = (f32[9,3,128]{2,1,0:T(4,128)S(1)}, f32[9,3,128]{2,1,0:T(4,128)S(1)}, u32[]{:S(2)}, u32[]{:S(2)}) collective-permute-start(f32[9,3,128]{2,1,0:T(4,128)S(1)} %get-tuple-element.31), channel_id=1, source_target_pairs={{8,0},{16,8},{24,16},{0,24},{9,1},{17,9},{25,17},{1,25},{10,2},{18... | collective-permute-start | bytes 41480 | tf_op jit(solution)/shard_map/ppermute | solution.py:654
  99.4 4.6 %collective-permute-start.2 = (f32[2,8,128]{2,1,0:T(8,128)S(1)}, f32[2,8,128]{2,1,0:T(8,128)S(1)}, u32[]{:S(2)}, u32[]{:S(2)}) collective-permute-start(f32[2,8,128]{2,1,0:T(8,128)S(1)} %get-tuple-element.25), channel_id=1, source_target_pairs={{0,8},{8,16},{16,24},{24,0},{1,9},{9,17},{17,25},{25,1},{2,10},{10... | collective-permute-start | bytes 24584 | tf_op jit(solution)/shard_map/ppermute | solution.py:654
  99.5 4.5 %collective-permute-start.3 = (f32[2,8,128]{2,1,0:T(8,128)S(1)}, f32[2,8,128]{2,1,0:T(8,128)S(1)}, u32[]{:S(2)}, u32[]{:S(2)}) collective-permute-start(f32[2,8,128]{2,1,0:T(8,128)S(1)} %get-tuple-element.27), channel_id=1, source_target_pairs={{8,0},{16,8},{24,16},{0,24},{9,1},{17,9},{25,17},{1,25},{10,2},{18... | collective-permute-start | bytes 24584 | tf_op jit(solution)/shard_map/ppermute | solution.py:654

commit v4 on v3

--- a/solution.py
+++ b/solution.py
@@ -401,7 +401,7 @@
                 waves[at(5)] = freq_x * u_y + freq_y * u_x
         return carry
 
-    lax.fori_loop(0, grid_len // step, operate, 0)
+    lax.fori_loop(0, grid_len // step, operate, 0, unroll=True)
 
     stores = []
     for tile in range(tile_count):
@@ -507,8 +507,7 @@
             high_cells_ref[cell - cell_count + 2] = found
 
 
-def pair_moments(state, fixed, scratch, first, last):
-    position = state
+def pair_moments(position, fixed, scratch, pairs, add=()):
     columns, features, moments = scratch
     slots = position[0].shape[0]
     lines, burgers = fixed
@@ -524,15 +523,15 @@
             for a in range(3):
                 features[shift, pl.ds((3 * a + b) * slots, slots), :] = lines[a] * burgers[b]
                 features[shift, pl.ds((9 + 3 * a + b) * slots, slots), :] = shifted[a] * burgers[b]
-    for source in range(first - 1, last + 1):
+    for source in sorted({target + shift - 1 for target in pairs for shift in pairs[target]}):
         for a in range(3):
             row = position[a][source : source + 1]
             columns[source, a] = jnp.broadcast_to(row, (LANES, LANES)).T
-    for target in range(first, last):
+    for target, shifts in pairs.items():
         weights = []
         sources = []
         own = [position[a][target : target + 1] for a in range(3)]
-        for shift in range(3):
+        for shift in shifts:
             source = target + shift - 1
             d_x = (own[0] - (shift - 1.0)) - columns[source, 0]
             d_y = own[1] - columns[source, 1]
@@ -543,7 +542,12 @@
         total = product(
             split(jnp.concatenate(sources, axis=1)), split(jnp.concatenate(weights, axis=0))
         )
-        moments[pl.ds(target * FEATURES, FEATURES), :] = total
+        rows = pl.ds(target * FEATURES, FEATURES)
+        moments[rows, :] = moments[rows, :] + total if target in add else total
+
+
+def every_pair(first, last):
+    return {target: (0, 1, 2) for target in range(first, last)}
 
 
 def pair_field(position, moments):
@@ -575,9 +579,64 @@
 def first_field_kernel(last, start_ref, out_ref, columns, features, moments):
     clear(features, moments)
     position, lines, burgers = load_fixed(start_ref)
-    pair_moments(position, (lines, burgers), (columns, features, moments), 1, last)
+    pair_moments(
+        position, (lines, burgers), (columns, features, moments), every_pair(1, last)
+    )
     for comp, value in enumerate(pair_field(position, moments)):
         out_ref[comp] = value
+
+
+def moved_on(position, lines, burgers, sampled, field):
+    sigma = [sampled[comp] + field[comp] for comp in range(COMPS)]
+    traction = [
+        sigma[full_index[a][0]] * burgers[0]
+        + sigma[full_index[a][1]] * burgers[1]
+        + sigma[full_index[a][2]] * burgers[2]
+        for a in range(3)
+    ]
+    return [
+        position[0] + step_size * (traction[1] * lines[2] - traction[2] * lines[1]),
+        position[1] + step_size * (traction[2] * lines[0] - traction[0] * lines[2]),
+        position[2] + step_size * (traction[0] * lines[1] - traction[1] * lines[0]),
+    ]
+
+
+def spread(sampled_ref, parts):
+    sampled_ref[...] = jnp.zeros_like(sampled_ref)
+    for begin, part in parts:
+        sampled_ref[pl.ds(8 * begin, 8 * part.shape[0]), :] = part[...].reshape(-1, LANES)
+    return [sampled_ref[pl.ds(comp, SLOTS, stride=8), :] for comp in range(COMPS)]
+
+
+def own_moves_kernel(
+    cell_count,
+    start_ref,
+    first_ref,
+    own_ref,
+    stress_ref,
+    stress_out_ref,
+    part_ref,
+    columns,
+    features,
+    moments,
+    sampled_ref,
+    sem,
+):
+    store = pltpu.make_async_copy(stress_ref, stress_out_ref, sem)
+    store.start()
+    clear(features, moments)
+    position, lines, burgers = load_fixed(start_ref)
+    sampled = spread(sampled_ref, [(3, own_ref)])
+    field = [first_ref[comp] for comp in range(COMPS)]
+    position = moved_on(position, lines, burgers, sampled, field)
+    first, last = 3, cell_count + 3
+    pairs = {
+        target: [s for s in range(3) if first <= target + s - 1 < last]
+        for target in range(first, last)
+    }
+    pair_moments(position, (lines, burgers), (columns, features, moments), pairs)
+    part_ref[...] = moments[...]
+    store.wait()
 
 
 def moves_kernel(
@@ -587,21 +646,20 @@
     left_ref,
     own_ref,
     right_ref,
+    part_ref,
     out_ref,
     columns,
     features,
     moments,
     sampled_ref,
 ):
-    clear(features, moments)
+    features[...] = jnp.zeros_like(features)
+    moments[...] = part_ref[...]
     position, lines, burgers = load_fixed(start_ref)
     initial = position
-    sampled_ref[...] = jnp.zeros_like(sampled_ref)
-    sampled_ref[pl.ds(8, 16), :] = left_ref[...].reshape(16, LANES)
-    sampled_ref[pl.ds(24, 8 * cell_count), :] = own_ref[...].reshape(8 * cell_count, LANES)
-    sampled_ref[pl.ds(24 + 8 * cell_count, 16), :] = right_ref[...].reshape(16, LANES)
-    slots = position[0].shape[0]
-    sampled = [sampled_ref[pl.ds(comp, slots, stride=8), :] for comp in range(COMPS)]
+    first, last = 3, cell_count + 3
+    sampled = spread(sampled_ref, [(1, left_ref), (first, own_ref), (last, right_ref)])
+    rest = {first - 1: (0, 1, 2), first: (0,), last - 1: (2,), last: (0, 1, 2)}
     for repeat in range(SUB):
         if repeat == 0:
             field = [first_ref[comp] for comp in range(COMPS)]
@@ -610,24 +668,13 @@
                 position,
                 (lines, burgers),
                 (columns, features, moments),
-                1 + repeat,
-                cell_count + 5 - repeat,
+                rest if repeat == 1 else every_pair(first, last),
+                (first, last - 1) if repeat == 1 else (),
             )
             field = pair_field(position, moments)
-        sigma = [sampled[comp] + field[comp] for comp in range(COMPS)]
-        traction = [
-            sigma[full_index[a][0]] * burgers[0]
-            + sigma[full_index[a][1]] * burgers[1]
-            + sigma[full_index[a][2]] * burgers[2]
-            for a in range(3)
-        ]
-        position = [
-            position[0] + step_size * (traction[1] * lines[2] - traction[2] * lines[1]),
-            position[1] + step_size * (traction[2] * lines[0] - traction[0] * lines[2]),
-            position[2] + step_size * (traction[0] * lines[1] - traction[1] * lines[0]),
-        ]
+        position = moved_on(position, lines, burgers, sampled, field)
     for a in range(3):
-        out_ref[a] = (position[a] - initial[a])[3 : 3 + cell_count]
+        out_ref[a] = (position[a] - initial[a])[first:last]
 
 
 def kernel_call(kernel, outs, scratch=(), flops=0, places="", out_places="", limit=VMEM_LIMIT):
@@ -737,13 +784,24 @@
         out_places="vvvv",
     )(voxels[0], waves.reshape(rows, LANES), flat_plastic, inverse_z)
     left, right = neighbours(low_cells, high_cells)
+    sampled = pltpu.VMEM((8 * SLOTS, LANES), f32)
+    stress, part = kernel_call(
+        functools.partial(own_moves_kernel, cell_count),
+        [
+            jax.ShapeDtypeStruct(stress.shape, f32),
+            jax.ShapeDtypeStruct((SLOTS * FEATURES, cap), f32),
+        ],
+        pair_scratch + [sampled, pltpu.SemaphoreType.DMA],
+        places="vvvv",
+        out_places="hv",
+    )(start, first, own_cells, stress)
     (moved,) = kernel_call(
         functools.partial(moves_kernel, cell_count),
         [jax.ShapeDtypeStruct((3, cell_count, cap), f32)],
-        pair_scratch + [pltpu.VMEM((8 * SLOTS, LANES), f32)],
-        places="vvvvv",
+        pair_scratch + [sampled],
+        places="vvvvvv",
         out_places="v",
-    )(start, first, left, own_cells, right)
+    )(start, first, left, own_cells, right, part)
     return (stress.reshape(plastic.shape), moved[:, None])
 
 

time: 107 us -> 106 us (level)
  local copies, waits for them, and re-layouts: 1.3 us -> 0.16 us
    pallas_call x0 -> x1, Pallas kernels: none -> 1.15 us  [slab_body(): kernel_call(functools.partial(own_moves_kernel, cell_count), [jax.ShapeDt...]
    unnamed x23 -> x22, local copies, waits for them, and re-layouts: 1.21 us -> 0.07 us
  transfers between devices with their start and end apart: 5 -> 5, of which waited for: 3 -> 3; matrix products, arithmetic and copies ran while one was open for 1% -> 0% of each run, Pallas kernels for 1% -> 2%
where the time goes in v4:
time: 106 us; the launch traced here: 105 us
  blocking collectives  45.9 us (43%)
  waiting for transfers between devices  34.9 us (33%)
  Pallas kernels  14.7 us (14%)
  starting transfers between devices  8.78 us (8%)
    all_to_all x1, blocking collectives, slab_body(): waves = lax.all_to_all(waves.reshape(blocks), axes, 0, 0, tiled=True)  45.9 us
    all_to_all x1, waiting for transfers between devices, slab_body(): waves = lax.all_to_all(waves.reshape(blocks), axes, 0, 0, tiled=True)  25.3 us
    ppermute x2, waiting for transfers between devices, neighbours(): lax.ppermute(high, 'gx', forward)  9.5 us
    pallas_call x1, Pallas kernels, slab_body(): kernel_call(functools.partial(spectral_kernel, gx_count, pa_count, y_loca...  5.05 us
    ppermute x2, starting transfers between devices, neighbours(): lax.ppermute(low, 'gx', backward)  4.2 us
    all_to_all x1, starting transfers between devices, slab_body(): waves = lax.all_to_all(waves.reshape(blocks), axes, 0, 0, tiled=True)  2.84 us
    pallas_call x1, Pallas kernels, slab_body(): kernel_call(functools.partial(forward_z_kernel, x_local, y_local), [pltpu...  2.74 us
    pallas_call x1, Pallas kernels, slab_body(): kernel_call(functools.partial(inverse_z_kernel, x_local, y_local, cell_co...  2.61 us
  transfers between devices with their start and end apart: 5, of which 3 were waited for; matrix products, arithmetic and copies ran while one was open for 0% of the time, Pallas kernels for 2%

profile of v4, /device:TPU:0, one launch (start us, length us, event | category | flops | bytes accessed | tf_op | source)
XLA Modules:
  0.0 105.4 jit_solution(18321755421012257649)
XLA Ops:
  0.6 2.7 %shard_map.131 = f32[3072,128]{1,0:T(8,128)S(1)} custom-call(f32[3072,128]{1,0:T(8,128)} %bitcast.17, bf16[2,128,128]{2,1,0:T(8,128)(2,1)} %constant.26.clone.table_ref), custom_call_target="tpu_custom_call" | custom-call | bytes 1048576 | tf_op jit(solution)/shard_map/pallas_call | solution.py:726
  3.4 0.0 copy-start.1
  3.4 0.0 copy-start.2
  3.4 0.0 copy-start.3
  3.4 0.0 copy-start.4
  3.4 45.9 %all_to_all.10 = f32[32,96,128]{2,1,0:T(8,128)S(1)} all-to-all(f32[32,96,128]{2,1,0:T(8,128)S(1)} %bitcast.16), channel_id=1, replica_groups=mesh['gx'=4,'pa'=8] {'gx','pa'}, dimensions={0} | all-to-all | bytes 3145728 | tf_op jit(solution)/shard_map/all_to_all | solution.py:738
  49.4 0.0 copy-done.1
  49.4 0.0 copy-done.2
  49.4 0.0 copy-done.3
  49.4 0.0 copy-done.4
  49.4 5.0 %shard_map.132 = f32[32,2,3,16,128]{4,3,2,1,0:T(8,128)} custom-call(f32[2]{0:T(128)S(1)} %add_convert_fusion.freq_ref, f32[32,2,3,16,128]{4,3,2,1,0:T(8,128)S(1)} %bitcast.15, bf16[2,256,256]{2,1,0:T(8,128)(2,1)S(1)} %copy-done.4, bf16[2,256,256]{2,1,0:T(8,128)(2,1)S(1)} %copy-done.3, bf16[2,256,256]{2,1,0:T(8,128)(2,1)S(1)} %copy-done.2, ...), custom_call_target="tpu_custom_call" | custom-call | bytes 1048576 | tf_op jit(solution)/shard_map/pallas_call | solution.py:739
  54.5 0.0 copy-start.10
  54.5 0.0 copy-start.9
  54.5 0.0 copy-start.7
  54.5 0.0 copy-start.8
  54.5 0.0 copy-start
  54.5 0.0 copy-start.5
  54.5 0.0 copy-start.6
  54.5 2.8 %all-to-all-start.1 = ((f32[32,96,128]{2,1,0:T(8,128)}), f32[32,96,128]{2,1,0:T(8,128)S(1)}, u32[]{:S(2)}, u32[]{:S(2)}) async-start(f32[32,96,128]{2,1,0:T(8,128)} %bitcast.7), calls=%async_computation.1 | async-start | bytes 3145728 | tf_op jit(solution)/shard_map/all_to_all | solution.py:753
  57.4 0.0 copy-done.10
  57.4 0.1 fusion
  57.5 0.0 copy-done.9
  57.5 0.0 copy-done.7
  57.5 0.0 copy-done.8
  57.5 1.7 %collective-permute-start = (f32[9,3,128]{2,1,0:T(4,128)S(1)}, f32[9,3,128]{2,1,0:T(4,128)S(1)}, u32[]{:S(2)}, u32[]{:S(2)}) collective-permute-start(f32[9,3,128]{2,1,0:T(4,128)S(1)} %get-tuple-element.34), channel_id=1, source_target_pairs={{0,8},{8,16},{16,24},{24,0},{1,9},{9,17},{17,25},{25,1},{2,10},{10... | collective-permute-start | bytes 41480 | tf_op jit(solution)/shard_map/ppermute | solution.py:701
  59.2 1.3 %collective-permute-start.1 = (f32[9,3,128]{2,1,0:T(4,128)S(1)}, f32[9,3,128]{2,1,0:T(4,128)S(1)}, u32[]{:S(2)}, u32[]{:S(2)}) collective-permute-start(f32[9,3,128]{2,1,0:T(4,128)S(1)} %get-tuple-element.35), channel_id=1, source_target_pairs={{8,0},{16,8},{24,16},{0,24},{9,1},{17,9},{25,17},{1,25},{10,2},{18... | collective-permute-start | bytes 41480 | tf_op jit(solution)/shard_map/ppermute | solution.py:701
  60.5 0.1 pad.5.clone
  60.6 9.0 %collective-permute-done = f32[9,3,128]{2,1,0:T(4,128)S(1)} collective-permute-done((f32[9,3,128]{2,1,0:T(4,128)S(1)}, f32[9,3,128]{2,1,0:T(4,128)S(1)}, u32[]{:S(2)}, u32[]{:S(2)}) %collective-permute-start) | collective-permute-done | bytes 13856 | tf_op jit(solution)/shard_map/ppermute | solution.py:701
  69.6 0.0 collective-permute-done.1
  69.6 0.1 maximum_maximum_fusion.start_ref
  69.7 1.2 %shard_map.133.first_ref = f32[6,16,128]{2,1,0:T(8,128)S(1)} custom-call(f32[9,16,128]{2,1,0:T(8,128)S(1)} %maximum_maximum_fusion.start_ref), custom_call_target="tpu_custom_call" | custom-call | bytes 1048576 | tf_op jit(solution)/shard_map/pallas_call | solution.py:765
  70.9 25.3 %all-to-all-done.1 = f32[32,96,128]{2,1,0:T(8,128)S(1)} async-done(((f32[32,96,128]{2,1,0:T(8,128)}), f32[32,96,128]{2,1,0:T(8,128)S(1)}, u32[]{:S(2)}, u32[]{:S(2)}) %all-to-all-start.1) | async-done | bytes 1572896 | tf_op jit(solution)/shard_map/all_to_all | solution.py:753
  96.2 0.0 copy-done
  96.2 0.0 copy-done.5
  96.3 0.0 copy-done.6
  96.3 2.6 %shard_map.134 = (f32[3072,128]{1,0:T(8,128)S(1)}, f32[4,8,128]{2,1,0:T(8,128)S(1)}, f32[2,8,128]{2,1,0:T(8,128)S(1)}, f32[2,8,128]{2,1,0:T(8,128)S(1)}) custom-call(s32[4,128]{1,0:T(4,128)S(1)} %bitcast.20, f32[3072,128]{1,0:T(8,128)S(1)} %bitcast.19, f32[3072,128]{1,0:T(8,128)S(1)} %bitcast.18, bf16[2,128,128]{2,1,0:T(8,128)(2,1)S(1)} %copy-done.5), custom_call_target="tpu_custom_call" | custom-call | bytes 1048576 | tf_op jit(solution)/shard_map/pallas_call | solution.py:775
  98.9 0.1 collective-permute-start.2
  98.9 2.9 %collective-permute-start.3 = (f32[2,8,128]{2,1,0:T(8,128)S(1)}, f32[2,8,128]{2,1,0:T(8,128)S(1)}, u32[]{:S(2)}, u32[]{:S(2)}) collective-permute-start(f32[2,8,128]{2,1,0:T(8,128)S(1)} %get-tuple-element.30), channel_id=1, source_target_pairs={{8,0},{16,8},{24,16},{0,24},{9,1},{17,9},{25,17},{1,25},{10,2},{18... | collective-permute-start | bytes 24584 | tf_op jit(solution)/shard_map/ppermute | solution.py:701
  101.8 1.2 %shard_map.135 = (f32[3072,128]{1,0:T(8,128)}, f32[384,128]{1,0:T(8,128)S(1)}) custom-call(f32[9,16,128]{2,1,0:T(8,128)S(1)} %maximum_maximum_fusion.start_ref, f32[6,16,128]{2,1,0:T(8,128)S(1)} %shard_map.133.first_ref, f32[4,8,128]{2,1,0:T(8,128)S(1)} %get-tuple-element.26.own_ref, f32[3072,128]{1,0:T(8,128)S(1)} %get-tuple-element.27.stress_ref), custom_call_target="tpu_custom_call" | custom-call | bytes 1048576 | tf_op jit(solution)/shard_map/pallas_call | solution.py:788
  103.0 0.5 collective-permute-done.2.left_ref
  103.5 0.0 collective-permute-done.3.right_ref
  103.5 1.9 %shard_map.136 = f32[3,4,128]{2,1,0:T(4,128)} custom-call(f32[9,16,128]{2,1,0:T(8,128)S(1)} %maximum_maximum_fusion.start_ref, f32[6,16,128]{2,1,0:T(8,128)S(1)} %shard_map.133.first_ref, f32[2,8,128]{2,1,0:T(8,128)S(1)} %collective-permute-done.2.left_ref, f32[4,8,128]{2,1,0:T(8,128)S(1)} %get-tuple-element.26.own_ref, ...), custom_call_target="tpu_custom_call" | custom-call | bytes 1048576 | tf_op jit(solution)/shard_map/pallas_call | solution.py:798
  (5 shorter events, 0.0 us)
Async XLA Ops:
  3.4 46.0 %copy-start.1 = (bf16[2,256,256]{2,1,0:T(8,128)(2,1)S(1)}, bf16[2,256,256]{2,1,0:T(8,128)(2,1)}, u32[]{:S(2)}) copy-start(bf16[2,256,256]{2,1,0:T(8,128)(2,1)} %constant.30.clone.inverse_y_ref) | copy-start | bytes 786436
  3.4 46.0 %copy-start.2 = (bf16[2,256,256]{2,1,0:T(8,128)(2,1)S(1)}, bf16[2,256,256]{2,1,0:T(8,128)(2,1)}, u32[]{:S(2)}) copy-start(bf16[2,256,256]{2,1,0:T(8,128)(2,1)} %constant.29.clone.inverse_x_ref) | copy-start | bytes 786436
  3.4 46.0 %copy-start.3 = (bf16[2,256,256]{2,1,0:T(8,128)(2,1)S(1)}, bf16[2,256,256]{2,1,0:T(8,128)(2,1)}, u32[]{:S(2)}) copy-start(bf16[2,256,256]{2,1,0:T(8,128)(2,1)} %constant.28.clone.forward_x_ref) | copy-start | bytes 786436
  3.4 46.0 %copy-start.4 = (bf16[2,256,256]{2,1,0:T(8,128)(2,1)S(1)}, bf16[2,256,256]{2,1,0:T(8,128)(2,1)}, u32[]{:S(2)}) copy-start(bf16[2,256,256]{2,1,0:T(8,128)(2,1)} %constant.27.clone.forward_y_ref) | copy-start | bytes 786436
  54.5 2.9 %copy-start.10 = (s32[1,4]{1,0:T(1,128)S(1)}, s32[1,4]{1,0:T(1,128)}, u32[]{:S(2)}) copy-start(s32[1,4]{1,0:T(1,128)} %param.16) | copy-start | bytes 52
  54.5 3.0 %copy-start.9 = (f32[3,1,4,128]{3,2,1,0:T(4,128)S(1)}, f32[3,1,4,128]{3,2,1,0:T(4,128)}, u32[]{:S(2)}) copy-start(f32[3,1,4,128]{3,2,1,0:T(4,128)} %param.15) | copy-start | bytes 18436
  54.5 3.0 %copy-start.7 = (f32[3,1,4,128]{3,2,1,0:T(4,128)S(1)}, f32[3,1,4,128]{3,2,1,0:T(4,128)}, u32[]{:S(2)}) copy-start(f32[3,1,4,128]{3,2,1,0:T(4,128)} %param.14) | copy-start | bytes 18436
  54.5 3.0 %copy-start.8 = (f32[3,1,4,128]{3,2,1,0:T(4,128)S(1)}, f32[3,1,4,128]{3,2,1,0:T(4,128)}, u32[]{:S(2)}) copy-start(f32[3,1,4,128]{3,2,1,0:T(4,128)} %param.13) | copy-start | bytes 18436
  54.5 41.8 %copy-start = (f32[6,32,16,128]{3,2,1,0:T(8,128)S(1)}, f32[6,32,16,128]{3,2,1,0:T(8,128)}, u32[]{:S(2)}) copy-start(f32[6,32,16,128]{3,2,1,0:T(8,128)} %param.12) | copy-start | bytes 4718596
  54.5 41.7 %copy-start.5 = (bf16[2,128,128]{2,1,0:T(8,128)(2,1)S(1)}, bf16[2,128,128]{2,1,0:T(8,128)(2,1)}, u32[]{:S(2)}) copy-start(bf16[2,128,128]{2,1,0:T(8,128)(2,1)} %constant.31.clone.table_ref) | copy-start | bytes 196612
  54.5 41.7 %copy-start.6 = (s32[1,4,128]{2,1,0:T(4,128)S(1)}, s32[1,4,128]{2,1,0:T(4,128)}, u32[]{:S(2)}) copy-start(s32[1,4,128]{2,1,0:T(4,128)} %param.17) | copy-start | bytes 6148
  54.5 41.7 %all-to-all-start.1 = ((f32[32,96,128]{2,1,0:T(8,128)}), f32[32,96,128]{2,1,0:T(8,128)S(1)}, u32[]{:S(2)}, u32[]{:S(2)}) async-start(f32[32,96,128]{2,1,0:T(8,128)} %bitcast.7), calls=%async_computation.1 | async-start | bytes 3145728 | tf_op jit(solution)/shard_map/all_to_all | solution.py:753
  57.5 12.1 %collective-permute-start = (f32[9,3,128]{2,1,0:T(4,128)S(1)}, f32[9,3,128]{2,1,0:T(4,128)S(1)}, u32[]{:S(2)}, u32[]{:S(2)}) collective-permute-start(f32[9,3,128]{2,1,0:T(4,128)S(1)} %get-tuple-element.34), channel_id=1, source_target_pairs={{0,8},{8,16},{16,24},{24,0},{1,9},{9,17},{17,25},{25,1},{2,10},{10... | collective-permute-start | bytes 41480 | tf_op jit(solution)/shard_map/ppermute | solution.py:701
  59.2 10.4 %collective-permute-start.1 = (f32[9,3,128]{2,1,0:T(4,128)S(1)}, f32[9,3,128]{2,1,0:T(4,128)S(1)}, u32[]{:S(2)}, u32[]{:S(2)}) collective-permute-start(f32[9,3,128]{2,1,0:T(4,128)S(1)} %get-tuple-element.35), channel_id=1, source_target_pairs={{8,0},{16,8},{24,16},{0,24},{9,1},{17,9},{25,17},{1,25},{10,2},{18... | collective-permute-start | bytes 41480 | tf_op jit(solution)/shard_map/ppermute | solution.py:701
  98.9 4.6 %collective-permute-start.2 = (f32[2,8,128]{2,1,0:T(8,128)S(1)}, f32[2,8,128]{2,1,0:T(8,128)S(1)}, u32[]{:S(2)}, u32[]{:S(2)}) collective-permute-start(f32[2,8,128]{2,1,0:T(8,128)S(1)} %get-tuple-element.29), channel_id=1, source_target_pairs={{0,8},{8,16},{16,24},{24,0},{1,9},{9,17},{17,25},{25,1},{2,10},{10... | collective-permute-start | bytes 24584 | tf_op jit(solution)/shard_map/ppermute | solution.py:701
  98.9 4.5 %collective-permute-start.3 = (f32[2,8,128]{2,1,0:T(8,128)S(1)}, f32[2,8,128]{2,1,0:T(8,128)S(1)}, u32[]{:S(2)}, u32[]{:S(2)}) collective-permute-start(f32[2,8,128]{2,1,0:T(8,128)S(1)} %get-tuple-element.30), channel_id=1, source_target_pairs={{8,0},{16,8},{24,16},{0,24},{9,1},{17,9},{25,17},{1,25},{10,2},{18... | collective-permute-start | bytes 24584 | tf_op jit(solution)/shard_map/ppermute | solution.py:701

commit v5 on v4

--- a/solution.py
+++ b/solution.py
@@ -349,7 +349,7 @@
     x_local = grid_len // gx_count
     for tile in range(tile_count):
         fields = [
-            data_ref[pl.ds(g * pa_count, pa_count), :, tile, :, :].reshape(size, LANES).T
+            data_ref[:, g, :, :, tile].reshape(size, LANES).T
             for g in range(gx_count)
         ]
         lines = product(split(jnp.concatenate(fields, axis=0)), forward_y)
@@ -416,9 +416,10 @@
                 rows.append(jnp.concatenate(parts, axis=1))
         lines = product(split(jnp.concatenate(rows, axis=0)), inverse_y)
         for g in range(gx_count):
-            blocks_ref[tile, pl.ds(g * size, size), :] = lines[g * LANES : (g + 1) * LANES].T
-        done = blocks_ref.at[tile].reshape(gx_count * pa_count, 2, y_local, LANES)
-        stores.append(pltpu.make_async_copy(done, out_ref.at[:, :, tile], sems.at[tile]))
+            field = lines[g * LANES : (g + 1) * LANES].T
+            blocks_ref[tile, :, g] = field.reshape(pa_count // 2, 2, 2, y_local, LANES)
+        place = out_ref.at[:, :, :, :, tile]
+        stores.append(pltpu.make_async_copy(blocks_ref.at[tile], place, sems.at[tile]))
         stores[-1].start()
     for store in stores:
         store.wait()
@@ -539,9 +540,16 @@
             inverse = lax.rsqrt(d_x * d_x + d_y * d_y + d_z * d_z + core_square)
             weights.append(inverse * inverse * inverse)
             sources.append(features[shift, pl.ds(source, FEATURES, stride=slots), :])
-        total = product(
-            split(jnp.concatenate(sources, axis=1)), split(jnp.concatenate(weights, axis=0))
+        source = jnp.concatenate(sources, axis=1)
+        high, rest = split(source)
+        low = (source - high.astype(jnp.float32) - rest.astype(jnp.float32)).astype(jnp.bfloat16)
+        parts = jnp.concatenate([high, rest, low], axis=0)
+        total = jnp.dot(
+            jnp.concatenate([parts, parts], axis=1),
+            jnp.concatenate(split(jnp.concatenate(weights, axis=0)), axis=0),
+            preferred_element_type=jnp.float32,
         )
+        total = total[:FEATURES] + (total[FEATURES : 2 * FEATURES] + total[2 * FEATURES :])
         rows = pl.ds(target * FEATURES, FEATURES)
         moments[rows, :] = moments[rows, :] + total if target in add else total
 
@@ -711,12 +719,28 @@
     tiles = comp_count // 2
     rows = devices * 2 * tiles * y_local
     blocks = (devices, rows // devices, LANES)
-    parts = (devices, 2, tiles, y_local, LANES)
+    parts = (pa_count // 2, gx_count, 2, 2, tiles, y_local, LANES)
     forward_z, forward_y, forward_x, inverse_x, inverse_y, inverse_z = [
         jnp.asarray(t) for t in tables(grid_len, pa_count, y_local)
     ]
-    axes = ("gx", "pa")
-    own = lax.axis_index(axes)
+    order = [
+        [
+            g * pa_count + 2 * z + core
+            for z in range(pa_count // 2)
+            for g in range(gx_count)
+            for core in range(2)
+        ]
+    ]
+    exchange = functools.partial(
+        lax.all_to_all,
+        axis_name=("gx", "pa"),
+        split_axis=0,
+        concat_axis=0,
+        axis_index_groups=order,
+        tiled=True,
+    )
+    pa_index = lax.axis_index("pa")
+    own = (pa_index // 2 * gx_count + lax.axis_index("gx")) * 2 + pa_index % 2
     bins = (own + devices * jnp.arange(2, dtype=jnp.int32)).astype(f32)
     flat_plastic = plastic.reshape(-1, grid_len)
     tile_sems = pltpu.SemaphoreType.DMA((tiles,))
@@ -735,13 +759,13 @@
         places="hh",
         out_places="v",
     )(in_hbm(flat_plastic), in_hbm(forward_z))
-    waves = lax.all_to_all(waves.reshape(blocks), axes, 0, 0, tiled=True)
+    waves = exchange(waves.reshape(blocks))
     (waves,) = kernel_call(
         functools.partial(spectral_kernel, gx_count, pa_count, y_local),
         [jax.ShapeDtypeStruct(parts, f32)],
         [
             pltpu.VMEM((tiles, 2 * grid_len, 4 * LANES), f32),
-            pltpu.VMEM((tiles, rows // tiles, LANES), f32),
+            pltpu.VMEM((tiles, pa_count // 2, gx_count, 2, 2, y_local, LANES), f32),
             tile_sems,
         ],
         places="svvvvv",
@@ -750,7 +774,7 @@
     waves, offsets, lines, burgers, counts = lax.optimization_barrier(
         (waves, offsets, lines, burgers, counts)
     )
-    waves = lax.all_to_all(waves.reshape(blocks), axes, 0, 0, tiled=True)
+    waves = exchange(waves.reshape(blocks))
 
     live = (jnp.arange(cap, dtype=jnp.int32)[None, :] < counts[0][:, None]).astype(f32)
     start = jnp.concatenate([offsets[:, 0], lines[:, 0], burgers[:, 0] * live[None]], axis=0)
@@ -814,6 +838,7 @@
         plastic.shape == (COMPS, LANES, LANES, LANES)
         and 4 * gx_count * pa_count == grid_len
         and 4 * x_local == LANES
+        and pa_count % 2 == 0
         and y_local % 8 == 0
         and voxels.shape[2] == LANES
         and 3 <= cell_count <= SLOTS - 6

time: 106 us -> 104 us (0.981)
    all_to_all x1, waiting for transfers between devices: 25.3 us -> 23.2 us  [slab_body(): waves = exchange(waves.reshape(blocks))]
    ppermute x2, starting transfers between devices: 1.75 us -> 3.1 us  [neighbours(): lax.ppermute(high, 'gx', forward)]
    ppermute x2, starting transfers between devices: 4.2 us -> 2.86 us  [neighbours(): lax.ppermute(low, 'gx', backward)]
  transfers between devices with their start and end apart: 5 -> 5, of which waited for: 3 -> 4; matrix products, arithmetic and copies ran while one was open for 0% -> 0% of each run, Pallas kernels for 2% -> 2%
where the time goes in v5:
time: 104 us
  blocking collectives  45.1 us (43%)
  waiting for transfers between devices  34 us (33%)
  Pallas kernels  14.8 us (14%)
  starting transfers between devices  9.04 us (9%)
    all_to_all x1, blocking collectives, slab_body(): waves = exchange(waves.reshape(blocks))  45.1 us
    all_to_all x1, waiting for transfers between devices, slab_body(): waves = exchange(waves.reshape(blocks))  23.2 us
    ppermute x2, waiting for transfers between devices, neighbours(): lax.ppermute(high, 'gx', forward)  10.4 us
    pallas_call x1, Pallas kernels, slab_body(): kernel_call(functools.partial(spectral_kernel, gx_count, pa_count, y_loca...  5.05 us
    ppermute x2, starting transfers between devices, neighbours(): lax.ppermute(high, 'gx', forward)  3.1 us
    all_to_all x1, starting transfers between devices, slab_body(): waves = exchange(waves.reshape(blocks))  3.09 us
    ppermute x2, starting transfers between devices, neighbours(): lax.ppermute(low, 'gx', backward)  2.86 us
    pallas_call x1, Pallas kernels, slab_body(): kernel_call(functools.partial(forward_z_kernel, x_local, y_local), [pltpu...  2.73 us
  transfers between devices with their start and end apart: 5, of which 4 were waited for; matrix products, arithmetic and copies ran while one was open for 0% of the time, Pallas kernels for 2%

profile of v5, /device:TPU:0, one launch (start us, length us, event | category | flops | bytes accessed | tf_op | source)
XLA Modules:
  0.0 104.1 jit_solution(2935671044687968897)
XLA Ops:
  0.7 2.7 %shard_map.131 = f32[3072,128]{1,0:T(8,128)S(1)} custom-call(f32[3072,128]{1,0:T(8,128)} %bitcast.17, bf16[2,128,128]{2,1,0:T(8,128)(2,1)} %constant.50.clone.table_ref), custom_call_target="tpu_custom_call" | custom-call | bytes 1048576 | tf_op jit(solution)/shard_map/pallas_call | solution.py:750
  3.4 0.0 copy-start.1
  3.4 0.0 copy-start.2
  3.4 0.0 copy-start.3
  3.4 0.0 copy-start.4
  3.5 45.1 %all_to_all.10 = f32[32,96,128]{2,1,0:T(8,128)S(1)} all-to-all(f32[32,96,128]{2,1,0:T(8,128)S(1)} %bitcast.16), channel_id=1, replica_groups={{0,1,8,9,16,17,24,25,2,3,10,11,18,19,26,27,4,5,12,13,20,21,28,29,6,7,14..., dimensions={0} | all-to-all | bytes 3145728 | tf_op jit(solution)/shard_map/all_to_all | solution.py:762
  48.6 0.0 copy-done.1
  48.6 0.0 copy-done.2
  48.6 0.0 copy-done.3
  48.6 0.0 copy-done.4
  48.6 5.0 %shard_map.132 = f32[4,4,2,2,3,16,128]{6,5,4,3,2,1,0:T(8,128)} custom-call(f32[2]{0:T(128)S(1)} %add_convert_fusion.freq_ref, f32[4,4,2,2,3,16,128]{6,5,4,3,2,1,0:T(8,128)S(1)} %bitcast.15, bf16[2,256,256]{2,1,0:T(8,128)(2,1)S(1)} %copy-done.4, bf16[2,256,256]{2,1,0:T(8,128)(2,1)S(1)} %copy-done.3, bf16[2,256,256]{2,1,0:T(8,128)(2,1)S(1)} %copy-done.2, ...), custom_call_target="tpu_custom_call" | custom-call | bytes 1048576 | tf_op jit(solution)/shard_map/pallas_call | solution.py:763
  53.7 0.0 copy-start.10
  53.7 0.0 copy-start.9
  53.7 0.0 copy-start.7
  53.7 0.0 copy-start.8
  53.7 0.0 copy-start
  53.7 0.0 copy-start.5
  53.7 0.0 copy-start.6
  53.7 3.1 %all-to-all-start.1 = ((f32[32,96,128]{2,1,0:T(8,128)}), f32[32,96,128]{2,1,0:T(8,128)S(1)}, u32[]{:S(2)}, u32[]{:S(2)}) async-start(f32[32,96,128]{2,1,0:T(8,128)} %bitcast.7), calls=%async_computation.1 | async-start | bytes 3145728 | tf_op jit(solution)/shard_map/all_to_all | solution.py:777
  56.8 0.0 copy-done.10
  56.8 0.1 fusion
  56.9 0.0 copy-done.9
  56.9 0.0 copy-done.7
  56.9 0.0 copy-done.8
  57.0 1.8 %collective-permute-start = (f32[9,3,128]{2,1,0:T(4,128)S(1)}, f32[9,3,128]{2,1,0:T(4,128)S(1)}, u32[]{:S(2)}, u32[]{:S(2)}) collective-permute-start(f32[9,3,128]{2,1,0:T(4,128)S(1)} %get-tuple-element.34), channel_id=1, source_target_pairs={{0,8},{8,16},{16,24},{24,0},{1,9},{9,17},{17,25},{25,1},{2,10},{10... | collective-permute-start | bytes 41480 | tf_op jit(solution)/shard_map/ppermute | solution.py:709
  58.8 1.2 %collective-permute-start.1 = (f32[9,3,128]{2,1,0:T(4,128)S(1)}, f32[9,3,128]{2,1,0:T(4,128)S(1)}, u32[]{:S(2)}, u32[]{:S(2)}) collective-permute-start(f32[9,3,128]{2,1,0:T(4,128)S(1)} %get-tuple-element.35), channel_id=1, source_target_pairs={{8,0},{16,8},{24,16},{0,24},{9,1},{17,9},{25,17},{1,25},{10,2},{18... | collective-permute-start | bytes 41480 | tf_op jit(solution)/shard_map/ppermute | solution.py:709
  59.9 0.1 pad.5.clone
  60.0 9.9 %collective-permute-done = f32[9,3,128]{2,1,0:T(4,128)S(1)} collective-permute-done((f32[9,3,128]{2,1,0:T(4,128)S(1)}, f32[9,3,128]{2,1,0:T(4,128)S(1)}, u32[]{:S(2)}, u32[]{:S(2)}) %collective-permute-start) | collective-permute-done | bytes 13856 | tf_op jit(solution)/shard_map/ppermute | solution.py:709
  70.0 0.0 collective-permute-done.1
  70.0 0.1 maximum_maximum_fusion.start_ref
  70.0 1.3 %shard_map.133.first_ref = f32[6,16,128]{2,1,0:T(8,128)S(1)} custom-call(f32[9,16,128]{2,1,0:T(8,128)S(1)} %maximum_maximum_fusion.start_ref), custom_call_target="tpu_custom_call" | custom-call | bytes 1048576 | tf_op jit(solution)/shard_map/pallas_call | solution.py:789
  71.3 23.2 %all-to-all-done.1 = f32[32,96,128]{2,1,0:T(8,128)S(1)} async-done(((f32[32,96,128]{2,1,0:T(8,128)}), f32[32,96,128]{2,1,0:T(8,128)S(1)}, u32[]{:S(2)}, u32[]{:S(2)}) %all-to-all-start.1) | async-done | bytes 1572896 | tf_op jit(solution)/shard_map/all_to_all | solution.py:777
  94.5 0.0 copy-done
  94.5 0.0 copy-done.5
  94.5 0.0 copy-done.6
  94.5 2.6 %shard_map.134 = (f32[3072,128]{1,0:T(8,128)S(1)}, f32[4,8,128]{2,1,0:T(8,128)S(1)}, f32[2,8,128]{2,1,0:T(8,128)S(1)}, f32[2,8,128]{2,1,0:T(8,128)S(1)}) custom-call(s32[4,128]{1,0:T(4,128)S(1)} %bitcast.20, f32[3072,128]{1,0:T(8,128)S(1)} %bitcast.19, f32[3072,128]{1,0:T(8,128)S(1)} %bitcast.18, bf16[2,128,128]{2,1,0:T(8,128)(2,1)S(1)} %copy-done.5), custom_call_target="tpu_custom_call" | custom-call | bytes 1048576 | tf_op jit(solution)/shard_map/pallas_call | solution.py:799
  97.2 1.3 %collective-permute-start.2 = (f32[2,8,128]{2,1,0:T(8,128)S(1)}, f32[2,8,128]{2,1,0:T(8,128)S(1)}, u32[]{:S(2)}, u32[]{:S(2)}) collective-permute-start(f32[2,8,128]{2,1,0:T(8,128)S(1)} %get-tuple-element.29), channel_id=1, source_target_pairs={{0,8},{8,16},{16,24},{24,0},{1,9},{9,17},{17,25},{25,1},{2,10},{10... | collective-permute-start | bytes 24584 | tf_op jit(solution)/shard_map/ppermute | solution.py:709
  98.4 1.7 %collective-permute-start.3 = (f32[2,8,128]{2,1,0:T(8,128)S(1)}, f32[2,8,128]{2,1,0:T(8,128)S(1)}, u32[]{:S(2)}, u32[]{:S(2)}) collective-permute-start(f32[2,8,128]{2,1,0:T(8,128)S(1)} %get-tuple-element.30), channel_id=1, source_target_pairs={{8,0},{16,8},{24,16},{0,24},{9,1},{17,9},{25,17},{1,25},{10,2},{18... | collective-permute-start | bytes 24584 | tf_op jit(solution)/shard_map/ppermute | solution.py:709
  100.1 1.2 %shard_map.135 = (f32[3072,128]{1,0:T(8,128)}, f32[384,128]{1,0:T(8,128)S(1)}) custom-call(f32[9,16,128]{2,1,0:T(8,128)S(1)} %maximum_maximum_fusion.start_ref, f32[6,16,128]{2,1,0:T(8,128)S(1)} %shard_map.133.first_ref, f32[4,8,128]{2,1,0:T(8,128)S(1)} %get-tuple-element.26.own_ref, f32[3072,128]{1,0:T(8,128)S(1)} %get-tuple-element.27.stress_ref), custom_call_target="tpu_custom_call" | custom-call | bytes 1048576 | tf_op jit(solution)/shard_map/pallas_call | solution.py:812
  101.3 0.5 collective-permute-done.2.left_ref
  101.8 0.3 collective-permute-done.3.right_ref
  102.1 2.0 %shard_map.136 = f32[3,4,128]{2,1,0:T(4,128)} custom-call(f32[9,16,128]{2,1,0:T(8,128)S(1)} %maximum_maximum_fusion.start_ref, f32[6,16,128]{2,1,0:T(8,128)S(1)} %shard_map.133.first_ref, f32[2,8,128]{2,1,0:T(8,128)S(1)} %collective-permute-done.2.left_ref, f32[4,8,128]{2,1,0:T(8,128)S(1)} %get-tuple-element.26.own_ref, ...), custom_call_target="tpu_custom_call" | custom-call | bytes 1048576 | tf_op jit(solution)/shard_map/pallas_call | solution.py:822
  (5 shorter events, 0.0 us)
Async XLA Ops:
  3.4 45.2 %copy-start.1 = (bf16[2,256,256]{2,1,0:T(8,128)(2,1)S(1)}, bf16[2,256,256]{2,1,0:T(8,128)(2,1)}, u32[]{:S(2)}) copy-start(bf16[2,256,256]{2,1,0:T(8,128)(2,1)} %constant.54.clone.inverse_y_ref) | copy-start | bytes 786436
  3.4 45.2 %copy-start.2 = (bf16[2,256,256]{2,1,0:T(8,128)(2,1)S(1)}, bf16[2,256,256]{2,1,0:T(8,128)(2,1)}, u32[]{:S(2)}) copy-start(bf16[2,256,256]{2,1,0:T(8,128)(2,1)} %constant.53.clone.inverse_x_ref) | copy-start | bytes 786436
  3.4 45.2 %copy-start.3 = (bf16[2,256,256]{2,1,0:T(8,128)(2,1)S(1)}, bf16[2,256,256]{2,1,0:T(8,128)(2,1)}, u32[]{:S(2)}) copy-start(bf16[2,256,256]{2,1,0:T(8,128)(2,1)} %constant.52.clone.forward_x_ref) | copy-start | bytes 786436
  3.4 45.1 %copy-start.4 = (bf16[2,256,256]{2,1,0:T(8,128)(2,1)S(1)}, bf16[2,256,256]{2,1,0:T(8,128)(2,1)}, u32[]{:S(2)}) copy-start(bf16[2,256,256]{2,1,0:T(8,128)(2,1)} %constant.51.clone.forward_y_ref) | copy-start | bytes 786436
  53.7 3.2 %copy-start.10 = (s32[1,4]{1,0:T(1,128)S(1)}, s32[1,4]{1,0:T(1,128)}, u32[]{:S(2)}) copy-start(s32[1,4]{1,0:T(1,128)} %param.16) | copy-start | bytes 52
  53.7 3.2 %copy-start.9 = (f32[3,1,4,128]{3,2,1,0:T(4,128)S(1)}, f32[3,1,4,128]{3,2,1,0:T(4,128)}, u32[]{:S(2)}) copy-start(f32[3,1,4,128]{3,2,1,0:T(4,128)} %param.15) | copy-start | bytes 18436
  53.7 3.2 %copy-start.7 = (f32[3,1,4,128]{3,2,1,0:T(4,128)S(1)}, f32[3,1,4,128]{3,2,1,0:T(4,128)}, u32[]{:S(2)}) copy-start(f32[3,1,4,128]{3,2,1,0:T(4,128)} %param.14) | copy-start | bytes 18436
  53.7 3.2 %copy-start.8 = (f32[3,1,4,128]{3,2,1,0:T(4,128)S(1)}, f32[3,1,4,128]{3,2,1,0:T(4,128)}, u32[]{:S(2)}) copy-start(f32[3,1,4,128]{3,2,1,0:T(4,128)} %param.13) | copy-start | bytes 18436
  53.7 40.8 %copy-start = (f32[6,32,16,128]{3,2,1,0:T(8,128)S(1)}, f32[6,32,16,128]{3,2,1,0:T(8,128)}, u32[]{:S(2)}) copy-start(f32[6,32,16,128]{3,2,1,0:T(8,128)} %param.12) | copy-start | bytes 4718596
  53.7 40.8 %copy-start.5 = (bf16[2,128,128]{2,1,0:T(8,128)(2,1)S(1)}, bf16[2,128,128]{2,1,0:T(8,128)(2,1)}, u32[]{:S(2)}) copy-start(bf16[2,128,128]{2,1,0:T(8,128)(2,1)} %constant.55.clone.table_ref) | copy-start | bytes 196612
  53.7 40.8 %copy-start.6 = (s32[1,4,128]{2,1,0:T(4,128)S(1)}, s32[1,4,128]{2,1,0:T(4,128)}, u32[]{:S(2)}) copy-start(s32[1,4,128]{2,1,0:T(4,128)} %param.17) | copy-start | bytes 6148
  53.7 40.8 %all-to-all-start.1 = ((f32[32,96,128]{2,1,0:T(8,128)}), f32[32,96,128]{2,1,0:T(8,128)S(1)}, u32[]{:S(2)}, u32[]{:S(2)}) async-start(f32[32,96,128]{2,1,0:T(8,128)} %bitcast.7), calls=%async_computation.1 | async-start | bytes 3145728 | tf_op jit(solution)/shard_map/all_to_all | solution.py:777
  57.0 13.0 %collective-permute-start = (f32[9,3,128]{2,1,0:T(4,128)S(1)}, f32[9,3,128]{2,1,0:T(4,128)S(1)}, u32[]{:S(2)}, u32[]{:S(2)}) collective-permute-start(f32[9,3,128]{2,1,0:T(4,128)S(1)} %get-tuple-element.34), channel_id=1, source_target_pairs={{0,8},{8,16},{16,24},{24,0},{1,9},{9,17},{17,25},{25,1},{2,10},{10... | collective-permute-start | bytes 41480 | tf_op jit(solution)/shard_map/ppermute | solution.py:709
  58.8 11.2 %collective-permute-start.1 = (f32[9,3,128]{2,1,0:T(4,128)S(1)}, f32[9,3,128]{2,1,0:T(4,128)S(1)}, u32[]{:S(2)}, u32[]{:S(2)}) collective-permute-start(f32[9,3,128]{2,1,0:T(4,128)S(1)} %get-tuple-element.35), channel_id=1, source_target_pairs={{8,0},{16,8},{24,16},{0,24},{9,1},{17,9},{25,17},{1,25},{10,2},{18... | collective-permute-start | bytes 41480 | tf_op jit(solution)/shard_map/ppermute | solution.py:709
  97.2 4.6 %collective-permute-start.2 = (f32[2,8,128]{2,1,0:T(8,128)S(1)}, f32[2,8,128]{2,1,0:T(8,128)S(1)}, u32[]{:S(2)}, u32[]{:S(2)}) collective-permute-start(f32[2,8,128]{2,1,0:T(8,128)S(1)} %get-tuple-element.29), channel_id=1, source_target_pairs={{0,8},{8,16},{16,24},{24,0},{1,9},{9,17},{17,25},{25,1},{2,10},{10... | collective-permute-start | bytes 24584 | tf_op jit(solution)/shard_map/ppermute | solution.py:709
  98.4 3.7 %collective-permute-start.3 = (f32[2,8,128]{2,1,0:T(8,128)S(1)}, f32[2,8,128]{2,1,0:T(8,128)S(1)}, u32[]{:S(2)}, u32[]{:S(2)}) collective-permute-start(f32[2,8,128]{2,1,0:T(8,128)S(1)} %get-tuple-element.30), channel_id=1, source_target_pairs={{8,0},{16,8},{24,16},{0,24},{9,1},{17,9},{25,17},{1,25},{10,2},{18... | collective-permute-start | bytes 24584 | tf_op jit(solution)/shard_map/ppermute | solution.py:709

commit v6 on v5

--- a/solution.py
+++ b/solution.py
@@ -347,12 +347,13 @@
     inverse_x = (inverse_x_ref[0], inverse_x_ref[1])
     inverse_y = (inverse_y_ref[0], inverse_y_ref[1])
     x_local = grid_len // gx_count
-    for tile in range(tile_count):
+    def along_y(tile):
         fields = [
-            data_ref[:, g, :, :, tile].reshape(size, LANES).T
-            for g in range(gx_count)
+            data_ref[:, g, :, :, tile].reshape(size, LANES).T for g in range(gx_count)
         ]
-        lines = product(split(jnp.concatenate(fields, axis=0)), forward_y)
+        return product(split(jnp.concatenate(fields, axis=0)), forward_y)
+
+    def along_x(tile, lines):
         planes = []
         for slot in range(4):
             rows = [
@@ -361,6 +362,12 @@
             plane = jnp.concatenate(rows, axis=0)
             planes.append(jnp.concatenate([plane[:, :LANES], plane[:, LANES:]], axis=0))
         waves[tile] = product(forward_x, split(jnp.concatenate(planes, axis=1)))
+
+    lines = along_y(0)
+    for tile in range(tile_count):
+        later = along_y(tile + 1) if tile + 1 < tile_count else None
+        along_x(tile, lines)
+        lines = later
 
     def signed(index):
         plain = jnp.where(index < grid_len // 2, index, index - grid_len)
@@ -425,15 +432,54 @@
         store.wait()
 
 
+def sample(field_ref, voxel_ref, per_comp, cell_count, cell):
+    cell_rows = per_comp // cell_count
+    place = lax.broadcasted_iota(jnp.int32, (LANES, LANES), 0)
+    row = lax.broadcasted_iota(jnp.int32, (cell_rows, LANES), 0)
+    voxel = voxel_ref[pl.ds(cell, 1), :]
+    picked_row = lax.shift_right_logical(voxel, LANES.bit_length() - 1)
+    picked_place = lax.bitwise_and(voxel, LANES - 1)
+    choose = (place == picked_place).astype(jnp.bfloat16)
+    keep = row == picked_row - cell * cell_rows
+    blocks = [
+        jnp.concatenate(
+            split(field_ref[pl.ds(comp * per_comp + cell * cell_rows, cell_rows), :]), axis=1
+        )
+        for comp in range(COMPS)
+    ]
+    picked = jnp.dot(
+        jnp.concatenate(blocks, axis=0),
+        jnp.concatenate([choose, choose], axis=0),
+        preferred_element_type=jnp.float32,
+    )
+    found = [
+        jnp.sum(
+            jnp.where(keep, picked[comp * cell_rows : (comp + 1) * cell_rows], 0.0),
+            axis=0,
+            keepdims=True,
+        )
+        for comp in range(COMPS)
+    ]
+    return jnp.concatenate(found + [jnp.zeros((8 - COMPS, LANES), jnp.float32)], axis=0)
+
+
+def stress_from(elastic):
+    trace = lame_lambda * (elastic[0] + elastic[1] + elastic[2])
+    return [
+        2.0 * shear_modulus * value + (trace if comp < 3 else 0.0)
+        for comp, value in enumerate(elastic)
+    ]
+
+
 def inverse_z_kernel(
     x_local,
     y_local,
     cell_count,
     voxel_ref,
     waves_ref,
-    plastic_ref,
+    local_ref,
     table_ref,
-    stress_ref,
+    strain_ref,
     own_ref,
     low_cells_ref,
     high_cells_ref,
@@ -444,7 +490,6 @@
     stride = (COMPS // 2) * y_local
     first_half = lane_iota(half) < half
     for pair in range(y_local // 2):
-        elastic = [[None] * COMPS for _ in range(2)]
         for tile in range(COMPS // 2):
             base = tile * y_local + 2 * pair
             even = waves_ref[pl.ds(base, half, stride=stride), :]
@@ -456,51 +501,10 @@
             for y in range(2):
                 for c in range(2):
                     begin = (2 * y + c) * x_local
-                    comp = 2 * tile + c
-                    own = plastic_ref[
-                        pl.ds(comp * per_comp + 2 * pair + y, x_local, stride=y_local), :
-                    ]
-                    elastic[y][comp] = lines[begin : begin + x_local] - own
-        for y in range(2):
-            trace = lame_lambda * (elastic[y][0] + elastic[y][1] + elastic[y][2])
-            for comp in range(COMPS):
-                value = 2.0 * shear_modulus * elastic[y][comp]
-                if comp < 3:
-                    value = value + trace
-                stress_ref[
-                    pl.ds(comp * per_comp + 2 * pair + y, x_local, stride=y_local), :
-                ] = value
-
-    cell_rows = per_comp // cell_count
-    place = lax.broadcasted_iota(jnp.int32, (LANES, LANES), 0)
-    row = lax.broadcasted_iota(jnp.int32, (cell_rows, LANES), 0)
-    unused = jnp.zeros((8 - COMPS, LANES), jnp.float32)
+                    place = (2 * tile + c) * per_comp + 2 * pair + y
+                    strain_ref[pl.ds(place, x_local, stride=y_local), :] = lines[begin:][:x_local]
     for cell in range(cell_count):
-        voxel = voxel_ref[pl.ds(cell, 1), :]
-        picked_row = lax.shift_right_logical(voxel, LANES.bit_length() - 1)
-        picked_place = lax.bitwise_and(voxel, LANES - 1)
-        choose = (place == picked_place).astype(jnp.bfloat16)
-        keep = row == picked_row - cell * cell_rows
-        blocks = [
-            jnp.concatenate(
-                split(stress_ref[pl.ds(comp * per_comp + cell * cell_rows, cell_rows), :]), axis=1
-            )
-            for comp in range(COMPS)
-        ]
-        picked = jnp.dot(
-            jnp.concatenate(blocks, axis=0),
-            jnp.concatenate([choose, choose], axis=0),
-            preferred_element_type=jnp.float32,
-        )
-        found = [
-            jnp.sum(
-                jnp.where(keep, picked[comp * cell_rows : (comp + 1) * cell_rows], 0.0),
-                axis=0,
-                keepdims=True,
-            )
-            for comp in range(COMPS)
-        ]
-        found = jnp.concatenate(found + [unused], axis=0)
+        found = sample(strain_ref, voxel_ref, per_comp, cell_count, cell) - local_ref[cell]
         own_ref[cell] = found
         if cell < 2:
             low_cells_ref[cell] = found
@@ -584,11 +588,24 @@
     moments[...] = jnp.zeros_like(moments)
 
 
-def first_field_kernel(last, start_ref, out_ref, columns, features, moments):
+def first_field_kernel(
+    per_comp,
+    cell_count,
+    start_ref,
+    voxel_ref,
+    plastic_ref,
+    out_ref,
+    local_ref,
+    columns,
+    features,
+    moments,
+):
+    for cell in range(cell_count):
+        local_ref[cell] = sample(plastic_ref, voxel_ref, per_comp, cell_count, cell)
     clear(features, moments)
     position, lines, burgers = load_fixed(start_ref)
     pair_moments(
-        position, (lines, burgers), (columns, features, moments), every_pair(1, last)
+        position, (lines, burgers), (columns, features, moments), every_pair(1, cell_count + 5)
     )
     for comp, value in enumerate(pair_field(position, moments)):
         out_ref[comp] = value
@@ -613,7 +630,7 @@
     sampled_ref[...] = jnp.zeros_like(sampled_ref)
     for begin, part in parts:
         sampled_ref[pl.ds(8 * begin, 8 * part.shape[0]), :] = part[...].reshape(-1, LANES)
-    return [sampled_ref[pl.ds(comp, SLOTS, stride=8), :] for comp in range(COMPS)]
+    return stress_from([sampled_ref[pl.ds(comp, SLOTS, stride=8), :] for comp in range(COMPS)])
 
 
 def own_moves_kernel(
@@ -621,17 +638,28 @@
     start_ref,
     first_ref,
     own_ref,
+    strain_ref,
+    plastic_ref,
     stress_ref,
-    stress_out_ref,
     part_ref,
     columns,
     features,
     moments,
     sampled_ref,
-    sem,
+    block,
+    sems,
 ):
-    store = pltpu.make_async_copy(stress_ref, stress_out_ref, sem)
-    store.start()
+    rows = stress_ref.shape[1] // cell_count
+    stores = []
+    for cell in range(cell_count):
+        span = pl.ds(cell * rows, rows)
+        elastic = [strain_ref[c, span, :] - plastic_ref[c, span, :] for c in range(COMPS)]
+        for comp, value in enumerate(stress_from(elastic)):
+            block[comp, span, :] = value
+        stores.append(
+            pltpu.make_async_copy(block.at[:, span], stress_ref.at[:, span], sems.at[cell])
+        )
+        stores[-1].start()
     clear(features, moments)
     position, lines, burgers = load_fixed(start_ref)
     sampled = spread(sampled_ref, [(3, own_ref)])
@@ -644,7 +672,8 @@
     }
     pair_moments(position, (lines, burgers), (columns, features, moments), pairs)
     part_ref[...] = moments[...]
-    store.wait()
+    for store in stores:
+        store.wait()
 
 
 def moves_kernel(
@@ -762,7 +791,7 @@
     waves = exchange(waves.reshape(blocks))
     (waves,) = kernel_call(
         functools.partial(spectral_kernel, gx_count, pa_count, y_local),
-        [jax.ShapeDtypeStruct(parts, f32)],
+        [pltpu.HBM(parts, f32)],
         [
             pltpu.VMEM((tiles, 2 * grid_len, 4 * LANES), f32),
             pltpu.VMEM((tiles, pa_count // 2, gx_count, 2, 2, y_local, LANES), f32),
@@ -786,39 +815,38 @@
         pltpu.VMEM((3, FEATURES * SLOTS, LANES), f32),
         pltpu.VMEM((SLOTS * FEATURES, LANES), f32),
     ]
-    (first,) = kernel_call(
-        functools.partial(first_field_kernel, cell_count + 5),
-        [jax.ShapeDtypeStruct((comp_count, SLOTS, cap), f32)],
+    per_comp = x_local * y_local
+    cells = jax.ShapeDtypeStruct((cell_count, 8, cap), f32)
+    first, local = kernel_call(
+        functools.partial(first_field_kernel, per_comp, cell_count),
+        [jax.ShapeDtypeStruct((comp_count, SLOTS, cap), f32), cells],
         pair_scratch,
-        places="v",
-        out_places="v",
-    )(start)
-
-    waves, first = lax.optimization_barrier((waves, first))
+        places="vvv",
+        out_places="vv",
+    )(start, voxels[0], flat_plastic)
+
+    waves, first, local = lax.optimization_barrier((waves, first, local))
     end = jax.ShapeDtypeStruct((2, 8, cap), f32)
-    stress, own_cells, low_cells, high_cells = kernel_call(
+    strain, own_cells, low_cells, high_cells = kernel_call(
         functools.partial(inverse_z_kernel, x_local, y_local, cell_count),
-        [
-            pltpu.VMEM(flat_plastic.shape, f32),
-            jax.ShapeDtypeStruct((cell_count, 8, cap), f32),
-            end,
-            end,
-        ],
+        [pltpu.VMEM(flat_plastic.shape, f32), cells, end, end],
         places="vvvv",
         out_places="vvvv",
-    )(voxels[0], waves.reshape(rows, LANES), flat_plastic, inverse_z)
+    )(voxels[0], waves.reshape(rows, LANES), local, inverse_z)
     left, right = neighbours(low_cells, high_cells)
     sampled = pltpu.VMEM((8 * SLOTS, LANES), f32)
+    whole = (comp_count, per_comp, LANES)
     stress, part = kernel_call(
         functools.partial(own_moves_kernel, cell_count),
         [
-            jax.ShapeDtypeStruct(stress.shape, f32),
+            jax.ShapeDtypeStruct(whole, f32),
             jax.ShapeDtypeStruct((SLOTS * FEATURES, cap), f32),
         ],
-        pair_scratch + [sampled, pltpu.SemaphoreType.DMA],
-        places="vvvv",
+        pair_scratch
+        + [sampled, pltpu.VMEM(whole, f32), pltpu.SemaphoreType.DMA((cell_count,))],
+        places="vvvvv",
         out_places="hv",
-    )(start, first, own_cells, stress)
+    )(start, first, own_cells, strain.reshape(whole), plastic.reshape(whole))
     (moved,) = kernel_call(
         functools.partial(moves_kernel, cell_count),
         [jax.ShapeDtypeStruct((3, cell_count, cap), f32)],

time: 104 us -> 104 us (level)
  waiting for transfers between devices: 34 us -> 32.9 us
  transfers between devices with their start and end apart: 5 -> 5, of which waited for: 4 -> 3; matrix products, arithmetic and copies ran while one was open for 0% -> 0% of each run, Pallas kernels for 2% -> 3%
where the time goes in v6:
time: 104 us
  blocking collectives  45.1 us (43%)
  waiting for transfers between devices  32.9 us (32%)
  Pallas kernels  15.3 us (15%)
  starting transfers between devices  9.04 us (9%)
    all_to_all x1, blocking collectives, slab_body(): waves = exchange(waves.reshape(blocks))  45.1 us
    all_to_all x1, waiting for transfers between devices, slab_body(): waves = exchange(waves.reshape(blocks))  22.9 us
    ppermute x2, waiting for transfers between devices, neighbours(): lax.ppermute(high, 'gx', forward)  9.93 us
    pallas_call x1, Pallas kernels, slab_body(): kernel_call(functools.partial(spectral_kernel, gx_count, pa_count, y_loca...  4.95 us
    ppermute x2, starting transfers between devices, neighbours(): lax.ppermute(high, 'gx', forward)  3.1 us
    all_to_all x1, starting transfers between devices, slab_body(): waves = exchange(waves.reshape(blocks))  3.09 us
    ppermute x2, starting transfers between devices, neighbours(): lax.ppermute(low, 'gx', backward)  2.85 us
    pallas_call x1, Pallas kernels, slab_body(): kernel_call(functools.partial(forward_z_kernel, x_local, y_local), [pltpu...  2.73 us
  transfers between devices with their start and end apart: 5, of which 3 were waited for; matrix products, arithmetic and copies ran while one was open for 0% of the time, Pallas kernels for 3%

profile of v6, /device:TPU:0, one launch (start us, length us, event | category | flops | bytes accessed | tf_op | source)
XLA Modules:
  0.0 103.6 jit_solution(6700131713415961433)
XLA Ops:
  0.7 2.7 %shard_map.131 = f32[3072,128]{1,0:T(8,128)S(1)} custom-call(f32[3072,128]{1,0:T(8,128)} %bitcast.17, bf16[2,128,128]{2,1,0:T(8,128)(2,1)} %constant.50.clone.table_ref), custom_call_target="tpu_custom_call" | custom-call | bytes 1048576 | tf_op jit(solution)/shard_map/pallas_call | solution.py:779
  3.4 0.0 copy-start.1
  3.4 0.0 copy-start.2
  3.4 0.0 copy-start.3
  3.4 0.0 copy-start.4
  3.5 45.1 %all_to_all.10 = f32[32,96,128]{2,1,0:T(8,128)S(1)} all-to-all(f32[32,96,128]{2,1,0:T(8,128)S(1)} %bitcast.22), channel_id=1, replica_groups={{0,1,8,9,16,17,24,25,2,3,10,11,18,19,26,27,4,5,12,13,20,21,28,29,6,7,14..., dimensions={0} | all-to-all | bytes 3145728 | tf_op jit(solution)/shard_map/all_to_all | solution.py:791
  48.6 0.0 copy-done.1
  48.6 0.0 copy-done.2
  48.6 0.0 copy-done.3
  48.6 0.0 copy-done.4
  48.6 4.9 %shard_map.132 = f32[4,4,2,2,3,16,128]{6,5,4,3,2,1,0:T(8,128)} custom-call(f32[2]{0:T(128)S(1)} %add_convert_fusion.freq_ref, f32[4,4,2,2,3,16,128]{6,5,4,3,2,1,0:T(8,128)S(1)} %bitcast.21, bf16[2,256,256]{2,1,0:T(8,128)(2,1)S(1)} %copy-done.4, bf16[2,256,256]{2,1,0:T(8,128)(2,1)S(1)} %copy-done.3, bf16[2,256,256]{2,1,0:T(8,128)(2,1)S(1)} %copy-done.2, ...), custom_call_target="tpu_custom_call" | custom-call | bytes 1048576 | tf_op jit(solution)/shard_map/pallas_call | solution.py:792
  53.6 0.0 copy-start.10
  53.6 0.0 copy-start.9
  53.6 0.0 copy-start.7
  53.6 0.0 copy-start.8
  53.6 0.0 copy-start
  53.6 0.0 copy-start.6
  53.6 3.1 %all-to-all-start.1 = ((f32[32,96,128]{2,1,0:T(8,128)}), f32[32,96,128]{2,1,0:T(8,128)S(1)}, u32[]{:S(2)}, u32[]{:S(2)}) async-start(f32[32,96,128]{2,1,0:T(8,128)} %bitcast.26), calls=%async_computation.1 | async-start | bytes 3145728 | tf_op jit(solution)/shard_map/all_to_all | solution.py:806
  56.7 0.0 copy-start.5
  56.7 0.0 copy-done.10
  56.7 0.1 fusion
  56.8 0.0 copy-done.9
  56.8 0.0 copy-done.7
  56.8 0.0 copy-done.8
  56.9 1.8 %collective-permute-start = (f32[9,3,128]{2,1,0:T(4,128)S(1)}, f32[9,3,128]{2,1,0:T(4,128)S(1)}, u32[]{:S(2)}, u32[]{:S(2)}) collective-permute-start(f32[9,3,128]{2,1,0:T(4,128)S(1)} %get-tuple-element.40), channel_id=1, source_target_pairs={{0,8},{8,16},{16,24},{24,0},{1,9},{9,17},{17,25},{25,1},{2,10},{10... | collective-permute-start | bytes 41480 | tf_op jit(solution)/shard_map/ppermute | solution.py:738
  58.7 1.2 %collective-permute-start.1 = (f32[9,3,128]{2,1,0:T(4,128)S(1)}, f32[9,3,128]{2,1,0:T(4,128)S(1)}, u32[]{:S(2)}, u32[]{:S(2)}) collective-permute-start(f32[9,3,128]{2,1,0:T(4,128)S(1)} %get-tuple-element.41), channel_id=1, source_target_pairs={{8,0},{16,8},{24,16},{0,24},{9,1},{17,9},{25,17},{1,25},{10,2},{18... | collective-permute-start | bytes 41480 | tf_op jit(solution)/shard_map/ppermute | solution.py:738
  59.8 0.1 pad.5.clone
  59.9 9.9 %collective-permute-done = f32[9,3,128]{2,1,0:T(4,128)S(1)} collective-permute-done((f32[9,3,128]{2,1,0:T(4,128)S(1)}, f32[9,3,128]{2,1,0:T(4,128)S(1)}, u32[]{:S(2)}, u32[]{:S(2)}) %collective-permute-start) | collective-permute-done | bytes 13856 | tf_op jit(solution)/shard_map/ppermute | solution.py:738
  69.9 0.0 collective-permute-done.1
  69.9 0.1 maximum_maximum_fusion.start_ref
  69.9 0.0 copy-done
  69.9 0.0 copy-done.6
  69.9 1.6 %shard_map.133 = (f32[6,16,128]{2,1,0:T(8,128)S(1)}, f32[4,8,128]{2,1,0:T(8,128)S(1)}) custom-call(f32[9,16,128]{2,1,0:T(8,128)S(1)} %maximum_maximum_fusion.start_ref, s32[4,128]{1,0:T(4,128)S(1)} %bitcast.24, f32[3072,128]{1,0:T(8,128)S(1)} %bitcast.18), custom_call_target="tpu_custom_call" | custom-call | bytes 1048576 | tf_op jit(solution)/shard_map/pallas_call | solution.py:820
  71.5 22.9 %all-to-all-done.1 = f32[32,96,128]{2,1,0:T(8,128)S(1)} async-done(((f32[32,96,128]{2,1,0:T(8,128)}), f32[32,96,128]{2,1,0:T(8,128)S(1)}, u32[]{:S(2)}, u32[]{:S(2)}) %all-to-all-start.1) | async-done | bytes 1572896 | tf_op jit(solution)/shard_map/all_to_all | solution.py:806
  94.4 0.0 copy-done.5
  94.4 2.2 %shard_map.134 = (f32[3072,128]{1,0:T(8,128)S(1)}, f32[4,8,128]{2,1,0:T(8,128)S(1)}, f32[2,8,128]{2,1,0:T(8,128)S(1)}, f32[2,8,128]{2,1,0:T(8,128)S(1)}) custom-call(s32[4,128]{1,0:T(4,128)S(1)} %bitcast.25, f32[3072,128]{1,0:T(8,128)S(1)} %bitcast.20, f32[4,8,128]{2,1,0:T(8,128)S(1)} %get-tuple-element.31.local_ref, bf16[2,128,128]{2,1,0:T(8,128)(2,1)S(1)} %copy-done.5), custom_call_target="tpu_custom_call" | custom-call | bytes 1048576 | tf_op jit(solution)/shard_map/pallas_call | solution.py:830
  96.6 1.3 %collective-permute-start.2 = (f32[2,8,128]{2,1,0:T(8,128)S(1)}, f32[2,8,128]{2,1,0:T(8,128)S(1)}, u32[]{:S(2)}, u32[]{:S(2)}) collective-permute-start(f32[2,8,128]{2,1,0:T(8,128)S(1)} %get-tuple-element.35), channel_id=1, source_target_pairs={{0,8},{8,16},{16,24},{24,0},{1,9},{9,17},{17,25},{25,1},{2,10},{10... | collective-permute-start | bytes 24584 | tf_op jit(solution)/shard_map/ppermute | solution.py:738
  97.9 1.7 %collective-permute-start.3 = (f32[2,8,128]{2,1,0:T(8,128)S(1)}, f32[2,8,128]{2,1,0:T(8,128)S(1)}, u32[]{:S(2)}, u32[]{:S(2)}) collective-permute-start(f32[2,8,128]{2,1,0:T(8,128)S(1)} %get-tuple-element.36), channel_id=1, source_target_pairs={{8,0},{16,8},{24,16},{0,24},{9,1},{17,9},{25,17},{1,25},{10,2},{18... | collective-permute-start | bytes 24584 | tf_op jit(solution)/shard_map/ppermute | solution.py:738
  99.6 1.8 %shard_map.135 = (f32[6,512,128]{2,1,0:T(8,128)}, f32[384,128]{1,0:T(8,128)S(1)}) custom-call(f32[9,16,128]{2,1,0:T(8,128)S(1)} %maximum_maximum_fusion.start_ref, f32[6,16,128]{2,1,0:T(8,128)S(1)} %get-tuple-element.29.first_ref, f32[4,8,128]{2,1,0:T(8,128)S(1)} %get-tuple-element.32.own_ref, f32[6,512,128]{2,1,0:T(8,128)S(1)} %bitcast.23, ...), custom_call_target="tpu_custom_call" | custom-call | bytes 1048576 | tf_op jit(solution)/shard_map/pallas_call | solution.py:839
  101.5 0.0 collective-permute-done.2.left_ref
  101.5 0.1 collective-permute-done.3.right_ref
  101.6 2.0 %shard_map.136 = f32[3,4,128]{2,1,0:T(4,128)} custom-call(f32[9,16,128]{2,1,0:T(8,128)S(1)} %maximum_maximum_fusion.start_ref, f32[6,16,128]{2,1,0:T(8,128)S(1)} %get-tuple-element.29.first_ref, f32[2,8,128]{2,1,0:T(8,128)S(1)} %collective-permute-done.2.left_ref, f32[4,8,128]{2,1,0:T(8,128)S(1)} %get-tuple-element.32.own_ref, ...), custom_call_target="tpu_custom_call" | custom-call | bytes 1048576 | tf_op jit(solution)/shard_map/pallas_call | solution.py:850
  (5 shorter events, 0.0 us)
Async XLA Ops:
  3.4 45.2 %copy-start.1 = (bf16[2,256,256]{2,1,0:T(8,128)(2,1)S(1)}, bf16[2,256,256]{2,1,0:T(8,128)(2,1)}, u32[]{:S(2)}) copy-start(bf16[2,256,256]{2,1,0:T(8,128)(2,1)} %constant.54.clone.inverse_y_ref) | copy-start | bytes 786436
  3.4 45.2 %copy-start.2 = (bf16[2,256,256]{2,1,0:T(8,128)(2,1)S(1)}, bf16[2,256,256]{2,1,0:T(8,128)(2,1)}, u32[]{:S(2)}) copy-start(bf16[2,256,256]{2,1,0:T(8,128)(2,1)} %constant.53.clone.inverse_x_ref) | copy-start | bytes 786436
  3.4 45.2 %copy-start.3 = (bf16[2,256,256]{2,1,0:T(8,128)(2,1)S(1)}, bf16[2,256,256]{2,1,0:T(8,128)(2,1)}, u32[]{:S(2)}) copy-start(bf16[2,256,256]{2,1,0:T(8,128)(2,1)} %constant.52.clone.forward_x_ref) | copy-start | bytes 786436
  3.4 45.1 %copy-start.4 = (bf16[2,256,256]{2,1,0:T(8,128)(2,1)S(1)}, bf16[2,256,256]{2,1,0:T(8,128)(2,1)}, u32[]{:S(2)}) copy-start(bf16[2,256,256]{2,1,0:T(8,128)(2,1)} %constant.51.clone.forward_y_ref) | copy-start | bytes 786436
  53.6 3.2 %copy-start.10 = (s32[1,4]{1,0:T(1,128)S(1)}, s32[1,4]{1,0:T(1,128)}, u32[]{:S(2)}) copy-start(s32[1,4]{1,0:T(1,128)} %param.16) | copy-start | bytes 52
  53.6 3.3 %copy-start.9 = (f32[3,1,4,128]{3,2,1,0:T(4,128)S(1)}, f32[3,1,4,128]{3,2,1,0:T(4,128)}, u32[]{:S(2)}) copy-start(f32[3,1,4,128]{3,2,1,0:T(4,128)} %param.15) | copy-start | bytes 18436
  53.6 3.2 %copy-start.7 = (f32[3,1,4,128]{3,2,1,0:T(4,128)S(1)}, f32[3,1,4,128]{3,2,1,0:T(4,128)}, u32[]{:S(2)}) copy-start(f32[3,1,4,128]{3,2,1,0:T(4,128)} %param.14) | copy-start | bytes 18436
  53.6 3.2 %copy-start.8 = (f32[3,1,4,128]{3,2,1,0:T(4,128)S(1)}, f32[3,1,4,128]{3,2,1,0:T(4,128)}, u32[]{:S(2)}) copy-start(f32[3,1,4,128]{3,2,1,0:T(4,128)} %param.13) | copy-start | bytes 18436
  53.6 16.3 %copy-start = (f32[6,32,16,128]{3,2,1,0:T(8,128)S(1)}, f32[6,32,16,128]{3,2,1,0:T(8,128)}, u32[]{:S(2)}) copy-start(f32[6,32,16,128]{3,2,1,0:T(8,128)} %param.12) | copy-start | bytes 4718596
  53.6 16.3 %copy-start.6 = (s32[1,4,128]{2,1,0:T(4,128)S(1)}, s32[1,4,128]{2,1,0:T(4,128)}, u32[]{:S(2)}) copy-start(s32[1,4,128]{2,1,0:T(4,128)} %param.17) | copy-start | bytes 6148
  53.6 40.8 %all-to-all-start.1 = ((f32[32,96,128]{2,1,0:T(8,128)}), f32[32,96,128]{2,1,0:T(8,128)S(1)}, u32[]{:S(2)}, u32[]{:S(2)}) async-start(f32[32,96,128]{2,1,0:T(8,128)} %bitcast.26), calls=%async_computation.1 | async-start | bytes 3145728 | tf_op jit(solution)/shard_map/all_to_all | solution.py:806
  56.7 37.7 %copy-start.5 = (bf16[2,128,128]{2,1,0:T(8,128)(2,1)S(1)}, bf16[2,128,128]{2,1,0:T(8,128)(2,1)}, u32[]{:S(2)}) copy-start(bf16[2,128,128]{2,1,0:T(8,128)(2,1)} %constant.55.clone.table_ref) | copy-start | bytes 196612
  56.9 13.0 %collective-permute-start = (f32[9,3,128]{2,1,0:T(4,128)S(1)}, f32[9,3,128]{2,1,0:T(4,128)S(1)}, u32[]{:S(2)}, u32[]{:S(2)}) collective-permute-start(f32[9,3,128]{2,1,0:T(4,128)S(1)} %get-tuple-element.40), channel_id=1, source_target_pairs={{0,8},{8,16},{16,24},{24,0},{1,9},{9,17},{17,25},{25,1},{2,10},{10... | collective-permute-start | bytes 41480 | tf_op jit(solution)/shard_map/ppermute | solution.py:738
  58.7 11.2 %collective-permute-start.1 = (f32[9,3,128]{2,1,0:T(4,128)S(1)}, f32[9,3,128]{2,1,0:T(4,128)S(1)}, u32[]{:S(2)}, u32[]{:S(2)}) collective-permute-start(f32[9,3,128]{2,1,0:T(4,128)S(1)} %get-tuple-element.41), channel_id=1, source_target_pairs={{8,0},{16,8},{24,16},{0,24},{9,1},{17,9},{25,17},{1,25},{10,2},{18... | collective-permute-start | bytes 41480 | tf_op jit(solution)/shard_map/ppermute | solution.py:738
  96.6 4.8 %collective-permute-start.2 = (f32[2,8,128]{2,1,0:T(8,128)S(1)}, f32[2,8,128]{2,1,0:T(8,128)S(1)}, u32[]{:S(2)}, u32[]{:S(2)}) collective-permute-start(f32[2,8,128]{2,1,0:T(8,128)S(1)} %get-tuple-element.35), channel_id=1, source_target_pairs={{0,8},{8,16},{16,24},{24,0},{1,9},{9,17},{17,25},{25,1},{2,10},{10... | collective-permute-start | bytes 24584 | tf_op jit(solution)/shard_map/ppermute | solution.py:738
  97.9 3.7 %collective-permute-start.3 = (f32[2,8,128]{2,1,0:T(8,128)S(1)}, f32[2,8,128]{2,1,0:T(8,128)S(1)}, u32[]{:S(2)}, u32[]{:S(2)}) collective-permute-start(f32[2,8,128]{2,1,0:T(8,128)S(1)} %get-tuple-element.36), channel_id=1, source_target_pairs={{8,0},{16,8},{24,16},{0,24},{9,1},{17,9},{25,17},{1,25},{10,2},{18... | collective-permute-start | bytes 24584 | tf_op jit(solution)/shard_map/ppermute | solution.py:738

commit v7 on v6

--- a/solution.py
+++ b/solution.py
@@ -248,6 +248,10 @@
     )
 
 
+def gray(count):
+    return [i ^ (i >> 1) for i in range(count)]
+
+
 def tables(grid_len, pa_count, y_local):
     index = np.arange(grid_len)
     bins = np.arange(grid_len // 2)
@@ -264,9 +268,12 @@
     ahead = np.array([[cos, sin], [-sin, cos]]).transpose(0, 2, 1, 3)
     back = np.array([[cos, -sin], [sin, cos]]).transpose(0, 2, 1, 3) / grid_len
     size = 2 * grid_len
-    forward_y = ahead.reshape(2, grid_len, 2, pa_count, y_local).transpose(3, 2, 4, 0, 1)
+    chips = gray(pa_count // 2)
+    forward_y = ahead.reshape(2, grid_len, 2, pa_count // 2, 2, y_local)
+    forward_y = forward_y.transpose(3, 4, 2, 5, 0, 1)[chips]
     forward_y = forward_y.reshape(size, size)
-    inverse_y = back.reshape(2, pa_count, y_local, 2, grid_len).transpose(3, 4, 1, 0, 2)
+    inverse_y = back.reshape(2, pa_count // 2, 2, y_local, 2, grid_len)
+    inverse_y = inverse_y.transpose(4, 5, 1, 2, 0, 3)[:, :, chips]
     inverse_y = inverse_y.reshape(size, size)
     forward_x = ahead.reshape(size, size)
     inverse_x = back.reshape(size, size)
@@ -755,7 +762,7 @@
     order = [
         [
             g * pa_count + 2 * z + core
-            for z in range(pa_count // 2)
+            for z in gray(pa_count // 2)
             for g in range(gx_count)
             for core in range(2)
         ]
@@ -769,7 +776,10 @@
         tiled=True,
     )
     pa_index = lax.axis_index("pa")
-    own = (pa_index // 2 * gx_count + lax.axis_index("gx")) * 2 + pa_index % 2
+    place = pa_index // 2
+    for shift in (1, 2, 4, 8):
+        place = place ^ (pa_index // 2 >> shift)
+    own = (place * gx_count + lax.axis_index("gx")) * 2 + pa_index % 2
     bins = (own + devices * jnp.arange(2, dtype=jnp.int32)).astype(f32)
     flat_plastic = plastic.reshape(-1, grid_len)
     tile_sems = pltpu.SemaphoreType.DMA((tiles,))

time: 104 us -> 103 us (level)
    all_to_all x1, waiting for transfers between devices: 22.9 us -> 20.5 us  [slab_body(): waves = exchange(waves.reshape(blocks))]
    ppermute x2, waiting for transfers between devices: 9.93 us -> 11.6 us  [neighbours(): lax.ppermute(high, 'gx', forward)]
where the time goes in v7:
time: 103 us
  blocking collectives  44.7 us (43%)
  waiting for transfers between devices  32.3 us (31%)
  Pallas kernels  15.3 us (15%)
  starting transfers between devices  9.06 us (9%)
    all_to_all x1, blocking collectives, slab_body(): waves = exchange(waves.reshape(blocks))  44.7 us
    all_to_all x1, waiting for transfers between devices, slab_body(): waves = exchange(waves.reshape(blocks))  20.5 us
    ppermute x2, waiting for transfers between devices, neighbours(): lax.ppermute(high, 'gx', forward)  11.6 us
    pallas_call x1, Pallas kernels, slab_body(): kernel_call(functools.partial(spectral_kernel, gx_count, pa_count, y_loca...  4.95 us
    ppermute x2, starting transfers between devices, neighbours(): lax.ppermute(high, 'gx', forward)  3.28 us
    all_to_all x1, starting transfers between devices, slab_body(): waves = exchange(waves.reshape(blocks))  3.11 us
    pallas_call x1, Pallas kernels, slab_body(): kernel_call(functools.partial(forward_z_kernel, x_local, y_local), [pltpu...  2.74 us
    ppermute x2, starting transfers between devices, neighbours(): lax.ppermute(low, 'gx', backward)  2.67 us
  transfers between devices with their start and end apart: 5, of which 3 were waited for; matrix products, arithmetic and copies ran while one was open for 0% of the time, Pallas kernels for 3%

profile of v7, /device:TPU:0, one launch (start us, length us, event | category | flops | bytes accessed | tf_op | source)
XLA Modules:
  0.0 102.6 jit_solution(5134371016811748189)
XLA Ops:
  0.7 2.7 %shard_map.131 = f32[3072,128]{1,0:T(8,128)S(1)} custom-call(f32[3072,128]{1,0:T(8,128)} %bitcast.17, bf16[2,128,128]{2,1,0:T(8,128)(2,1)} %constant.61.clone.table_ref), custom_call_target="tpu_custom_call" | custom-call | bytes 1048576 | tf_op jit(solution)/shard_map/pallas_call | solution.py:789
  3.4 0.0 copy-start.1
  3.4 0.0 copy-start.2
  3.4 0.0 copy-start.3
  3.4 0.0 copy-start.4
  3.5 44.7 %all_to_all.10 = f32[32,96,128]{2,1,0:T(8,128)S(1)} all-to-all(f32[32,96,128]{2,1,0:T(8,128)S(1)} %bitcast.22), channel_id=1, replica_groups={{0,1,8,9,16,17,24,25,2,3,10,11,18,19,26,27,6,7,14,15,22,23,30,31,4,5,12..., dimensions={0} | all-to-all | bytes 3145728 | tf_op jit(solution)/shard_map/all_to_all | solution.py:801
  48.2 0.0 copy-done.1
  48.2 0.0 copy-done.2
  48.2 0.0 copy-done.3
  48.2 0.0 copy-done.4
  48.2 5.0 %shard_map.132 = f32[4,4,2,2,3,16,128]{6,5,4,3,2,1,0:T(8,128)} custom-call(f32[2]{0:T(128)S(1)} %add_convert_fusion.freq_ref, f32[4,4,2,2,3,16,128]{6,5,4,3,2,1,0:T(8,128)S(1)} %bitcast.21, bf16[2,256,256]{2,1,0:T(8,128)(2,1)S(1)} %copy-done.4, bf16[2,256,256]{2,1,0:T(8,128)(2,1)S(1)} %copy-done.3, bf16[2,256,256]{2,1,0:T(8,128)(2,1)S(1)} %copy-done.2, ...), custom_call_target="tpu_custom_call" | custom-call | bytes 1048576 | tf_op jit(solution)/shard_map/pallas_call | solution.py:802
  53.1 0.0 copy-start.10
  53.1 0.0 copy-start.9
  53.2 0.0 copy-start.7
  53.2 0.0 copy-start.8
  53.2 0.0 copy-start
  53.2 0.0 copy-start.6
  53.2 3.1 %all-to-all-start.1 = ((f32[32,96,128]{2,1,0:T(8,128)}), f32[32,96,128]{2,1,0:T(8,128)S(1)}, u32[]{:S(2)}, u32[]{:S(2)}) async-start(f32[32,96,128]{2,1,0:T(8,128)} %bitcast.26), calls=%async_computation.1 | async-start | bytes 3145728 | tf_op jit(solution)/shard_map/all_to_all | solution.py:816
  56.3 0.0 copy-start.5
  56.3 0.0 copy-done.10
  56.3 0.1 fusion
  56.4 0.0 copy-done.9
  56.4 0.0 copy-done.7
  56.4 0.0 copy-done.8
  56.5 1.8 %collective-permute-start = (f32[9,3,128]{2,1,0:T(4,128)S(1)}, f32[9,3,128]{2,1,0:T(4,128)S(1)}, u32[]{:S(2)}, u32[]{:S(2)}) collective-permute-start(f32[9,3,128]{2,1,0:T(4,128)S(1)} %get-tuple-element.40), channel_id=1, source_target_pairs={{0,8},{8,16},{16,24},{24,0},{1,9},{9,17},{17,25},{25,1},{2,10},{10... | collective-permute-start | bytes 41480 | tf_op jit(solution)/shard_map/ppermute | solution.py:745
  58.3 1.2 %collective-permute-start.1 = (f32[9,3,128]{2,1,0:T(4,128)S(1)}, f32[9,3,128]{2,1,0:T(4,128)S(1)}, u32[]{:S(2)}, u32[]{:S(2)}) collective-permute-start(f32[9,3,128]{2,1,0:T(4,128)S(1)} %get-tuple-element.41), channel_id=1, source_target_pairs={{8,0},{16,8},{24,16},{0,24},{9,1},{17,9},{25,17},{1,25},{10,2},{18... | collective-permute-start | bytes 41480 | tf_op jit(solution)/shard_map/ppermute | solution.py:745
  59.5 0.1 pad.5.clone
  59.5 11.6 %collective-permute-done = f32[9,3,128]{2,1,0:T(4,128)S(1)} collective-permute-done((f32[9,3,128]{2,1,0:T(4,128)S(1)}, f32[9,3,128]{2,1,0:T(4,128)S(1)}, u32[]{:S(2)}, u32[]{:S(2)}) %collective-permute-start) | collective-permute-done | bytes 13856 | tf_op jit(solution)/shard_map/ppermute | solution.py:745
  71.1 0.0 collective-permute-done.1
  71.1 0.1 maximum_maximum_fusion.start_ref
  71.2 0.0 copy-done
  71.2 0.0 copy-done.6
  71.2 1.6 %shard_map.133 = (f32[6,16,128]{2,1,0:T(8,128)S(1)}, f32[4,8,128]{2,1,0:T(8,128)S(1)}) custom-call(f32[9,16,128]{2,1,0:T(8,128)S(1)} %maximum_maximum_fusion.start_ref, s32[4,128]{1,0:T(4,128)S(1)} %bitcast.24, f32[3072,128]{1,0:T(8,128)S(1)} %bitcast.18), custom_call_target="tpu_custom_call" | custom-call | bytes 1048576 | tf_op jit(solution)/shard_map/pallas_call | solution.py:830
  72.8 20.5 %all-to-all-done.1 = f32[32,96,128]{2,1,0:T(8,128)S(1)} async-done(((f32[32,96,128]{2,1,0:T(8,128)}), f32[32,96,128]{2,1,0:T(8,128)S(1)}, u32[]{:S(2)}, u32[]{:S(2)}) %all-to-all-start.1) | async-done | bytes 1572896 | tf_op jit(solution)/shard_map/all_to_all | solution.py:816
  93.2 0.0 copy-done.5
  93.2 2.2 %shard_map.134 = (f32[3072,128]{1,0:T(8,128)S(1)}, f32[4,8,128]{2,1,0:T(8,128)S(1)}, f32[2,8,128]{2,1,0:T(8,128)S(1)}, f32[2,8,128]{2,1,0:T(8,128)S(1)}) custom-call(s32[4,128]{1,0:T(4,128)S(1)} %bitcast.25, f32[3072,128]{1,0:T(8,128)S(1)} %bitcast.20, f32[4,8,128]{2,1,0:T(8,128)S(1)} %get-tuple-element.31.local_ref, bf16[2,128,128]{2,1,0:T(8,128)(2,1)S(1)} %copy-done.5), custom_call_target="tpu_custom_call" | custom-call | bytes 1048576 | tf_op jit(solution)/shard_map/pallas_call | solution.py:840
  95.4 1.5 %collective-permute-start.2 = (f32[2,8,128]{2,1,0:T(8,128)S(1)}, f32[2,8,128]{2,1,0:T(8,128)S(1)}, u32[]{:S(2)}, u32[]{:S(2)}) collective-permute-start(f32[2,8,128]{2,1,0:T(8,128)S(1)} %get-tuple-element.35), channel_id=1, source_target_pairs={{0,8},{8,16},{16,24},{24,0},{1,9},{9,17},{17,25},{25,1},{2,10},{10... | collective-permute-start | bytes 24584 | tf_op jit(solution)/shard_map/ppermute | solution.py:745
  96.9 1.5 %collective-permute-start.3 = (f32[2,8,128]{2,1,0:T(8,128)S(1)}, f32[2,8,128]{2,1,0:T(8,128)S(1)}, u32[]{:S(2)}, u32[]{:S(2)}) collective-permute-start(f32[2,8,128]{2,1,0:T(8,128)S(1)} %get-tuple-element.36), channel_id=1, source_target_pairs={{8,0},{16,8},{24,16},{0,24},{9,1},{17,9},{25,17},{1,25},{10,2},{18... | collective-permute-start | bytes 24584 | tf_op jit(solution)/shard_map/ppermute | solution.py:745
  98.4 1.8 %shard_map.135 = (f32[6,512,128]{2,1,0:T(8,128)}, f32[384,128]{1,0:T(8,128)S(1)}) custom-call(f32[9,16,128]{2,1,0:T(8,128)S(1)} %maximum_maximum_fusion.start_ref, f32[6,16,128]{2,1,0:T(8,128)S(1)} %get-tuple-element.29.first_ref, f32[4,8,128]{2,1,0:T(8,128)S(1)} %get-tuple-element.32.own_ref, f32[6,512,128]{2,1,0:T(8,128)S(1)} %bitcast.23, ...), custom_call_target="tpu_custom_call" | custom-call | bytes 1048576 | tf_op jit(solution)/shard_map/pallas_call | solution.py:849
  100.3 0.0 collective-permute-done.2.left_ref
  100.3 0.3 collective-permute-done.3.right_ref
  100.5 2.0 %shard_map.136 = f32[3,4,128]{2,1,0:T(4,128)} custom-call(f32[9,16,128]{2,1,0:T(8,128)S(1)} %maximum_maximum_fusion.start_ref, f32[6,16,128]{2,1,0:T(8,128)S(1)} %get-tuple-element.29.first_ref, f32[2,8,128]{2,1,0:T(8,128)S(1)} %collective-permute-done.2.left_ref, f32[4,8,128]{2,1,0:T(8,128)S(1)} %get-tuple-element.32.own_ref, ...), custom_call_target="tpu_custom_call" | custom-call | bytes 1048576 | tf_op jit(solution)/shard_map/pallas_call | solution.py:860
  (5 shorter events, 0.0 us)
Async XLA Ops:
  3.4 44.7 %copy-start.1 = (bf16[2,256,256]{2,1,0:T(8,128)(2,1)S(1)}, bf16[2,256,256]{2,1,0:T(8,128)(2,1)}, u32[]{:S(2)}) copy-start(bf16[2,256,256]{2,1,0:T(8,128)(2,1)} %constant.65.clone.inverse_y_ref) | copy-start | bytes 786436
  3.4 44.7 %copy-start.2 = (bf16[2,256,256]{2,1,0:T(8,128)(2,1)S(1)}, bf16[2,256,256]{2,1,0:T(8,128)(2,1)}, u32[]{:S(2)}) copy-start(bf16[2,256,256]{2,1,0:T(8,128)(2,1)} %constant.64.clone.inverse_x_ref) | copy-start | bytes 786436
  3.4 44.7 %copy-start.3 = (bf16[2,256,256]{2,1,0:T(8,128)(2,1)S(1)}, bf16[2,256,256]{2,1,0:T(8,128)(2,1)}, u32[]{:S(2)}) copy-start(bf16[2,256,256]{2,1,0:T(8,128)(2,1)} %constant.63.clone.forward_x_ref) | copy-start | bytes 786436
  3.4 44.7 %copy-start.4 = (bf16[2,256,256]{2,1,0:T(8,128)(2,1)S(1)}, bf16[2,256,256]{2,1,0:T(8,128)(2,1)}, u32[]{:S(2)}) copy-start(bf16[2,256,256]{2,1,0:T(8,128)(2,1)} %constant.62.clone.forward_y_ref) | copy-start | bytes 786436
  53.1 3.2 %copy-start.10 = (s32[1,4]{1,0:T(1,128)S(1)}, s32[1,4]{1,0:T(1,128)}, u32[]{:S(2)}) copy-start(s32[1,4]{1,0:T(1,128)} %param.16) | copy-start | bytes 52
  53.1 3.3 %copy-start.9 = (f32[3,1,4,128]{3,2,1,0:T(4,128)S(1)}, f32[3,1,4,128]{3,2,1,0:T(4,128)}, u32[]{:S(2)}) copy-start(f32[3,1,4,128]{3,2,1,0:T(4,128)} %param.15) | copy-start | bytes 18436
  53.2 3.3 %copy-start.7 = (f32[3,1,4,128]{3,2,1,0:T(4,128)S(1)}, f32[3,1,4,128]{3,2,1,0:T(4,128)}, u32[]{:S(2)}) copy-start(f32[3,1,4,128]{3,2,1,0:T(4,128)} %param.14) | copy-start | bytes 18436
  53.2 3.3 %copy-start.8 = (f32[3,1,4,128]{3,2,1,0:T(4,128)S(1)}, f32[3,1,4,128]{3,2,1,0:T(4,128)}, u32[]{:S(2)}) copy-start(f32[3,1,4,128]{3,2,1,0:T(4,128)} %param.13) | copy-start | bytes 18436
  53.2 18.0 %copy-start = (f32[6,32,16,128]{3,2,1,0:T(8,128)S(1)}, f32[6,32,16,128]{3,2,1,0:T(8,128)}, u32[]{:S(2)}) copy-start(f32[6,32,16,128]{3,2,1,0:T(8,128)} %param.12) | copy-start | bytes 4718596
  53.2 18.0 %copy-start.6 = (s32[1,4,128]{2,1,0:T(4,128)S(1)}, s32[1,4,128]{2,1,0:T(4,128)}, u32[]{:S(2)}) copy-start(s32[1,4,128]{2,1,0:T(4,128)} %param.17) | copy-start | bytes 6148
  53.2 40.0 %all-to-all-start.1 = ((f32[32,96,128]{2,1,0:T(8,128)}), f32[32,96,128]{2,1,0:T(8,128)S(1)}, u32[]{:S(2)}, u32[]{:S(2)}) async-start(f32[32,96,128]{2,1,0:T(8,128)} %bitcast.26), calls=%async_computation.1 | async-start | bytes 3145728 | tf_op jit(solution)/shard_map/all_to_all | solution.py:816
  56.3 36.9 %copy-start.5 = (bf16[2,128,128]{2,1,0:T(8,128)(2,1)S(1)}, bf16[2,128,128]{2,1,0:T(8,128)(2,1)}, u32[]{:S(2)}) copy-start(bf16[2,128,128]{2,1,0:T(8,128)(2,1)} %constant.66.clone.table_ref) | copy-start | bytes 196612
  56.5 14.6 %collective-permute-start = (f32[9,3,128]{2,1,0:T(4,128)S(1)}, f32[9,3,128]{2,1,0:T(4,128)S(1)}, u32[]{:S(2)}, u32[]{:S(2)}) collective-permute-start(f32[9,3,128]{2,1,0:T(4,128)S(1)} %get-tuple-element.40), channel_id=1, source_target_pairs={{0,8},{8,16},{16,24},{24,0},{1,9},{9,17},{17,25},{25,1},{2,10},{10... | collective-permute-start | bytes 41480 | tf_op jit(solution)/shard_map/ppermute | solution.py:745
  58.3 12.8 %collective-permute-start.1 = (f32[9,3,128]{2,1,0:T(4,128)S(1)}, f32[9,3,128]{2,1,0:T(4,128)S(1)}, u32[]{:S(2)}, u32[]{:S(2)}) collective-permute-start(f32[9,3,128]{2,1,0:T(4,128)S(1)} %get-tuple-element.41), channel_id=1, source_target_pairs={{8,0},{16,8},{24,16},{0,24},{9,1},{17,9},{25,17},{1,25},{10,2},{18... | collective-permute-start | bytes 41480 | tf_op jit(solution)/shard_map/ppermute | solution.py:745
  95.4 4.8 %collective-permute-start.2 = (f32[2,8,128]{2,1,0:T(8,128)S(1)}, f32[2,8,128]{2,1,0:T(8,128)S(1)}, u32[]{:S(2)}, u32[]{:S(2)}) collective-permute-start(f32[2,8,128]{2,1,0:T(8,128)S(1)} %get-tuple-element.35), channel_id=1, source_target_pairs={{0,8},{8,16},{16,24},{24,0},{1,9},{9,17},{17,25},{25,1},{2,10},{10... | collective-permute-start | bytes 24584 | tf_op jit(solution)/shard_map/ppermute | solution.py:745
  96.9 3.7 %collective-permute-start.3 = (f32[2,8,128]{2,1,0:T(8,128)S(1)}, f32[2,8,128]{2,1,0:T(8,128)S(1)}, u32[]{:S(2)}, u32[]{:S(2)}) collective-permute-start(f32[2,8,128]{2,1,0:T(8,128)S(1)} %get-tuple-element.36), channel_id=1, source_target_pairs={{8,0},{16,8},{24,16},{0,24},{9,1},{17,9},{25,17},{1,25},{10,2},{18... | collective-permute-start | bytes 24584 | tf_op jit(solution)/shard_map/ppermute | solution.py:745

commit v8 on v7

--- a/solution.py
+++ b/solution.py
@@ -519,7 +519,7 @@
             high_cells_ref[cell - cell_count + 2] = found
 
 
-def pair_moments(position, fixed, scratch, pairs, add=()):
+def pair_moments(position, fixed, scratch, pairs, add=(), fresh=True):
     columns, features, moments = scratch
     slots = position[0].shape[0]
     lines, burgers = fixed
@@ -533,7 +533,8 @@
         shifted = [moved[0], moved[1] - offset * lines[2], moved[2] + offset * lines[1]]
         for b in range(3):
             for a in range(3):
-                features[shift, pl.ds((3 * a + b) * slots, slots), :] = lines[a] * burgers[b]
+                if fresh:
+                    features[shift, pl.ds((3 * a + b) * slots, slots), :] = lines[a] * burgers[b]
                 features[shift, pl.ds((9 + 3 * a + b) * slots, slots), :] = shifted[a] * burgers[b]
     for source in sorted({target + shift - 1 for target in pairs for shift in pairs[target]}):
         for a in range(3):
@@ -590,11 +591,6 @@
     return values[0:3], values[3:6], values[6:9]
 
 
-def clear(features, moments):
-    features[...] = jnp.zeros_like(features)
-    moments[...] = jnp.zeros_like(moments)
-
-
 def first_field_kernel(
     per_comp,
     cell_count,
@@ -609,7 +605,7 @@
 ):
     for cell in range(cell_count):
         local_ref[cell] = sample(plastic_ref, voxel_ref, per_comp, cell_count, cell)
-    clear(features, moments)
+    moments[...] = jnp.zeros_like(moments)
     position, lines, burgers = load_fixed(start_ref)
     pair_moments(
         position, (lines, burgers), (columns, features, moments), every_pair(1, cell_count + 5)
@@ -667,7 +663,7 @@
             pltpu.make_async_copy(block.at[:, span], stress_ref.at[:, span], sems.at[cell])
         )
         stores[-1].start()
-    clear(features, moments)
+    moments[...] = jnp.zeros_like(moments)
     position, lines, burgers = load_fixed(start_ref)
     sampled = spread(sampled_ref, [(3, own_ref)])
     field = [first_ref[comp] for comp in range(COMPS)]
@@ -697,7 +693,6 @@
     moments,
     sampled_ref,
 ):
-    features[...] = jnp.zeros_like(features)
     moments[...] = part_ref[...]
     position, lines, burgers = load_fixed(start_ref)
     initial = position
@@ -714,6 +709,7 @@
                 (columns, features, moments),
                 rest if repeat == 1 else every_pair(first, last),
                 (first, last - 1) if repeat == 1 else (),
+                repeat == 1,
             )
             field = pair_field(position, moments)
         position = moved_on(position, lines, burgers, sampled, field)

time: 103 us -> 103 us (level)
  no operation moved by 1% of the time
where the time goes in v8:
time: 103 us
  blocking collectives  44.7 us (43%)
  waiting for transfers between devices  32.3 us (31%)
  Pallas kernels  15.3 us (15%)
  starting transfers between devices  9.06 us (9%)
    all_to_all x1, blocking collectives, slab_body(): waves = exchange(waves.reshape(blocks))  44.7 us
    all_to_all x1, waiting for transfers between devices, slab_body(): waves = exchange(waves.reshape(blocks))  20.5 us
    ppermute x2, waiting for transfers between devices, neighbours(): lax.ppermute(high, 'gx', forward)  11.6 us
    pallas_call x1, Pallas kernels, slab_body(): kernel_call(functools.partial(spectral_kernel, gx_count, pa_count, y_loca...  4.95 us
    ppermute x2, starting transfers between devices, neighbours(): lax.ppermute(high, 'gx', forward)  3.28 us
    all_to_all x1, starting transfers between devices, slab_body(): waves = exchange(waves.reshape(blocks))  3.11 us
    pallas_call x1, Pallas kernels, slab_body(): kernel_call(functools.partial(forward_z_kernel, x_local, y_local), [pltpu...  2.74 us
    ppermute x2, starting transfers between devices, neighbours(): lax.ppermute(low, 'gx', backward)  2.67 us
  transfers between devices with their start and end apart: 5, of which 3 were waited for; matrix products, arithmetic and copies ran while one was open for 0% of the time, Pallas kernels for 3%

profile of v8, /device:TPU:0, one launch (start us, length us, event | category | flops | bytes accessed | tf_op | source)
XLA Modules:
  0.0 102.5 jit_solution(6437192640044524637)
XLA Ops:
  0.7 2.7 %shard_map.131 = f32[3072,128]{1,0:T(8,128)S(1)} custom-call(f32[3072,128]{1,0:T(8,128)} %bitcast.17, bf16[2,128,128]{2,1,0:T(8,128)(2,1)} %constant.61.clone.table_ref), custom_call_target="tpu_custom_call" | custom-call | bytes 1048576 | tf_op jit(solution)/shard_map/pallas_call | solution.py:785
  3.4 0.0 copy-start.1
  3.4 0.0 copy-start.2
  3.4 0.0 copy-start.3
  3.4 0.0 copy-start.4
  3.5 44.7 %all_to_all.10 = f32[32,96,128]{2,1,0:T(8,128)S(1)} all-to-all(f32[32,96,128]{2,1,0:T(8,128)S(1)} %bitcast.22), channel_id=1, replica_groups={{0,1,8,9,16,17,24,25,2,3,10,11,18,19,26,27,6,7,14,15,22,23,30,31,4,5,12..., dimensions={0} | all-to-all | bytes 3145728 | tf_op jit(solution)/shard_map/all_to_all | solution.py:797
  48.2 0.0 copy-done.1
  48.2 0.0 copy-done.2
  48.2 0.0 copy-done.3
  48.2 0.0 copy-done.4
  48.2 5.0 %shard_map.132 = f32[4,4,2,2,3,16,128]{6,5,4,3,2,1,0:T(8,128)} custom-call(f32[2]{0:T(128)S(1)} %add_convert_fusion.freq_ref, f32[4,4,2,2,3,16,128]{6,5,4,3,2,1,0:T(8,128)S(1)} %bitcast.21, bf16[2,256,256]{2,1,0:T(8,128)(2,1)S(1)} %copy-done.4, bf16[2,256,256]{2,1,0:T(8,128)(2,1)S(1)} %copy-done.3, bf16[2,256,256]{2,1,0:T(8,128)(2,1)S(1)} %copy-done.2, ...), custom_call_target="tpu_custom_call" | custom-call | bytes 1048576 | tf_op jit(solution)/shard_map/pallas_call | solution.py:798
  53.1 0.0 copy-start.10
  53.1 0.0 copy-start.9
  53.2 0.0 copy-start.7
  53.2 0.0 copy-start.8
  53.2 0.0 copy-start
  53.2 0.0 copy-start.6
  53.2 3.1 %all-to-all-start.1 = ((f32[32,96,128]{2,1,0:T(8,128)}), f32[32,96,128]{2,1,0:T(8,128)S(1)}, u32[]{:S(2)}, u32[]{:S(2)}) async-start(f32[32,96,128]{2,1,0:T(8,128)} %bitcast.26), calls=%async_computation.1 | async-start | bytes 3145728 | tf_op jit(solution)/shard_map/all_to_all | solution.py:812
  56.3 0.0 copy-start.5
  56.3 0.0 copy-done.10
  56.3 0.1 fusion
  56.4 0.0 copy-done.9
  56.4 0.0 copy-done.7
  56.4 0.0 copy-done.8
  56.5 1.8 %collective-permute-start = (f32[9,3,128]{2,1,0:T(4,128)S(1)}, f32[9,3,128]{2,1,0:T(4,128)S(1)}, u32[]{:S(2)}, u32[]{:S(2)}) collective-permute-start(f32[9,3,128]{2,1,0:T(4,128)S(1)} %get-tuple-element.40), channel_id=1, source_target_pairs={{0,8},{8,16},{16,24},{24,0},{1,9},{9,17},{17,25},{25,1},{2,10},{10... | collective-permute-start | bytes 41480 | tf_op jit(solution)/shard_map/ppermute | solution.py:741
  58.3 1.2 %collective-permute-start.1 = (f32[9,3,128]{2,1,0:T(4,128)S(1)}, f32[9,3,128]{2,1,0:T(4,128)S(1)}, u32[]{:S(2)}, u32[]{:S(2)}) collective-permute-start(f32[9,3,128]{2,1,0:T(4,128)S(1)} %get-tuple-element.41), channel_id=1, source_target_pairs={{8,0},{16,8},{24,16},{0,24},{9,1},{17,9},{25,17},{1,25},{10,2},{18... | collective-permute-start | bytes 41480 | tf_op jit(solution)/shard_map/ppermute | solution.py:741
  59.5 0.1 pad.5.clone
  59.5 11.6 %collective-permute-done = f32[9,3,128]{2,1,0:T(4,128)S(1)} collective-permute-done((f32[9,3,128]{2,1,0:T(4,128)S(1)}, f32[9,3,128]{2,1,0:T(4,128)S(1)}, u32[]{:S(2)}, u32[]{:S(2)}) %collective-permute-start) | collective-permute-done | bytes 13856 | tf_op jit(solution)/shard_map/ppermute | solution.py:741
  71.1 0.0 collective-permute-done.1
  71.1 0.1 maximum_maximum_fusion.start_ref
  71.2 0.0 copy-done
  71.2 0.0 copy-done.6
  71.2 1.6 %shard_map.133 = (f32[6,16,128]{2,1,0:T(8,128)S(1)}, f32[4,8,128]{2,1,0:T(8,128)S(1)}) custom-call(f32[9,16,128]{2,1,0:T(8,128)S(1)} %maximum_maximum_fusion.start_ref, s32[4,128]{1,0:T(4,128)S(1)} %bitcast.24, f32[3072,128]{1,0:T(8,128)S(1)} %bitcast.18), custom_call_target="tpu_custom_call" | custom-call | bytes 1048576 | tf_op jit(solution)/shard_map/pallas_call | solution.py:826
  72.8 20.5 %all-to-all-done.1 = f32[32,96,128]{2,1,0:T(8,128)S(1)} async-done(((f32[32,96,128]{2,1,0:T(8,128)}), f32[32,96,128]{2,1,0:T(8,128)S(1)}, u32[]{:S(2)}, u32[]{:S(2)}) %all-to-all-start.1) | async-done | bytes 1572896 | tf_op jit(solution)/shard_map/all_to_all | solution.py:812
  93.2 0.0 copy-done.5
  93.2 2.2 %shard_map.134 = (f32[3072,128]{1,0:T(8,128)S(1)}, f32[4,8,128]{2,1,0:T(8,128)S(1)}, f32[2,8,128]{2,1,0:T(8,128)S(1)}, f32[2,8,128]{2,1,0:T(8,128)S(1)}) custom-call(s32[4,128]{1,0:T(4,128)S(1)} %bitcast.25, f32[3072,128]{1,0:T(8,128)S(1)} %bitcast.20, f32[4,8,128]{2,1,0:T(8,128)S(1)} %get-tuple-element.31.local_ref, bf16[2,128,128]{2,1,0:T(8,128)(2,1)S(1)} %copy-done.5), custom_call_target="tpu_custom_call" | custom-call | bytes 1048576 | tf_op jit(solution)/shard_map/pallas_call | solution.py:836
  95.4 1.5 %collective-permute-start.2 = (f32[2,8,128]{2,1,0:T(8,128)S(1)}, f32[2,8,128]{2,1,0:T(8,128)S(1)}, u32[]{:S(2)}, u32[]{:S(2)}) collective-permute-start(f32[2,8,128]{2,1,0:T(8,128)S(1)} %get-tuple-element.35), channel_id=1, source_target_pairs={{0,8},{8,16},{16,24},{24,0},{1,9},{9,17},{17,25},{25,1},{2,10},{10... | collective-permute-start | bytes 24584 | tf_op jit(solution)/shard_map/ppermute | solution.py:741
  96.9 1.5 %collective-permute-start.3 = (f32[2,8,128]{2,1,0:T(8,128)S(1)}, f32[2,8,128]{2,1,0:T(8,128)S(1)}, u32[]{:S(2)}, u32[]{:S(2)}) collective-permute-start(f32[2,8,128]{2,1,0:T(8,128)S(1)} %get-tuple-element.36), channel_id=1, source_target_pairs={{8,0},{16,8},{24,16},{0,24},{9,1},{17,9},{25,17},{1,25},{10,2},{18... | collective-permute-start | bytes 24584 | tf_op jit(solution)/shard_map/ppermute | solution.py:741
  98.4 1.8 %shard_map.135 = (f32[6,512,128]{2,1,0:T(8,128)}, f32[384,128]{1,0:T(8,128)S(1)}) custom-call(f32[9,16,128]{2,1,0:T(8,128)S(1)} %maximum_maximum_fusion.start_ref, f32[6,16,128]{2,1,0:T(8,128)S(1)} %get-tuple-element.29.first_ref, f32[4,8,128]{2,1,0:T(8,128)S(1)} %get-tuple-element.32.own_ref, f32[6,512,128]{2,1,0:T(8,128)S(1)} %bitcast.23, ...), custom_call_target="tpu_custom_call" | custom-call | bytes 1048576 | tf_op jit(solution)/shard_map/pallas_call | solution.py:845
  100.3 0.0 collective-permute-done.2.left_ref
  100.3 0.3 collective-permute-done.3.right_ref
  100.5 2.0 %shard_map.136 = f32[3,4,128]{2,1,0:T(4,128)} custom-call(f32[9,16,128]{2,1,0:T(8,128)S(1)} %maximum_maximum_fusion.start_ref, f32[6,16,128]{2,1,0:T(8,128)S(1)} %get-tuple-element.29.first_ref, f32[2,8,128]{2,1,0:T(8,128)S(1)} %collective-permute-done.2.left_ref, f32[4,8,128]{2,1,0:T(8,128)S(1)} %get-tuple-element.32.own_ref, ...), custom_call_target="tpu_custom_call" | custom-call | bytes 1048576 | tf_op jit(solution)/shard_map/pallas_call | solution.py:856
  (5 shorter events, 0.0 us)
Async XLA Ops:
  3.4 44.7 %copy-start.1 = (bf16[2,256,256]{2,1,0:T(8,128)(2,1)S(1)}, bf16[2,256,256]{2,1,0:T(8,128)(2,1)}, u32[]{:S(2)}) copy-start(bf16[2,256,256]{2,1,0:T(8,128)(2,1)} %constant.65.clone.inverse_y_ref) | copy-start | bytes 786436
  3.4 44.7 %copy-start.2 = (bf16[2,256,256]{2,1,0:T(8,128)(2,1)S(1)}, bf16[2,256,256]{2,1,0:T(8,128)(2,1)}, u32[]{:S(2)}) copy-start(bf16[2,256,256]{2,1,0:T(8,128)(2,1)} %constant.64.clone.inverse_x_ref) | copy-start | bytes 786436
  3.4 44.7 %copy-start.3 = (bf16[2,256,256]{2,1,0:T(8,128)(2,1)S(1)}, bf16[2,256,256]{2,1,0:T(8,128)(2,1)}, u32[]{:S(2)}) copy-start(bf16[2,256,256]{2,1,0:T(8,128)(2,1)} %constant.63.clone.forward_x_ref) | copy-start | bytes 786436
  3.4 44.7 %copy-start.4 = (bf16[2,256,256]{2,1,0:T(8,128)(2,1)S(1)}, bf16[2,256,256]{2,1,0:T(8,128)(2,1)}, u32[]{:S(2)}) copy-start(bf16[2,256,256]{2,1,0:T(8,128)(2,1)} %constant.62.clone.forward_y_ref) | copy-start | bytes 786436
  53.1 3.2 %copy-start.10 = (s32[1,4]{1,0:T(1,128)S(1)}, s32[1,4]{1,0:T(1,128)}, u32[]{:S(2)}) copy-start(s32[1,4]{1,0:T(1,128)} %param.16) | copy-start | bytes 52
  53.1 3.3 %copy-start.9 = (f32[3,1,4,128]{3,2,1,0:T(4,128)S(1)}, f32[3,1,4,128]{3,2,1,0:T(4,128)}, u32[]{:S(2)}) copy-start(f32[3,1,4,128]{3,2,1,0:T(4,128)} %param.15) | copy-start | bytes 18436
  53.2 3.3 %copy-start.7 = (f32[3,1,4,128]{3,2,1,0:T(4,128)S(1)}, f32[3,1,4,128]{3,2,1,0:T(4,128)}, u32[]{:S(2)}) copy-start(f32[3,1,4,128]{3,2,1,0:T(4,128)} %param.14) | copy-start | bytes 18436
  53.2 3.3 %copy-start.8 = (f32[3,1,4,128]{3,2,1,0:T(4,128)S(1)}, f32[3,1,4,128]{3,2,1,0:T(4,128)}, u32[]{:S(2)}) copy-start(f32[3,1,4,128]{3,2,1,0:T(4,128)} %param.13) | copy-start | bytes 18436
  53.2 18.0 %copy-start = (f32[6,32,16,128]{3,2,1,0:T(8,128)S(1)}, f32[6,32,16,128]{3,2,1,0:T(8,128)}, u32[]{:S(2)}) copy-start(f32[6,32,16,128]{3,2,1,0:T(8,128)} %param.12) | copy-start | bytes 4718596
  53.2 18.0 %copy-start.6 = (s32[1,4,128]{2,1,0:T(4,128)S(1)}, s32[1,4,128]{2,1,0:T(4,128)}, u32[]{:S(2)}) copy-start(s32[1,4,128]{2,1,0:T(4,128)} %param.17) | copy-start | bytes 6148
  53.2 40.0 %all-to-all-start.1 = ((f32[32,96,128]{2,1,0:T(8,128)}), f32[32,96,128]{2,1,0:T(8,128)S(1)}, u32[]{:S(2)}, u32[]{:S(2)}) async-start(f32[32,96,128]{2,1,0:T(8,128)} %bitcast.26), calls=%async_computation.1 | async-start | bytes 3145728 | tf_op jit(solution)/shard_map/all_to_all | solution.py:812
  56.3 36.9 %copy-start.5 = (bf16[2,128,128]{2,1,0:T(8,128)(2,1)S(1)}, bf16[2,128,128]{2,1,0:T(8,128)(2,1)}, u32[]{:S(2)}) copy-start(bf16[2,128,128]{2,1,0:T(8,128)(2,1)} %constant.66.clone.table_ref) | copy-start | bytes 196612
  56.5 14.6 %collective-permute-start = (f32[9,3,128]{2,1,0:T(4,128)S(1)}, f32[9,3,128]{2,1,0:T(4,128)S(1)}, u32[]{:S(2)}, u32[]{:S(2)}) collective-permute-start(f32[9,3,128]{2,1,0:T(4,128)S(1)} %get-tuple-element.40), channel_id=1, source_target_pairs={{0,8},{8,16},{16,24},{24,0},{1,9},{9,17},{17,25},{25,1},{2,10},{10... | collective-permute-start | bytes 41480 | tf_op jit(solution)/shard_map/ppermute | solution.py:741
  58.3 12.8 %collective-permute-start.1 = (f32[9,3,128]{2,1,0:T(4,128)S(1)}, f32[9,3,128]{2,1,0:T(4,128)S(1)}, u32[]{:S(2)}, u32[]{:S(2)}) collective-permute-start(f32[9,3,128]{2,1,0:T(4,128)S(1)} %get-tuple-element.41), channel_id=1, source_target_pairs={{8,0},{16,8},{24,16},{0,24},{9,1},{17,9},{25,17},{1,25},{10,2},{18... | collective-permute-start | bytes 41480 | tf_op jit(solution)/shard_map/ppermute | solution.py:741
  95.4 4.8 %collective-permute-start.2 = (f32[2,8,128]{2,1,0:T(8,128)S(1)}, f32[2,8,128]{2,1,0:T(8,128)S(1)}, u32[]{:S(2)}, u32[]{:S(2)}) collective-permute-start(f32[2,8,128]{2,1,0:T(8,128)S(1)} %get-tuple-element.35), channel_id=1, source_target_pairs={{0,8},{8,16},{16,24},{24,0},{1,9},{9,17},{17,25},{25,1},{2,10},{10... | collective-permute-start | bytes 24584 | tf_op jit(solution)/shard_map/ppermute | solution.py:741
  96.9 3.7 %collective-permute-start.3 = (f32[2,8,128]{2,1,0:T(8,128)S(1)}, f32[2,8,128]{2,1,0:T(8,128)S(1)}, u32[]{:S(2)}, u32[]{:S(2)}) collective-permute-start(f32[2,8,128]{2,1,0:T(8,128)S(1)} %get-tuple-element.36), channel_id=1, source_target_pairs={{8,0},{16,8},{24,16},{0,24},{9,1},{17,9},{25,17},{1,25},{10,2},{18... | collective-permute-start | bytes 24584 | tf_op jit(solution)/shard_map/ppermute | solution.py:741
